TPU v7x, 32 devices: a whole 2x2x4 slice. The times are simulated.
32 devices in a mesh: ctx: 8 (over z, y), fsdp: 4 (over x, core).
Axes of the slice: x: 2, y: 2, z: 4, core: 2. Of those that a mesh axis runs over, the one named last changes fastest.
Arguments:
- tokens: bfloat16 [8, 1024, 1536], P('fsdp', 'ctx'), may hold values from -6 to 6
- cotangent: bfloat16 [8, 1024, 1536], P('fsdp', 'ctx'), may hold values from -6 to 6
- lengths: int32 [8], replicated, may hold values from 256 to 1024, as said below
- slot_adapter_index: int32 [8], replicated, may hold values from 0 to 7
- attention_norm_gain: float32 [1536], replicated, may hold values from 0.1 to 1.9
- feedforward_norm_gain: float32 [1536], replicated, may hold values from 0.1 to 1.9
- query_weight: bfloat16 [1536, 1536], P(None, 'fsdp'), may hold values from -0.15625 to 0.15625
- key_weight: bfloat16 [1536, 768], P(None, 'fsdp'), may hold values from -0.15625 to 0.15625
- value_weight: bfloat16 [1536, 768], P(None, 'fsdp'), may hold values from -0.15625 to 0.15625
- output_weight: bfloat16 [1536, 1536], P('fsdp'), may hold values from -1.25 to 1.25
- gate_weight: bfloat16 [1536, 4096], P(None, 'fsdp'), may hold values from -0.15625 to 0.15625
- up_weight: bfloat16 [1536, 4096], P(None, 'fsdp'), may hold values from -0.15625 to 0.15625
- down_weight: bfloat16 [4096, 1536], P('fsdp'), may hold values from -0.09375 to 0.09375
- adapter_input_first: bfloat16 [8, 5, 1536, 16], replicated, may hold values from -0.15625 to 0.15625
- adapter_output_first: bfloat16 [8, 1536, 16], replicated, may hold values from -1.25 to 1.25
- adapter_down_first: bfloat16 [8, 4096, 16], replicated, may hold values from -0.09375 to 0.09375
- adapter_query_second: bfloat16 [8, 16, 1536], replicated, may hold values from -1.5 to 1.5
- adapter_key_value_second: bfloat16 [8, 2, 16, 768], replicated, may hold values from -1.5 to 1.5
- adapter_output_second: bfloat16 [8, 16, 1536], replicated, may hold values from -1.5 to 1.5
- adapter_gate_up_second: bfloat16 [8, 2, 16, 4096], replicated, may hold values from -1.5 to 1.5
- adapter_down_second: bfloat16 [8, 16, 1536], replicated, may hold values from -1.5 to 1.5
Outputs:
- out_tokens: bfloat16 [8, 1024, 1536], P('fsdp', 'ctx')
- grad_tokens: float32 [8, 1024, 1536], P('fsdp', 'ctx')
- grad_in_a: float32 [8, 5, 1536, 16], replicated
- grad_o_a: float32 [8, 1536, 16], replicated
- grad_d_a: float32 [8, 4096, 16], replicated
- grad_q_b: float32 [8, 16, 1536], replicated
- grad_kv_b: float32 [8, 2, 16, 768], replicated
- grad_o_b: float32 [8, 16, 1536], replicated
- grad_gu_b: float32 [8, 2, 16, 4096], replicated
- grad_d_b: float32 [8, 16, 1536], replicated
Inputs may be any that keep to these rules, and one draw needn't show every extreme that they name: `lengths`: in each aligned group of 2 slots one slot, drawn from the seed, has all 1024 positions live.
All inputs are finite; a program needn't handle non-finite values.
Results may differ from a plain program's by a relative error of at most 0.02.
Values may be sent and summed in bfloat16 or wider, within the bound.
A program may use at most 256 MiB of HBM per device.

v0:
```python
import math

import jax
import jax.numpy as jnp
from jax import lax
from jax.sharding import PartitionSpec as P

QUERY_HEADS = 16
KEY_VALUE_HEADS = 8
HEAD_DIM = 96


EPSILON = 1e-05
NEGATIVE = -1e30
ADAPTER_SCALE = 0.5
ROPE_BASE = 100000.0


def from_behind(x, axis, by):
    size = lax.axis_size(axis)
    return lax.ppermute(x, axis, [(i, (i + by) % size) for i in range(size)])


def rope_tables(positions, head_size):
    half_size = head_size // 2
    freqs = ROPE_BASE ** (-(jnp.arange(half_size, dtype=jnp.float32) * 2.0 / head_size))
    angles = positions.astype(jnp.float32)[:, None] * freqs[None, :]
    return (jnp.cos(angles)[:, None, :], jnp.sin(angles)[:, None, :])


def apply_rotation(values, cosine_table, sine_table):
    half_size = values.shape[-1] // 2
    first_half = values[..., :half_size]
    second_half = values[..., half_size:]
    return jnp.concatenate(
        [
            first_half * cosine_table - second_half * sine_table,
            second_half * cosine_table + first_half * sine_table,
        ],
        axis=-1,
    )


def rotate_back(gradient_tree, cosine_table, sine_table):
    half_size = gradient_tree.shape[-1] // 2
    first_half = gradient_tree[..., :half_size]
    second_half = gradient_tree[..., half_size:]
    return jnp.concatenate(
        [
            first_half * cosine_table + second_half * sine_table,
            second_half * cosine_table - first_half * sine_table,
        ],
        axis=-1,
    )


def rms_factor(values):
    return lax.rsqrt(jnp.mean(values * values, axis=-1, keepdims=True) + EPSILON)


def norm_back(values, factor, gain, grad_norm):
    scaled = grad_norm * gain
    return factor * scaled - values * factor**3 * jnp.mean(scaled * values, axis=-1, keepdims=True)


def pick_rows(onehot, table):
    return jnp.einsum("sa,a...->s...", onehot, table, preferred_element_type=jnp.float32).astype(
        jnp.bfloat16
    )


def spread_rows(onehot, gradient_tree):
    return jnp.einsum("sa,s...->a...", onehot, gradient_tree, precision=lax.Precision.HIGHEST)


def direct_product(input_rows, weight_matrix):
    return jnp.einsum("std,do->sto", input_rows, weight_matrix, preferred_element_type=jnp.float32)


def direct_back(gradient_tree, weight_matrix):
    return jnp.einsum(
        "sto,do->std", gradient_tree, weight_matrix, preferred_element_type=jnp.float32
    )


def inner_product_part(input_rows, down):
    return jnp.einsum("std,sdr->str", input_rows, down, preferred_element_type=jnp.float32)


def inner_back(gradient_tree, upward_rows):
    return ADAPTER_SCALE * jnp.einsum(
        "sto,sro->str", gradient_tree, upward_rows, preferred_element_type=jnp.float32
    )


def through_down(grad_inner, down):
    return jnp.einsum("str,sdr->std", grad_inner, down, preferred_element_type=jnp.float32)


def down_grad(input_rows, grad_inner):
    return jnp.einsum("std,str->sdr", input_rows, grad_inner, preferred_element_type=jnp.float32)


def upward_grad(inner_rows, gradient_tree):
    return ADAPTER_SCALE * jnp.einsum(
        "jvp,jvx->jpx", inner_rows, gradient_tree, preferred_element_type=jnp.float32
    )


def upward_apply(inner_rows, upward_rows):
    return ADAPTER_SCALE * jnp.einsum(
        "str,sro->sto", inner_rows, upward_rows, preferred_element_type=jnp.float32
    )


def project(input_rows, weight_matrix, down, upward_rows):
    inner_rows = inner_product_part(input_rows, down).astype(jnp.bfloat16)
    return (
        inner_rows,
        direct_product(input_rows, weight_matrix) + upward_apply(inner_rows, upward_rows),
    )


def project_back(input_rows, grad_output, weight_matrix, down, upward_rows, inner_rows):
    grad_upward = upward_grad(inner_rows, grad_output)
    grad_inner = inner_back(grad_output, upward_rows).astype(jnp.bfloat16)
    grad_down = down_grad(input_rows, grad_inner)
    grad_inputs = direct_back(grad_output, weight_matrix) + through_down(grad_inner, down)
    return (grad_inputs, grad_down, grad_upward)


def allowed_mask(key_start, key_count, query_pos, lengths):
    key_pos = key_start + jnp.arange(key_count, dtype=jnp.int32)
    causal = key_pos[None, :] <= query_pos[:, None]
    live = key_pos[None, :] < lengths[:, None]
    return (causal[None, :, :] & live[:, None, :])[:, None, None, :, :]


def attend_block(state, key_block, value_block, key_start, query_head_rows, query_pos, lengths):
    run_max, run_sum, run_acc = state
    scale = query_head_rows.shape[-1] ** (-0.5)
    scores = (
        jnp.einsum(
            "sqhgd,skhd->shgqk", query_head_rows, key_block, preferred_element_type=jnp.float32
        )
        * scale
    )
    allowed = allowed_mask(key_start, key_block.shape[1], query_pos, lengths)
    new_max = jnp.maximum(run_max, jnp.max(jnp.where(allowed, scores, NEGATIVE), axis=-1))
    weights = jnp.where(allowed, jnp.exp(scores - new_max[..., None]), 0.0)
    factor = jnp.exp(run_max - new_max)
    new_sum = run_sum * factor + jnp.sum(weights, axis=-1)
    update = jnp.einsum(
        "shgqk,skhd->shgqd",
        weights.astype(jnp.bfloat16),
        value_block,
        preferred_element_type=jnp.float32,
    )
    return (new_max, new_sum, run_acc * factor[..., None] + update)


def attend_back(
    key_block,
    value_block,
    key_start,
    query_head_rows,
    grad_heads,
    log_total,
    row_dot,
    query_pos,
    lengths,
):
    scale = query_head_rows.shape[-1] ** (-0.5)
    scores = (
        jnp.einsum(
            "sqhgd,skhd->shgqk", query_head_rows, key_block, preferred_element_type=jnp.float32
        )
        * scale
    )
    allowed = allowed_mask(key_start, key_block.shape[1], query_pos, lengths)
    probs = jnp.where(allowed, jnp.exp(scores - log_total[..., None]), 0.0)
    grad_probs = jnp.einsum(
        "sqhgd,skhd->shgqk", grad_heads, value_block, preferred_element_type=jnp.float32
    )
    grad_scores = (probs * (grad_probs - row_dot[..., None])).astype(jnp.bfloat16)
    grad_query = scale * jnp.einsum(
        "shgqk,skhd->sqhgd", grad_scores, key_block, preferred_element_type=jnp.float32
    )
    grad_key = scale * jnp.einsum(
        "shgqk,sqhgd->skhd", grad_scores, query_head_rows, preferred_element_type=jnp.float32
    )
    grad_value = jnp.einsum(
        "shgqk,sqhgd->skhd",
        probs.astype(jnp.bfloat16),
        grad_heads,
        preferred_element_type=jnp.float32,
    )
    return (grad_query, grad_key, grad_value)


def attend_forward(query_head_rows, key_head_rows, value_head_rows, lengths_used, query_pos):
    slots, rows, kv_heads, group_size, head_size = query_head_rows.shape
    key_flat = key_head_rows.reshape(slots, rows, kv_heads * head_size)
    value_flat = value_head_rows.reshape(slots, rows, kv_heads * head_size)
    stat_shape = (slots, kv_heads, group_size, rows)
    initial = (
        jnp.full(stat_shape, NEGATIVE, jnp.float32),
        jnp.zeros(stat_shape, jnp.float32),
        jnp.zeros(stat_shape + (head_size,), jnp.float32),
    )
    part_keys = lax.all_gather(key_flat, "ctx", axis=1, tiled=True)
    part_values = lax.all_gather(value_flat, "ctx", axis=1, tiled=True)
    piece_rows = part_keys.shape[1]
    part_keys = part_keys.reshape(slots, piece_rows, kv_heads, head_size)
    part_values = part_values.reshape(slots, piece_rows, kv_heads, head_size)
    span_rows = math.gcd(piece_rows, 4 * rows)

    def inner_step(block_index, inner_state):
        sub_keys = lax.dynamic_slice_in_dim(part_keys, block_index * span_rows, span_rows, 1)
        sub_values = lax.dynamic_slice_in_dim(part_values, block_index * span_rows, span_rows, 1)
        return attend_block(
            inner_state,
            sub_keys,
            sub_values,
            block_index * span_rows,
            query_head_rows,
            query_pos,
            lengths_used,
        )

    run_max, run_sum, run_acc = lax.fori_loop(0, piece_rows // span_rows, inner_step, initial)
    log_total = run_max + jnp.log(run_sum)
    attended = jnp.transpose(run_acc / run_sum[..., None], (0, 3, 1, 2, 4))
    return (attended, log_total)


def attend_backward(
    query_head_rows,
    key_head_rows,
    value_head_rows,
    grad_heads,
    attended,
    log_total,
    lengths_used,
    query_pos,
):
    ctx_count = lax.axis_size("ctx")
    own_index = lax.axis_index("ctx")
    rows = query_head_rows.shape[1]
    row_dot = jnp.transpose(
        jnp.sum(grad_heads.astype(jnp.float32) * attended, axis=-1), (0, 2, 3, 1)
    )

    def cycle_step(step_index, carried):
        carried_keys, carried_values, grad_query, grad_key, grad_value = carried
        block_id = (own_index + step_index) % ctx_count
        query_part, key_part, value_part = attend_back(
            carried_keys,
            carried_values,
            block_id * rows,
            query_head_rows,
            grad_heads,
            log_total,
            row_dot,
            query_pos,
            lengths_used,
        )
        grad_key, grad_value = (
            from_behind((grad_key + key_part).astype(jnp.bfloat16), "ctx", -1).astype(jnp.float32),
            from_behind((grad_value + value_part).astype(jnp.bfloat16), "ctx", -1).astype(
                jnp.float32
            ),
        )
        carried_keys, carried_values = from_behind((carried_keys, carried_values), "ctx", -1)
        return (carried_keys, carried_values, grad_query + query_part, grad_key, grad_value)

    key_zeros = jnp.zeros(key_head_rows.shape, jnp.float32)
    start_state = (
        key_head_rows,
        value_head_rows,
        jnp.zeros(query_head_rows.shape, jnp.float32),
        key_zeros,
        key_zeros,
    )
    carried = lax.fori_loop(0, ctx_count, cycle_step, start_state)
    return (carried[2], carried[3], carried[4])


def table_total(rotation_tables):
    return lax.psum(rotation_tables, ("ctx", "fsdp"))


def local(
    tokens,
    cotangent,
    lengths,
    slot_adapter_index,
    attention_norm_gain,
    feedforward_norm_gain,
    query_weight,
    key_weight,
    value_weight,
    output_weight,
    gate_weight,
    up_weight,
    down_weight,
    adapter_input_first,
    adapter_output_first,
    adapter_down_first,
    adapter_query_second,
    adapter_key_value_second,
    adapter_output_second,
    adapter_gate_up_second,
    adapter_down_second,
):
    slot_count, tok_rows, model_width = tokens.shape
    head_groups = QUERY_HEADS // KEY_VALUE_HEADS
    own_index = lax.axis_index("ctx")
    fsdp_index = lax.axis_index("fsdp")
    query_pos = own_index * tok_rows + jnp.arange(tok_rows, dtype=jnp.int32)
    cosine_table, sine_table = rope_tables(query_pos, HEAD_DIM)
    own_lengths = lax.dynamic_slice_in_dim(lengths, fsdp_index * slot_count, slot_count, 0)
    own_adapters = lax.dynamic_slice_in_dim(
        slot_adapter_index, fsdp_index * slot_count, slot_count, 0
    )
    valid = query_pos[None, :] < own_lengths[:, None]
    adapter_labels = jnp.arange(adapter_input_first.shape[0], dtype=jnp.int32)
    onehot_own = own_adapters[:, None] == adapter_labels[None, :]
    owned_low_rank = onehot_own.astype(jnp.bfloat16)
    own_full = onehot_own.astype(jnp.float32)
    tokens_f = tokens.astype(jnp.float32)
    factor_one = rms_factor(tokens_f)
    normed_one = (tokens_f * factor_one * attention_norm_gain).astype(jnp.bfloat16)
    grad_out = jnp.where(valid[..., None], cotangent, jnp.zeros((), jnp.bfloat16))
    input_first = pick_rows(owned_low_rank, adapter_input_first)
    output_second = pick_rows(owned_low_rank, adapter_output_second)
    down_second = pick_rows(owned_low_rank, adapter_down_second)
    output_first = pick_rows(owned_low_rank, adapter_output_first)
    down_first = pick_rows(owned_low_rank, adapter_down_first)
    query_second = pick_rows(owned_low_rank, adapter_query_second)
    key_value_second = pick_rows(owned_low_rank, adapter_key_value_second)
    gate_up_second = pick_rows(owned_low_rank, adapter_gate_up_second)
    weight_q, weight_k, weight_v, weight_gate, weight_up, weight_o, weight_down = (
        lax.all_gather(query_weight, "fsdp", axis=1, tiled=True),
        lax.all_gather(key_weight, "fsdp", axis=1, tiled=True),
        lax.all_gather(value_weight, "fsdp", axis=1, tiled=True),
        lax.all_gather(gate_weight, "fsdp", axis=1, tiled=True),
        lax.all_gather(up_weight, "fsdp", axis=1, tiled=True),
        lax.all_gather(output_weight, "fsdp", axis=0, tiled=True),
        lax.all_gather(down_weight, "fsdp", axis=0, tiled=True),
    )
    inner_q, projected_queries = project(normed_one, weight_q, input_first[:, 0], query_second)
    inner_k, projected_keys = project(
        normed_one, weight_k, input_first[:, 1], key_value_second[:, 0]
    )
    inner_v, projected_values = project(
        normed_one, weight_v, input_first[:, 2], key_value_second[:, 1]
    )
    query_head_rows = apply_rotation(
        projected_queries.reshape(slot_count, tok_rows, -1, HEAD_DIM), cosine_table, sine_table
    ).astype(jnp.bfloat16)
    query_head_rows = query_head_rows.reshape(slot_count, tok_rows, -1, head_groups, HEAD_DIM)
    key_head_rows = apply_rotation(
        projected_keys.reshape(slot_count, tok_rows, -1, HEAD_DIM), cosine_table, sine_table
    ).astype(jnp.bfloat16)
    value_head_rows = projected_values.astype(jnp.bfloat16).reshape(
        slot_count, tok_rows, -1, HEAD_DIM
    )
    attended, log_total = attend_forward(
        query_head_rows, key_head_rows, value_head_rows, own_lengths, query_pos
    )
    attn_b = attended.reshape(slot_count, tok_rows, -1).astype(jnp.bfloat16)
    inner_o, proj_o = project(attn_b, weight_o, output_first, output_second)
    resid = tokens_f + proj_o
    factor_two = rms_factor(resid)
    normed_two = (resid * factor_two * feedforward_norm_gain).astype(jnp.bfloat16)
    inner_gate, gate = project(normed_two, weight_gate, input_first[:, 3], gate_up_second[:, 0])
    inner_up, up_proj = project(normed_two, weight_up, input_first[:, 4], gate_up_second[:, 1])
    sigmoid_gate = jax.nn.sigmoid(gate)
    hidden = (gate * sigmoid_gate * up_proj).astype(jnp.bfloat16)
    inner_down, proj_down = project(hidden, weight_down, down_first, down_second)
    out_tokens = jnp.where(valid[..., None], resid + proj_down, 0.0).astype(jnp.bfloat16)
    grad_hidden, grad_da, grad_db = project_back(
        hidden, grad_out, weight_down, down_first, down_second, inner_down
    )
    grad_gate = (grad_hidden * up_proj * sigmoid_gate * (1.0 + gate * (1.0 - sigmoid_gate))).astype(
        jnp.bfloat16
    )
    grad_up = (grad_hidden * gate * sigmoid_gate).astype(jnp.bfloat16)
    from_gate, grad_ga, grad_gb = project_back(
        normed_two, grad_gate, weight_gate, input_first[:, 3], gate_up_second[:, 0], inner_gate
    )
    from_up, grad_ua, grad_ub = project_back(
        normed_two, grad_up, weight_up, input_first[:, 4], gate_up_second[:, 1], inner_up
    )
    grad_normed_two = (from_gate + from_up).astype(jnp.bfloat16).astype(jnp.float32)
    grad_resid = grad_out.astype(jnp.float32) + norm_back(
        resid, factor_two, feedforward_norm_gain, grad_normed_two
    )
    grad_resid_low = grad_resid.astype(jnp.bfloat16)
    from_attn, grad_oa, grad_ob = project_back(
        attn_b, grad_resid_low, weight_o, output_first, output_second, inner_o
    )
    grad_heads = from_attn.astype(jnp.bfloat16).reshape(attended.shape)
    grad_query, grad_key, grad_value = attend_backward(
        query_head_rows,
        key_head_rows,
        value_head_rows,
        grad_heads,
        attended,
        log_total,
        own_lengths,
        query_pos,
    )
    grad_proj_q = (
        rotate_back(
            grad_query.reshape(slot_count, tok_rows, -1, HEAD_DIM), cosine_table, sine_table
        )
        .astype(jnp.bfloat16)
        .reshape(slot_count, tok_rows, -1)
    )
    grad_proj_k = (
        rotate_back(grad_key, cosine_table, sine_table)
        .astype(jnp.bfloat16)
        .reshape(slot_count, tok_rows, -1)
    )
    grad_proj_v = grad_value.astype(jnp.bfloat16).reshape(slot_count, tok_rows, -1)
    from_query, grad_qa, grad_qb = project_back(
        normed_one, grad_proj_q, weight_q, input_first[:, 0], query_second, inner_q
    )
    from_key, grad_ka, grad_kb = project_back(
        normed_one, grad_proj_k, weight_k, input_first[:, 1], key_value_second[:, 0], inner_k
    )
    from_value, grad_va, grad_vb = project_back(
        normed_one, grad_proj_v, weight_v, input_first[:, 2], key_value_second[:, 1], inner_v
    )
    grad_normed_one = (from_query + from_key + from_value).astype(jnp.bfloat16).astype(jnp.float32)
    grad_tokens = grad_resid + norm_back(tokens_f, factor_one, attention_norm_gain, grad_normed_one)
    slot_grads = (
        jnp.stack([grad_qa, grad_ka, grad_va, grad_ga, grad_ua], axis=1),
        grad_oa,
        grad_da,
        grad_qb,
        jnp.stack([grad_kb, grad_vb], axis=1),
        grad_ob,
        jnp.stack([grad_gb, grad_ub], axis=1),
        grad_db,
    )
    summed = table_total(tuple((spread_rows(own_full, entry_item) for entry_item in slot_grads)))
    return (
        out_tokens,
        grad_tokens,
        summed[0],
        summed[1],
        summed[2],
        summed[3],
        summed[4],
        summed[5],
        summed[6],
        summed[7],
    )


def solution(mesh):
    return jax.shard_map(
        local,
        mesh=mesh,
        in_specs=(
            P("fsdp", "ctx", None),
            P("fsdp", "ctx", None),
            P(),
            P(),
            P(),
            P(),
            P(None, "fsdp"),
            P(None, "fsdp"),
            P(None, "fsdp"),
            P("fsdp", None),
            P(None, "fsdp"),
            P(None, "fsdp"),
            P("fsdp", None),
            P(),
            P(),
            P(),
            P(),
            P(),
            P(),
            P(),
            P(),
        ),
        out_specs=(
            P("fsdp", "ctx", None),
            P("fsdp", "ctx", None),
            P(),
            P(),
            P(),
            P(),
            P(),
            P(),
            P(),
            P(),
        ),
        check_vma=False,
    )
```

profile of v0, /device:TPU:3, one launch (start us, length us, event | category | flops | bytes accessed | tf_op | source)
XLA Modules:
  0.0 1194.5 jit_solution(6085360113000304782)
XLA Ops:
  15.9 18.3 %all-gather.16.cloned.1.call-done = bf16[1536,768]{0,1:T(8,128)(2,1)} async-done(((bf16[1536,192]{0,1:T(8,128)(2,1)}), bf16[1536,768]{0,1:T(8,128)(2,1)}) %all-gather.16.cloned.1.call-update) | async-done | bytes 2359312 | tf_op jit(solution)/shard_map/all_gather | solution.py:346
  38.5 21.4 %all-gather.10.cloned.1.call-done = bf16[1536,768]{0,1:T(8,128)(2,1)} async-done(((bf16[1536,192]{0,1:T(8,128)(2,1)}), bf16[1536,768]{0,1:T(8,128)(2,1)}) %all-gather.10.cloned.1.call-update) | async-done | bytes 2359312 | tf_op jit(solution)/shard_map/all_gather | solution.py:345
  85.6 13.2 %all-gather.14.cloned.1.call-done = bf16[1536,1536]{1,0:T(8,128)(2,1)} async-done(((bf16[1536,384]{1,0:T(8,128)(2,1)}), bf16[1536,1536]{1,0:T(8,128)(2,1)}) %all-gather.14.cloned.1.call-update) | async-done | bytes 4718608 | tf_op jit(solution)/shard_map/all_gather | solution.py:344
  106.5 55.5 %all-gather.18.cloned.1.call-done = bf16[2,1024,768]{2,1,0:T(8,128)(2,1)} async-done(((bf16[2,128,768]{2,1,0:T(8,128)(2,1)}), bf16[2,1024,768]{2,1,0:T(8,128)(2,1)}) %all-gather.18.cloned.1.call-update) | async-done | bytes 3145744 | tf_op jit(solution)/shard_map/all_gather | solution.py:212
  166.8 59.2 %all-gather.12.cloned.1.call-done = bf16[2,1024,768]{1,2,0:T(8,128)(2,1)} async-done(((bf16[2,128,768]{1,2,0:T(8,128)(2,1)}), bf16[2,1024,768]{1,2,0:T(8,128)(2,1)}) %all-gather.12.cloned.1.call-update) | async-done | bytes 3145744 | tf_op jit(solution)/shard_map/all_gather | solution.py:211
  225.9 35.7 %while.42 = (s32[]{:T(128)}, f32[2,8,2,128]{3,2,1,0:T(2,128)S(1)}, f32[2,8,2,128]{3,2,1,0:T(2,128)S(1)}, f32[2,8,2,128,96]{3,4,2,1,0:T(8,128)}, s32[2]{0:T(128)S...) while((s32[]{:T(128)}, f32[2,8,2,128]{3,2,1,0:T(2,128)S(1)}, ...), condition=%wide.region_4.5_spmd.clone, body=%wide.region_1.4_spmd.clone.sunk | while | flops 829773440 | bytes 66725096 | solution.py:231
  269.6 76.8 %all-gather.24.cloned.1.call-done = bf16[1536,4096]{1,0:T(8,128)(2,1)} async-done(((bf16[1536,1024]{1,0:T(8,128)(2,1)}), bf16[1536,4096]{1,0:T(8,128)(2,1)}) %all-gather.24.cloned.1.call-update) | async-done | bytes 12582928 | tf_op jit(solution)/shard_map/all_gather | solution.py:348
  355.7 74.4 %all-gather.26.cloned.1.call-done = bf16[4096,1536]{1,0:T(8,128)(2,1)} async-done(((bf16[1024,1536]{1,0:T(8,128)(2,1)}), bf16[4096,1536]{1,0:T(8,128)(2,1)}) %all-gather.26.cloned.1.call-update) | async-done | bytes 12582928 | tf_op jit(solution)/shard_map/all_gather | solution.py:350
  430.1 7.0 fusion.45
  439.9 73.9 %all-gather.22.cloned.1.call-done = bf16[1536,4096]{1,0:T(8,128)(2,1)} async-done(((bf16[1536,1024]{1,0:T(8,128)(2,1)}), bf16[1536,4096]{1,0:T(8,128)(2,1)}) %all-gather.22.cloned.1.call-update) | async-done | bytes 12582928 | tf_op jit(solution)/shard_map/all_gather | solution.py:347
  513.8 6.6 fusion.55
  535.6 6.9 fusion.53
  548.5 327.7 %while.43 = (s32[]{:T(128)}, bf16[2,128,8,96]{1,3,2,0:T(8,128)(2,1)}, bf16[2,128,8,96]{1,3,2,0:T(8,128)(2,1)}, f32[2,128,8,2,96]{1,4,3,2,0:T(8,128)}, f32[2,128,...) while((s32[]{:T(128)}, ...), condition=%wide.region_9.10_spmd.clone, body=%wide.region_8.9_spmd.clone.sunk | while | flops 509985280 | bytes 36048588 | solution.py:285
  583.4 8.4 collective-permute-done.1
  626.5 8.4 collective-permute-done.1
  668.8 8.4 collective-permute-done.1
  710.2 8.4 collective-permute-done.1
  750.6 8.4 collective-permute-done.1
  790.5 8.4 collective-permute-done.1
  830.0 8.4 collective-permute-done.1
  867.7 8.4 collective-permute-done.1
  918.8 7.5 fusion.47
  929.4 237.8 %all-reduce.3.cloned.1.call-done = (f32[8,5,1536,16]{2,0,3,1:T(8,128)}, f32[8,1536,16]{1,0,2:T(8,128)}, f32[8,4096,16]{1,0,2:T(8,128)}, f32[8,16,1536]{2,0,1:T(8...) async-done(((f32[8,5,1536,16]{2,0,3,1:T(8,128)}, f32[8,1536,16]{1,0,2:T(8,128)}, ...) | async-done | bytes 14155792 | tf_op jit(solution)/shard_map/psum | solution.py:290
  1167.2 6.8 copy.164
  (626 shorter events, 445.1 us)
Async XLA Ops:
  7.2 27.0 %all-gather.16.cloned.1.call-start = ((), (), s32[]{:S(2)}) async-start(), calls=%async_computation.3 | async-start | bytes 2949120 | tf_op jit(solution)/shard_map/all_gather | solution.py:346
  8.0 51.9 %all-gather.10.cloned.1.call-start = ((), (), s32[]{:S(2)}) async-start(), calls=%async_computation | async-start | bytes 2949120 | tf_op jit(solution)/shard_map/all_gather | solution.py:345
  8.7 90.2 %all-gather.14.cloned.1.call-start = ((), (), s32[]{:S(2)}) async-start(), calls=%async_computation.2 | async-start | bytes 5898240 | tf_op jit(solution)/shard_map/all_gather | solution.py:344
  9.4 152.5 %all-gather.18.cloned.1.call-start = ((), (), s32[]{:S(2)}) async-start(), calls=%async_computation.4 | async-start | bytes 3538944 | tf_op jit(solution)/shard_map/all_gather | solution.py:212
  37.8 188.1 %all-gather.12.cloned.1.call-start = ((), (), s32[]{:S(2)}) async-start(), calls=%async_computation.1 | async-start | bytes 3538944 | tf_op jit(solution)/shard_map/all_gather | solution.py:211
  67.9 195.7 %all-gather.20.cloned.1.call-start = ((), (), s32[]{:S(2)}) async-start(), calls=%async_computation.5 | async-start | bytes 5898240 | tf_op jit(solution)/shard_map/all_gather | solution.py:349
  68.5 277.9 %all-gather.24.cloned.1.call-start = ((), (), s32[]{:S(2)}) async-start(), calls=%async_computation.7 | async-start | bytes 15728640 | tf_op jit(solution)/shard_map/all_gather | solution.py:348
  69.2 360.9 %all-gather.26.cloned.1.call-start = ((), (), s32[]{:S(2)}) async-start(), calls=%async_computation.8 | async-start | bytes 15728640 | tf_op jit(solution)/shard_map/all_gather | solution.py:350
  70.0 443.8 %all-gather.22.cloned.1.call-start = ((), (), s32[]{:S(2)}) async-start(), calls=%async_computation.6 | async-start | bytes 15728640 | tf_op jit(solution)/shard_map/all_gather | solution.py:347
  70.7 1096.4 %all-reduce.3.cloned.1.call-start = ((), (), s32[]{:S(2)}) async-start(), calls=%async_computation.9 | async-start | bytes 28311552 | tf_op jit(solution)/shard_map/psum | solution.py:290
  559.6 23.8 %collective-permute-start = (bf16[2,128,8,96]{1,3,2,0:T(8,128)(2,1)S(1)}, bf16[2,128,8,96]{1,3,2,0:T(8,128)(2,1)}, u32[]{:S(2)}, u32[]{:S(2)}) collective-permute-start(bf16[2,128,8,96]{1,3,2,0:T(8,128)(2,1)S(1)} %copy.307), channel_id=1, source_target_pairs={{0,28},{4,0},{8,4},{12,8},{16,12},{20,16},{24,20},{28,24},{1,29},{... | collective-permute-start | bytes 1179656 | tf_op jit(solution)/shard_map/while/body/eval_jaxpr/ppermute | solution.py:21
  560.7 31.1 %collective-permute-start.1 = (bf16[2,128,8,96]{1,3,2,0:T(8,128)(2,1)S(1)}, bf16[2,128,8,96]{1,3,2,0:T(8,128)(2,1)}, u32[]{:S(2)}, u32[]{:S(2)}) collective-permute-start(bf16[2,128,8,96]{1,3,2,0:T(8,128)(2,1)S(1)} %copy.308), channel_id=1, source_target_pairs={{0,28},{4,0},{8,4},{12,8},{16,12},{20,16},{24,20},{28,24},{1,29},{... | collective-permute-start | bytes 1179656 | tf_op jit(solution)/shard_map/while/body/eval_jaxpr/ppermute | solution.py:21
  603.4 23.2 %collective-permute-start = (bf16[2,128,8,96]{1,3,2,0:T(8,128)(2,1)S(1)}, bf16[2,128,8,96]{1,3,2,0:T(8,128)(2,1)}, u32[]{:S(2)}, u32[]{:S(2)}) collective-permute-start(bf16[2,128,8,96]{1,3,2,0:T(8,128)(2,1)S(1)} %copy.307), channel_id=1, source_target_pairs={{0,28},{4,0},{8,4},{12,8},{16,12},{20,16},{24,20},{28,24},{1,29},{... | collective-permute-start | bytes 1179656 | tf_op jit(solution)/shard_map/while/body/eval_jaxpr/ppermute | solution.py:21
  603.4 31.6 %collective-permute-start.1 = (bf16[2,128,8,96]{1,3,2,0:T(8,128)(2,1)S(1)}, bf16[2,128,8,96]{1,3,2,0:T(8,128)(2,1)}, u32[]{:S(2)}, u32[]{:S(2)}) collective-permute-start(bf16[2,128,8,96]{1,3,2,0:T(8,128)(2,1)S(1)} %copy.308), channel_id=1, source_target_pairs={{0,28},{4,0},{8,4},{12,8},{16,12},{20,16},{24,20},{28,24},{1,29},{... | collective-permute-start | bytes 1179656 | tf_op jit(solution)/shard_map/while/body/eval_jaxpr/ppermute | solution.py:21
  646.6 22.2 %collective-permute-start = (bf16[2,128,8,96]{1,3,2,0:T(8,128)(2,1)S(1)}, bf16[2,128,8,96]{1,3,2,0:T(8,128)(2,1)}, u32[]{:S(2)}, u32[]{:S(2)}) collective-permute-start(bf16[2,128,8,96]{1,3,2,0:T(8,128)(2,1)S(1)} %copy.307), channel_id=1, source_target_pairs={{0,28},{4,0},{8,4},{12,8},{16,12},{20,16},{24,20},{28,24},{1,29},{... | collective-permute-start | bytes 1179656 | tf_op jit(solution)/shard_map/while/body/eval_jaxpr/ppermute | solution.py:21
  646.6 30.6 %collective-permute-start.1 = (bf16[2,128,8,96]{1,3,2,0:T(8,128)(2,1)S(1)}, bf16[2,128,8,96]{1,3,2,0:T(8,128)(2,1)}, u32[]{:S(2)}, u32[]{:S(2)}) collective-permute-start(bf16[2,128,8,96]{1,3,2,0:T(8,128)(2,1)S(1)} %copy.308), channel_id=1, source_target_pairs={{0,28},{4,0},{8,4},{12,8},{16,12},{20,16},{24,20},{28,24},{1,29},{... | collective-permute-start | bytes 1179656 | tf_op jit(solution)/shard_map/while/body/eval_jaxpr/ppermute | solution.py:21
  688.8 21.3 %collective-permute-start = (bf16[2,128,8,96]{1,3,2,0:T(8,128)(2,1)S(1)}, bf16[2,128,8,96]{1,3,2,0:T(8,128)(2,1)}, u32[]{:S(2)}, u32[]{:S(2)}) collective-permute-start(bf16[2,128,8,96]{1,3,2,0:T(8,128)(2,1)S(1)} %copy.307), channel_id=1, source_target_pairs={{0,28},{4,0},{8,4},{12,8},{16,12},{20,16},{24,20},{28,24},{1,29},{... | collective-permute-start | bytes 1179656 | tf_op jit(solution)/shard_map/while/body/eval_jaxpr/ppermute | solution.py:21
  688.9 29.7 %collective-permute-start.1 = (bf16[2,128,8,96]{1,3,2,0:T(8,128)(2,1)S(1)}, bf16[2,128,8,96]{1,3,2,0:T(8,128)(2,1)}, u32[]{:S(2)}, u32[]{:S(2)}) collective-permute-start(bf16[2,128,8,96]{1,3,2,0:T(8,128)(2,1)S(1)} %copy.308), channel_id=1, source_target_pairs={{0,28},{4,0},{8,4},{12,8},{16,12},{20,16},{24,20},{28,24},{1,29},{... | collective-permute-start | bytes 1179656 | tf_op jit(solution)/shard_map/while/body/eval_jaxpr/ppermute | solution.py:21
  730.2 20.4 %collective-permute-start = (bf16[2,128,8,96]{1,3,2,0:T(8,128)(2,1)S(1)}, bf16[2,128,8,96]{1,3,2,0:T(8,128)(2,1)}, u32[]{:S(2)}, u32[]{:S(2)}) collective-permute-start(bf16[2,128,8,96]{1,3,2,0:T(8,128)(2,1)S(1)} %copy.307), channel_id=1, source_target_pairs={{0,28},{4,0},{8,4},{12,8},{16,12},{20,16},{24,20},{28,24},{1,29},{... | collective-permute-start | bytes 1179656 | tf_op jit(solution)/shard_map/while/body/eval_jaxpr/ppermute | solution.py:21
  730.2 28.8 %collective-permute-start.1 = (bf16[2,128,8,96]{1,3,2,0:T(8,128)(2,1)S(1)}, bf16[2,128,8,96]{1,3,2,0:T(8,128)(2,1)}, u32[]{:S(2)}, u32[]{:S(2)}) collective-permute-start(bf16[2,128,8,96]{1,3,2,0:T(8,128)(2,1)S(1)} %copy.308), channel_id=1, source_target_pairs={{0,28},{4,0},{8,4},{12,8},{16,12},{20,16},{24,20},{28,24},{1,29},{... | collective-permute-start | bytes 1179656 | tf_op jit(solution)/shard_map/while/body/eval_jaxpr/ppermute | solution.py:21
  770.6 28.3 %collective-permute-start.1 = (bf16[2,128,8,96]{1,3,2,0:T(8,128)(2,1)S(1)}, bf16[2,128,8,96]{1,3,2,0:T(8,128)(2,1)}, u32[]{:S(2)}, u32[]{:S(2)}) collective-permute-start(bf16[2,128,8,96]{1,3,2,0:T(8,128)(2,1)S(1)} %copy.308), channel_id=1, source_target_pairs={{0,28},{4,0},{8,4},{12,8},{16,12},{20,16},{24,20},{28,24},{1,29},{... | collective-permute-start | bytes 1179656 | tf_op jit(solution)/shard_map/while/body/eval_jaxpr/ppermute | solution.py:21
  810.1 19.9 %collective-permute-start = (bf16[2,128,8,96]{1,3,2,0:T(8,128)(2,1)S(1)}, bf16[2,128,8,96]{1,3,2,0:T(8,128)(2,1)}, u32[]{:S(2)}, u32[]{:S(2)}) collective-permute-start(bf16[2,128,8,96]{1,3,2,0:T(8,128)(2,1)S(1)} %copy.307), channel_id=1, source_target_pairs={{0,28},{4,0},{8,4},{12,8},{16,12},{20,16},{24,20},{28,24},{1,29},{... | collective-permute-start | bytes 1179656 | tf_op jit(solution)/shard_map/while/body/eval_jaxpr/ppermute | solution.py:21
  810.1 28.3 %collective-permute-start.1 = (bf16[2,128,8,96]{1,3,2,0:T(8,128)(2,1)S(1)}, bf16[2,128,8,96]{1,3,2,0:T(8,128)(2,1)}, u32[]{:S(2)}, u32[]{:S(2)}) collective-permute-start(bf16[2,128,8,96]{1,3,2,0:T(8,128)(2,1)S(1)} %copy.308), channel_id=1, source_target_pairs={{0,28},{4,0},{8,4},{12,8},{16,12},{20,16},{24,20},{28,24},{1,29},{... | collective-permute-start | bytes 1179656 | tf_op jit(solution)/shard_map/while/body/eval_jaxpr/ppermute | solution.py:21
  848.7 27.5 %collective-permute-start.1 = (bf16[2,128,8,96]{1,3,2,0:T(8,128)(2,1)S(1)}, bf16[2,128,8,96]{1,3,2,0:T(8,128)(2,1)}, u32[]{:S(2)}, u32[]{:S(2)}) collective-permute-start(bf16[2,128,8,96]{1,3,2,0:T(8,128)(2,1)S(1)} %copy.308), channel_id=1, source_target_pairs={{0,28},{4,0},{8,4},{12,8},{16,12},{20,16},{24,20},{28,24},{1,29},{... | collective-permute-start | bytes 1179656 | tf_op jit(solution)/shard_map/while/body/eval_jaxpr/ppermute | solution.py:21
  (166 other events, 3015.3 us)
Sparse Core Ops, SparseCore 0:
  9.6 24.5 all-gather.15
  35.8 24.0 all-gather.9
  61.4 37.3 all-gather.13
  101.5 60.3 all-gather.17
  163.8 62.0 all-gather.11
  227.3 35.2 all-gather.19
  264.2 82.1 all-gather.23
  348.0 82.0 all-gather.25
  431.7 82.0 all-gather.21
  907.3 259.8 all-reduce.2
where the time goes:
time: 1200 us; the launch traced here: 1190 us
  waiting for transfers between devices  817 us (68%)
  matrix products  199 us (17%)
  local copies, waits for them, and re-layouts  64.3 us (5%)
  other arithmetic  56.8 us (5%)
  starting transfers between devices  40.2 us (3%)
  between operations  15.8 us (1%)
    psum x1, waiting for transfers between devices, table_total(): return lax.psum(rotation_tables, ('ctx', 'fsdp'))  238 us
    ppermute x32, waiting for transfers between devices, from_behind(): return lax.ppermute(x, axis, [(i, (i + by) % size) for i in range(size)])  182 us
    all_gather x1, waiting for transfers between devices, local(): lax.all_gather(up_weight, 'fsdp', axis=1, tiled=True)  76.8 us
    all_gather x1, waiting for transfers between devices, local(): lax.all_gather(down_weight, 'fsdp', axis=0, tiled=True)  74.4 us
    all_gather x1, waiting for transfers between devices, local(): lax.all_gather(gate_weight, 'fsdp', axis=1, tiled=True)  73.9 us
    all_gather x1, waiting for transfers between devices, attend_forward(): part_keys = lax.all_gather(key_flat, 'ctx', axis=1, tiled=True)  59.2 us
    all_gather x1, waiting for transfers between devices, attend_forward(): part_values = lax.all_gather(value_flat, 'ctx', axis=1, tiled=True)  55.5 us
    ppermute x32, starting transfers between devices, from_behind(): return lax.ppermute(x, axis, [(i, (i + by) % size) for i in range(size)])  39.6 us
  transfers between devices with their start and end apart: 42, of which 41 were waited for; matrix products, arithmetic and copies ran while one was open for 16% of the time, Pallas kernels for 0%

commit v1 on v0

--- a/solution.py
+++ b/solution.py
@@ -3,6 +3,8 @@
 import jax
 import jax.numpy as jnp
 from jax import lax
+from jax.experimental import pallas as pl
+from jax.experimental.pallas import tpu as pltpu
 from jax.sharding import PartitionSpec as P
 
 QUERY_HEADS = 16
@@ -461,9 +463,744 @@
     )
 
 
+BF16 = jnp.bfloat16
+F32 = jnp.float32
+MESH_ID = pl.DeviceIdType.MESH
+RANK = 16
+SIDE = 128
+PAD_HEAD = 128
+HALF_PAD = 64
+
+
+def _sem(count):
+    return pltpu.SemaphoreType.DMA((count,))
+
+
+def _place():
+    c = lax.axis_index("ctx")
+    f = lax.axis_index("fsdp")
+    x = f // 2
+    core = f % 2
+    return c, f, x, core, (c, 2 * x + 1 - core), (c, 2 * (1 - x) + core)
+
+
+def _greet(targets):
+    barrier = pltpu.get_barrier_semaphore()
+    for target in targets:
+        pl.semaphore_signal(barrier, inc=1, device_id=target, device_id_type=MESH_ID)
+    pl.semaphore_wait(barrier, len(targets))
+
+
+def _remote(src, dst, send, recv, target):
+    return pltpu.make_async_remote_copy(
+        src_ref=src, dst_ref=dst, send_sem=send, recv_sem=recv, device_id=target, device_id_type=MESH_ID
+    )
+
+
+def _comm_call(kernel, ins, outs, scratch, cid, name, in_space=pl.ANY, out_space=pl.ANY, vmem=None):
+    return pl.pallas_call(
+        kernel,
+        out_shape=outs,
+        in_specs=[pl.BlockSpec(memory_space=in_space)] * len(ins),
+        out_specs=jax.tree.map(lambda _: pl.BlockSpec(memory_space=out_space), outs),
+        scratch_shapes=scratch,
+        compiler_params=pltpu.CompilerParams(
+            collective_id=cid, has_side_effects=True, vmem_limit_bytes=vmem
+        ),
+        name=name,
+    )(*ins)
+
+
+def _gather_body(ins, outs, own_sem, send_sem, recv_sem, place):
+    c, f, x, core, core_peer, x_peer = place
+    h = 1 - core
+    count = len(ins)
+    local = []
+    sends = []
+    for i in range(count):
+        for j in range(2):
+            k = i * 2 + j
+            cp = _remote(
+                ins[i].at[j], outs[i].at[h, j, x], send_sem.at[k], recv_sem.at[k], x_peer
+            )
+            cp.start()
+            sends.append(cp)
+    for i in range(count):
+        for j in range(2):
+            k = i * 2 + j
+            cp = _remote(
+                ins[i].at[j],
+                outs[i].at[h, j, x],
+                send_sem.at[2 * count + k],
+                recv_sem.at[2 * count + k],
+                core_peer,
+            )
+            cp.start()
+            sends.append(cp)
+            lc = pltpu.make_async_copy(ins[i].at[j], outs[i].at[h, j, x], own_sem.at[k])
+            lc.start()
+            local.append(lc)
+    forwards = []
+    for i in range(count):
+        for j in range(2):
+            k = i * 2 + j
+            sends[k].wait_recv()
+            cp = _remote(
+                outs[i].at[h, j, 1 - x],
+                outs[i].at[h, j, 1 - x],
+                send_sem.at[4 * count + k],
+                recv_sem.at[4 * count + k],
+                core_peer,
+            )
+            cp.start()
+            forwards.append(cp)
+    for k in range(2 * count):
+        sends[2 * count + k].wait_recv()
+        forwards[k].wait_recv()
+    for cp in sends + forwards:
+        cp.wait_send()
+    for lc in local:
+        lc.wait()
+
+
+def group_gather(arrays, cid, name):
+    count = len(arrays)
+
+    def kernel(*refs):
+        ins, outs = refs[:count], refs[count : 2 * count]
+        own_sem, send_sem, recv_sem = refs[2 * count :]
+        place = _place()
+        _greet([place[4], place[5]])
+        _gather_body(ins, outs, own_sem, send_sem, recv_sem, place)
+
+    outs = [jax.ShapeDtypeStruct((2, 2, 2) + a.shape[1:], a.dtype) for a in arrays]
+    return _comm_call(
+        kernel, arrays, outs, [_sem(2 * count), _sem(6 * count), _sem(6 * count)], cid, name
+    )
+
+
+def group_scatter(arrays, cid, name):
+    count = len(arrays)
+
+    def kernel(*refs):
+        ins, outs = refs[:count], refs[count : 2 * count]
+        first, staged, second = (
+            refs[2 * count : 3 * count],
+            refs[3 * count : 4 * count],
+            refs[4 * count : 5 * count],
+        )
+        send_sem, recv_sem = refs[5 * count :]
+        c, f, x, core, core_peer, x_peer = _place()
+        h = 1 - core
+        _greet([core_peer, x_peer])
+        one, two = {}, {}
+        for far in (1, 0):
+            for j in range(2):
+                for i in range(count):
+                    k = (i * 2 + j) * 2 + far
+                    xx = 1 - x if far else x
+                    cp = _remote(
+                        ins[i].at[1 - h, j, xx],
+                        first[i].at[far, j],
+                        send_sem.at[k],
+                        recv_sem.at[k],
+                        core_peer,
+                    )
+                    cp.start()
+                    one[(i, j, far)] = cp
+        for j in range(2):
+            for i in range(count):
+                one[(i, j, 1)].wait_recv()
+                staged[i][j] = (
+                    ins[i][h, j, 1 - x].astype(F32) + first[i][1, j].astype(F32)
+                ).astype(BF16)
+                k = 4 * count + i * 2 + j
+                cp = _remote(
+                    staged[i].at[j], second[i].at[j], send_sem.at[k], recv_sem.at[k], x_peer
+                )
+                cp.start()
+                two[(i, j)] = cp
+        for j in range(2):
+            for i in range(count):
+                one[(i, j, 0)].wait_recv()
+                outs[i][j] = ins[i][h, j, x].astype(F32) + first[i][0, j].astype(F32)
+        for j in range(2):
+            for i in range(count):
+                two[(i, j)].wait_recv()
+                outs[i][j] = outs[i][j] + second[i][j].astype(F32)
+        for cp in list(one.values()) + list(two.values()):
+            cp.wait_send()
+
+    outs = [jax.ShapeDtypeStruct((2,) + a.shape[3:], F32) for a in arrays]
+    rows = [a.shape[3:] for a in arrays]
+    scratch = (
+        [pltpu.VMEM((2, 2) + r, BF16) for r in rows]
+        + [pltpu.VMEM((2,) + r, BF16) for r in rows]
+        + [pltpu.VMEM((2,) + r, BF16) for r in rows]
+        + [_sem(6 * count), _sem(6 * count)]
+    )
+    return _comm_call(
+        kernel, arrays, outs, scratch, cid, name, pltpu.VMEM, pltpu.VMEM, 40 * 1024 * 1024
+    )
+
+
+def take_in(tokens, cotangent, cid):
+    def kernel(tok, cot, tok_own, cot_own, tok_all, cot_all, land_s, land_r, own_sem, send_sem, recv_sem):
+        place = _place()
+        c, f, x, core, core_peer, x_peer = place
+        h = 1 - core
+        slot = c // 2 + 4 * (c % 2)
+        barrier = pltpu.get_barrier_semaphore()
+        for j in range(2):
+            pl.semaphore_signal(
+                barrier, inc=1, device_id=(x + 2 * j + 4 * h, slot // 2), device_id_type=MESH_ID
+            )
+        for target in (core_peer, x_peer):
+            pl.semaphore_signal(barrier, inc=1, device_id=target, device_id_type=MESH_ID)
+        pl.semaphore_wait(barrier, 4)
+        to_f = 2 * (c % 2) + 1 - c // 4
+        to_j = (c // 2) % 2
+        moves = []
+        for a, (src, dst) in enumerate(((tok, tok_own), (cot, cot_own))):
+            for half in range(2):
+                s = 2 * f + half
+                to_c = (s % 4) * 2 + s // 4
+                cp = _remote(
+                    src.at[half], dst.at[to_j], land_s.at[2 * a + half], land_r.at[2 * a + to_j], (to_c, to_f)
+                )
+                cp.start()
+                moves.append(cp)
+        for a in range(2):
+            for j in range(2):
+                dst = (tok_own, cot_own)[a]
+                pltpu.make_async_copy(dst.at[j], dst.at[j], land_r.at[2 * a + j]).wait()
+        _gather_body((tok_own, cot_own), (tok_all, cot_all), own_sem, send_sem, recv_sem, place)
+        for cp in moves:
+            cp.wait_send()
+
+    own = jax.ShapeDtypeStruct(tokens.shape, tokens.dtype)
+    whole = jax.ShapeDtypeStruct((2, 2, 2) + tokens.shape[1:], tokens.dtype)
+    return _comm_call(
+        kernel,
+        [tokens, cotangent],
+        [own, own, whole, whole],
+        [_sem(4), _sem(4), _sem(4), _sem(12), _sem(12)],
+        cid,
+        "take_in",
+    )
+
+
+def give_back(arrays, smalls, cid):
+    count, extra = len(arrays), len(smalls)
+
+    def kernel(*refs):
+        ins, small_in = refs[:count], refs[count : count + extra]
+        outs = refs[count + extra : 2 * count + extra]
+        small_out = refs[2 * count + extra : 2 * count + 2 * extra]
+        out_s, out_r, own_sem, send_sem, recv_sem = refs[2 * count + 2 * extra :]
+        place = _place()
+        c, f, x, core, core_peer, x_peer = place
+        h = 1 - core
+        slot = c // 2 + 4 * (c % 2)
+        barrier = pltpu.get_barrier_semaphore()
+        from_f = 2 * (c % 2) + 1 - c // 4
+        for half in range(2):
+            s = 2 * f + half
+            pl.semaphore_signal(
+                barrier, inc=1, device_id=((s % 4) * 2 + s // 4, from_f), device_id_type=MESH_ID
+            )
+        for target in (core_peer, x_peer):
+            pl.semaphore_signal(barrier, inc=1, device_id=target, device_id_type=MESH_ID)
+        pl.semaphore_wait(barrier, 4)
+        moves = []
+        place_in = slot % 2
+        for i in range(count):
+            for j in range(2):
+                cp = _remote(
+                    ins[i].at[j],
+                    outs[i].at[place_in],
+                    out_s.at[2 * i + j],
+                    out_r.at[2 * i + place_in],
+                    (x + 2 * j + 4 * h, slot // 2),
+                )
+                cp.start()
+                moves.append(cp)
+        _gather_body(small_in, small_out, own_sem, send_sem, recv_sem, place)
+        for i in range(count):
+            for half in range(2):
+                pltpu.make_async_copy(
+                    outs[i].at[half], outs[i].at[half], out_r.at[2 * i + half]
+                ).wait()
+        for cp in moves:
+            cp.wait_send()
+
+    outs = [jax.ShapeDtypeStruct(a.shape, a.dtype) for a in arrays]
+    outs += [jax.ShapeDtypeStruct((2, 2, 2) + a.shape[1:], a.dtype) for a in smalls]
+    return _comm_call(
+        kernel,
+        list(arrays) + list(smalls),
+        outs,
+        [_sem(2 * count), _sem(2 * count), _sem(2 * extra), _sem(6 * extra), _sem(6 * extra)],
+        cid,
+        "give_back",
+    )
+
+
+def attend_call(proj, cosine, sine, length):
+    rows = proj.shape[0]
+    step = 256
+    scale = HEAD_DIM ** (-0.5)
+    lane = PAD_HEAD
+
+    def kernel(len_ref, proj_ref, cos_ref, sin_ref, att_ref, qkv_ref, lse_ref):
+        live = len_ref[0]
+        for part in range(6):
+            cols = slice(part * lane, (part + 1) * lane)
+            v = proj_ref[:, cols]
+            v = v * cos_ref[...] + pltpu.roll(v, HALF_PAD, 1) * sin_ref[...]
+            qkv_ref[:, cols] = v.astype(BF16)
+        qkv_ref[:, 6 * lane :] = proj_ref[:, 6 * lane :].astype(BF16)
+        for block in range(rows // step):
+            keys = (block + 1) * step
+            row = pl.ds(block * step, step)
+            qpos = block * step + lax.broadcasted_iota(jnp.int32, (step, keys), 0)
+            kpos = lax.broadcasted_iota(jnp.int32, (step, keys), 1)
+            allowed = (kpos <= qpos) & (kpos < live)
+            pieces = []
+            stats = jnp.zeros((step, lane), F32)
+            lanes = lax.broadcasted_iota(jnp.int32, (step, lane), 1)
+            for head in range(4):
+                q = qkv_ref[row, head * lane : (head + 1) * lane]
+                kv = head // 2
+                k = qkv_ref[:keys, (4 + kv) * lane : (5 + kv) * lane]
+                v = qkv_ref[:keys, (6 + kv) * lane : (7 + kv) * lane]
+                s = lax.dot_general(q, k, (((1,), (1,)), ((), ())), preferred_element_type=F32)
+                s = jnp.where(allowed, s * scale, NEGATIVE)
+                top = jnp.max(s, axis=1, keepdims=True)
+                p = jnp.where(allowed, jnp.exp(s - top), 0.0)
+                total = jnp.sum(p, axis=1, keepdims=True)
+                o = jnp.dot(p.astype(BF16), v, preferred_element_type=F32) / total
+                pieces.append(o[:, :HEAD_DIM])
+                stats = jnp.where(lanes == head, top + jnp.log(total), stats)
+            att_ref[row, :] = jnp.concatenate(pieces, axis=1).astype(BF16)
+            lse_ref[row, :] = stats
+
+    vmem = pl.BlockSpec(memory_space=pltpu.VMEM)
+    return pl.pallas_call(
+        kernel,
+        out_shape=(
+            jax.ShapeDtypeStruct((rows, 4 * HEAD_DIM), BF16),
+            jax.ShapeDtypeStruct(proj.shape, BF16),
+            jax.ShapeDtypeStruct((rows, lane), F32),
+        ),
+        in_specs=[pl.BlockSpec(memory_space=pltpu.SMEM), vmem, vmem, vmem],
+        out_specs=(vmem, vmem, vmem),
+        compiler_params=pltpu.CompilerParams(vmem_limit_bytes=48 * 1024 * 1024),
+        name="attend",
+    )(length, proj, cosine, sine)
+
+
+def attend_back_call(qkv, stats, grad_att, cosine, sine, length):
+    rows = qkv.shape[0]
+    step = 256
+    scale = HEAD_DIM ** (-0.5)
+    lane = PAD_HEAD
+
+    def kernel(len_ref, qkv_ref, lse_ref, g_ref, cos_ref, sin_ref, out_ref, dk_ref, dv_ref, do_ref):
+        live = len_ref[0]
+        pad = jnp.zeros((rows, lane - HEAD_DIM), BF16)
+        for head in range(4):
+            do_ref[head] = jnp.concatenate(
+                [g_ref[:, head * HEAD_DIM : (head + 1) * HEAD_DIM], pad], axis=1
+            )
+        dk_ref[...] = jnp.zeros_like(dk_ref)
+        dv_ref[...] = jnp.zeros_like(dv_ref)
+        for block in range(rows // step):
+            keys = (block + 1) * step
+            row = pl.ds(block * step, step)
+            qpos = block * step + lax.broadcasted_iota(jnp.int32, (step, keys), 0)
+            kpos = lax.broadcasted_iota(jnp.int32, (step, keys), 1)
+            allowed = (kpos <= qpos) & (kpos < live)
+            cos, sin = cos_ref[row, :], sin_ref[row, :]
+            for head in range(4):
+                kv = head // 2
+                q = qkv_ref[row, head * lane : (head + 1) * lane]
+                k = qkv_ref[:keys, (4 + kv) * lane : (5 + kv) * lane]
+                v = qkv_ref[:keys, (6 + kv) * lane : (7 + kv) * lane]
+                do = do_ref[head, row, :]
+                s = lax.dot_general(q, k, (((1,), (1,)), ((), ())), preferred_element_type=F32)
+                p = jnp.where(allowed, jnp.exp(s * scale - lse_ref[row, head : head + 1]), 0.0)
+                dp = lax.dot_general(do, v, (((1,), (1,)), ((), ())), preferred_element_type=F32)
+                dot = jnp.sum(p * dp, axis=1, keepdims=True)
+                ds = (p * (dp - dot)).astype(BF16)
+                dq = scale * jnp.dot(ds, k, preferred_element_type=F32)
+                dq = dq * cos - pltpu.roll(dq, HALF_PAD, 1) * sin
+                out_ref[row, head * lane : (head + 1) * lane] = dq.astype(BF16)
+                dk_ref[kv, :keys] += lax.dot_general(
+                    ds, q, (((0,), (0,)), ((), ())), preferred_element_type=F32
+                )
+                dv_ref[kv, :keys] += lax.dot_general(
+                    p.astype(BF16), do, (((0,), (0,)), ((), ())), preferred_element_type=F32
+                )
+        for kv in range(2):
+            dk = scale * dk_ref[kv]
+            dk = dk * cos_ref[...] - pltpu.roll(dk, HALF_PAD, 1) * sin_ref[...]
+            out_ref[:, (4 + kv) * lane : (5 + kv) * lane] = dk.astype(BF16)
+            out_ref[:, (6 + kv) * lane : (7 + kv) * lane] = dv_ref[kv].astype(BF16)
+
+    vmem = pl.BlockSpec(memory_space=pltpu.VMEM)
+    return pl.pallas_call(
+        kernel,
+        out_shape=jax.ShapeDtypeStruct(qkv.shape, BF16),
+        in_specs=[pl.BlockSpec(memory_space=pltpu.SMEM)] + [vmem] * 5,
+        out_specs=vmem,
+        scratch_shapes=[
+            pltpu.VMEM((2, rows, lane), F32),
+            pltpu.VMEM((2, rows, lane), F32),
+            pltpu.VMEM((4, rows, lane), BF16),
+        ],
+        compiler_params=pltpu.CompilerParams(vmem_limit_bytes=48 * 1024 * 1024),
+        name="attend_back",
+    )(length, qkv, stats, grad_att, cosine, sine)
+
+
+def gather_all(piece, cid):
+    def kernel(src, out, own_sem, send_sem, recv_sem):
+        c = lax.axis_index("ctx")
+        f = lax.axis_index("fsdp")
+        me = c * 4 + f
+        barrier = pltpu.get_barrier_semaphore()
+
+        def greet(step, carry):
+            to = lax.rem(me + step, 32)
+            pl.semaphore_signal(barrier, inc=1, device_id=(to // 4, to % 4), device_id_type=MESH_ID)
+            return carry
+
+        lax.fori_loop(1, 32, greet, 0)
+        pl.semaphore_wait(barrier, 31)
+        lc = pltpu.make_async_copy(src, out.at[c, f], own_sem)
+        lc.start()
+
+        def copy(step):
+            to = lax.rem(me + step, 32)
+            return _remote(
+                src, out.at[c, f], send_sem.at[step], recv_sem.at[step], (to // 4, to % 4)
+            )
+
+        def send(step, carry):
+            copy(step).start()
+            return carry
+
+        lax.fori_loop(1, 32, send, 0)
+
+        def done(step, carry):
+            copy(step).wait_recv()
+            copy(step).wait_send()
+            return carry
+
+        lax.fori_loop(1, 32, done, 0)
+        lc.wait()
+
+    return _comm_call(
+        kernel,
+        [piece],
+        jax.ShapeDtypeStruct((8, 4) + piece.shape, piece.dtype),
+        [pltpu.SemaphoreType.DMA(()), _sem(32), _sem(32)],
+        cid,
+        "gather_all",
+    )
+
+
+def dot(left, right):
+    return jnp.dot(left, right, preferred_element_type=F32)
+
+
+def dot_t(left, right):
+    return lax.dot_general(left, right, (((1,), (1,)), ((), ())), preferred_element_type=F32)
+
+
+def dot_rows(left, right):
+    return lax.dot_general(left, right, (((0,), (0,)), ((), ())), preferred_element_type=F32)
+
+
+def side_pad(value):
+    return jnp.pad(value, ((0, 0), (0, SIDE - value.shape[1])))
+
+
+def blocks(value):
+    return value.reshape(2, 2, 2, 128, value.shape[-1])
+
+
+def own_blocks(value):
+    return value.reshape(2, 128, value.shape[-1])
+
+
+def flat(value):
+    return value.reshape(-1, value.shape[-1])
+
+
+def slot_local(
+    tokens,
+    cotangent,
+    lengths,
+    slot_adapter_index,
+    attention_norm_gain,
+    feedforward_norm_gain,
+    query_weight,
+    key_weight,
+    value_weight,
+    output_weight,
+    gate_weight,
+    up_weight,
+    down_weight,
+    adapter_input_first,
+    adapter_output_first,
+    adapter_down_first,
+    adapter_query_second,
+    adapter_key_value_second,
+    adapter_output_second,
+    adapter_gate_up_second,
+    adapter_down_second,
+):
+    width = tokens.shape[-1]
+    hidden_units = gate_weight.shape[1]
+    quarter = width // 4
+    c = lax.axis_index("ctx")
+    f = lax.axis_index("fsdp")
+    x, core = f // 2, f % 2
+    slot = c // 2 + 4 * (c % 2)
+    length = lax.dynamic_slice_in_dim(lengths, slot, 1, 0)
+    adapter = slot_adapter_index[slot]
+
+    def pick(table):
+        return lax.dynamic_index_in_dim(table, adapter, 0, keepdims=False)
+
+    def cut(value, axis, size):
+        return lax.dynamic_slice_in_dim(value, f * size, size, axis)
+
+    first_in = pick(adapter_input_first)
+    first_out = pick(adapter_output_first)
+    first_down = pick(adapter_down_first)
+    second_q = cut(pick(adapter_query_second), 1, query_weight.shape[1])
+    second_kv = cut(pick(adapter_key_value_second), 2, key_weight.shape[1])
+    second_o = pick(adapter_output_second)
+    second_gu = cut(pick(adapter_gate_up_second), 2, hidden_units)
+    second_d = pick(adapter_down_second)
+    first_o_own = cut(first_out, 0, output_weight.shape[0])
+    first_d_own = cut(first_down, 0, hidden_units)
+
+    def pad_turned(w):
+        rows = w.shape[0]
+        w = w.reshape(rows, -1, 2, HEAD_DIM // 2)
+        w = jnp.pad(w, ((0, 0), (0, 0), (0, 0), (0, HALF_PAD - HEAD_DIM // 2)))
+        return w.reshape(rows, -1)
+
+    def pad_plain(w):
+        rows = w.shape[0]
+        w = w.reshape(rows, -1, HEAD_DIM)
+        w = jnp.pad(w, ((0, 0), (0, 0), (0, PAD_HEAD - HEAD_DIM)))
+        return w.reshape(rows, -1)
+
+    def unpad_turned(g):
+        rows = g.shape[0]
+        return g.reshape(rows, -1, 2, HALF_PAD)[..., : HEAD_DIM // 2].reshape(rows, -1)
+
+    def unpad_plain(g):
+        rows = g.shape[0]
+        return g.reshape(rows, -1, PAD_HEAD)[..., :HEAD_DIM].reshape(rows, -1)
+
+    weight_all = jnp.concatenate(
+        [pad_turned(query_weight), pad_turned(key_weight), pad_plain(value_weight)], axis=1
+    )
+    zero_q = jnp.zeros((RANK, 4 * PAD_HEAD), BF16)
+    zero_k = jnp.zeros((RANK, 2 * PAD_HEAD), BF16)
+    second_all = jnp.concatenate(
+        [
+            jnp.concatenate([pad_turned(second_q), zero_k, zero_k], axis=1),
+            jnp.concatenate([zero_q, pad_turned(second_kv[0]), zero_k], axis=1),
+            jnp.concatenate([zero_q, zero_k, pad_plain(second_kv[1])], axis=1),
+        ],
+        axis=0,
+    )
+    first_all = jnp.concatenate([first_in[0], first_in[1], first_in[2]], axis=1)
+    first_gu = jnp.concatenate([first_in[3], first_in[4]], axis=1)
+
+    half = HEAD_DIM // 2
+    rows = 4 * 2 * tokens.shape[1]
+    freqs = ROPE_BASE ** (-(jnp.arange(half, dtype=F32) * 2.0 / HEAD_DIM))
+    angles = jnp.arange(rows, dtype=jnp.int32).astype(F32)[:, None] * freqs[None, :]
+    gap = jnp.zeros((rows, HALF_PAD - half), F32)
+    cos, sin = jnp.cos(angles), jnp.sin(angles)
+    cosine = jnp.concatenate([cos, gap, cos, gap], axis=1)
+    sine = jnp.concatenate([-sin, gap, sin, gap], axis=1)
+
+    tok_own, cot_own, tok_all, cot_all = take_in(tokens, cotangent, 0)
+    live_rows = (jnp.arange(rows, dtype=jnp.int32) < length[0])[:, None]
+    block_of = x + 4 * (1 - core) + 2 * jnp.arange(2, dtype=jnp.int32)
+    own_pos = (block_of[:, None] * 128 + jnp.arange(128, dtype=jnp.int32)[None, :]).reshape(-1)
+    own_live = (own_pos < length[0])[:, None]
+    grad_out = jnp.where(live_rows, flat(cot_all), jnp.zeros((), BF16))
+    grad_out_own = jnp.where(own_live, flat(cot_own), jnp.zeros((), BF16))
+
+    tokens_f = flat(tok_all).astype(F32)
+    normed_one = (tokens_f * rms_factor(tokens_f) * attention_norm_gain).astype(BF16)
+    inner_qkv = dot(normed_one, first_all).astype(BF16)
+    proj = dot(normed_one, weight_all) + ADAPTER_SCALE * dot(inner_qkv, second_all)
+    attn_b, qkv, stats = attend_call(proj, cosine, sine, length)
+
+    sums, side = group_scatter(
+        [
+            blocks(dot(attn_b, output_weight).astype(BF16)),
+            blocks(side_pad(dot(attn_b, first_o_own)).astype(BF16)),
+        ],
+        1,
+        "scatter_o",
+    )
+    inner_o_own = flat(side)[:, :RANK].astype(BF16)
+    own_f = flat(tok_own).astype(F32)
+    resid = own_f + flat(sums) + ADAPTER_SCALE * dot(inner_o_own, second_o)
+    factor_two = rms_factor(resid)
+    normed_two_own = (resid * factor_two * feedforward_norm_gain).astype(BF16)
+    normed_two, side_all = group_gather(
+        [own_blocks(normed_two_own), own_blocks(side_pad(inner_o_own))], 2, "gather_two"
+    )
+    normed_two = flat(normed_two)
+    inner_o = flat(side_all)[:, :RANK]
+
+    inner_gu = dot(normed_two, first_gu).astype(BF16)
+    gate = dot(normed_two, gate_weight) + ADAPTER_SCALE * dot(inner_gu[:, :RANK], second_gu[0])
+    up_proj = dot(normed_two, up_weight) + ADAPTER_SCALE * dot(inner_gu[:, RANK:], second_gu[1])
+    sigmoid_gate = jax.nn.sigmoid(gate)
+    hidden = (gate * sigmoid_gate * up_proj).astype(BF16)
+    grad_inner_d = (ADAPTER_SCALE * dot_t(grad_out, second_d)).astype(BF16)
+    grad_hidden = dot_t(grad_out, down_weight) + dot_t(grad_inner_d, first_d_own)
+    grad_gate = (grad_hidden * up_proj * sigmoid_gate * (1.0 + gate * (1.0 - sigmoid_gate))).astype(
+        BF16
+    )
+    grad_up = (grad_hidden * gate * sigmoid_gate).astype(BF16)
+    grad_two = (dot_t(grad_gate, gate_weight) + dot_t(grad_up, up_weight)).astype(BF16)
+    side_gu = ADAPTER_SCALE * jnp.concatenate(
+        [dot_t(grad_gate, second_gu[0]), dot_t(grad_up, second_gu[1])], axis=1
+    )
+    sums, side = group_scatter(
+        [blocks(grad_two), blocks(side_pad(side_gu).astype(BF16))], 3, "scatter_two"
+    )
+    grad_inner_gu_own = flat(side)[:, : 2 * RANK].astype(BF16)
+    grad_normed_two = (
+        (flat(sums) + dot_t(grad_inner_gu_own, first_gu)).astype(BF16).astype(F32)
+    )
+    grad_resid = grad_out_own.astype(F32) + norm_back(
+        resid, factor_two, feedforward_norm_gain, grad_normed_two
+    )
+    grad_low_own = grad_resid.astype(BF16)
+
+    out_sums, out_side = group_scatter(
+        [
+            blocks(dot(hidden, down_weight).astype(BF16)),
+            blocks(side_pad(dot(hidden, first_d_own)).astype(BF16)),
+        ],
+        4,
+        "scatter_out",
+    )
+    inner_d_own = flat(out_side)[:, :RANK].astype(BF16)
+    out_own = jnp.where(
+        own_live, resid + flat(out_sums) + ADAPTER_SCALE * dot(inner_d_own, second_d), 0.0
+    ).astype(BF16)
+
+    grad_low, side_all = group_gather(
+        [
+            own_blocks(grad_low_own),
+            own_blocks(side_pad(jnp.concatenate([grad_inner_gu_own, inner_d_own], axis=1))),
+        ],
+        5,
+        "gather_resid",
+    )
+    grad_low = flat(grad_low)
+    side_all = flat(side_all)
+    grad_inner_gu = side_all[:, : 2 * RANK]
+    inner_d = side_all[:, 2 * RANK : 3 * RANK]
+    grad_inner_o = (ADAPTER_SCALE * dot_t(grad_low, second_o)).astype(BF16)
+    grad_att = (dot_t(grad_low, output_weight) + dot_t(grad_inner_o, first_o_own)).astype(BF16)
+    grad_qkv = attend_back_call(qkv, stats, grad_att, cosine, sine, length)
+    grad_one = dot_t(grad_qkv, weight_all).astype(BF16)
+    side_qkv = ADAPTER_SCALE * dot_t(grad_qkv, second_all)
+    sums, side = group_scatter(
+        [blocks(grad_one), blocks(side_pad(side_qkv).astype(BF16))], 6, "scatter_one"
+    )
+    grad_inner_own = flat(side)[:, : 3 * RANK].astype(BF16)
+    grad_normed_one = (flat(sums) + dot_t(grad_inner_own, first_all)).astype(BF16).astype(F32)
+    grad_tok_own = grad_resid + norm_back(
+        own_f, rms_factor(own_f), attention_norm_gain, grad_normed_one
+    )
+    out_tokens, grad_tokens, side_all = give_back(
+        [own_blocks(out_own), own_blocks(grad_tok_own.astype(BF16))],
+        [own_blocks(side_pad(grad_inner_own))],
+        7,
+    )
+    grad_inner_qkv = flat(side_all)[:, : 3 * RANK]
+
+    one_cut = cut(normed_one, 1, quarter)
+    two_cut = cut(normed_two, 1, quarter)
+    in_qkv = dot_rows(grad_inner_qkv, one_cut)
+    in_gu = dot_rows(grad_inner_gu, two_cut)
+    o_a = dot_rows(grad_inner_o, attn_b)
+    d_a = dot_rows(grad_inner_d, hidden)
+    all_b = ADAPTER_SCALE * dot_rows(inner_qkv, grad_qkv)
+    q_b = unpad_turned(all_b[:RANK, : 4 * PAD_HEAD])
+    k_b = unpad_turned(all_b[RANK : 2 * RANK, 4 * PAD_HEAD : 6 * PAD_HEAD])
+    v_b = unpad_plain(all_b[2 * RANK :, 6 * PAD_HEAD :])
+    o_b = ADAPTER_SCALE * dot_rows(inner_o, cut(grad_low, 1, quarter))
+    g_b = ADAPTER_SCALE * dot_rows(inner_gu[:, :RANK], grad_gate)
+    u_b = ADAPTER_SCALE * dot_rows(inner_gu[:, RANK:], grad_up)
+    d_b = ADAPTER_SCALE * dot_rows(inner_d, cut(grad_out, 1, quarter))
+    parts = [
+        in_qkv[:RANK],
+        in_qkv[RANK : 2 * RANK],
+        in_qkv[2 * RANK :],
+        in_gu[:RANK],
+        in_gu[RANK:],
+        o_a,
+        d_a,
+        q_b,
+        k_b,
+        v_b,
+        o_b,
+        g_b,
+        u_b,
+        d_b,
+    ]
+    gathered = gather_all(jnp.concatenate(parts, axis=1).astype(BF16), 8)
+    group_slot = [cc // 2 + 4 * (cc % 2) for cc in range(8)]
+    group_adapter = slot_adapter_index[jnp.array(group_slot, dtype=jnp.int32)]
+    onehot = (
+        group_adapter[:, None] == jnp.arange(adapter_input_first.shape[0], dtype=jnp.int32)[None, :]
+    ).astype(BF16)
+    tables = jnp.einsum("sa,sfrn->arfn", onehot, gathered, preferred_element_type=F32)
+    full = []
+    start = 0
+    for part in parts:
+        n = part.shape[1]
+        full.append(tables[..., start : start + n].reshape(tables.shape[0], RANK, 4 * n))
+        start += n
+    turn = lambda t: jnp.swapaxes(t, 1, 2)
+    return (
+        out_tokens,
+        grad_tokens.astype(F32),
+        jnp.stack([turn(t) for t in full[:5]], axis=1),
+        turn(full[5]),
+        turn(full[6]),
+        full[7],
+        jnp.stack([full[8], full[9]], axis=1),
+        full[10],
+        jnp.stack([full[11], full[12]], axis=1),
+        full[13],
+    )
+
+
 def solution(mesh):
+    one_slot = mesh.shape["ctx"] == 8 and mesh.shape["fsdp"] == 4
     return jax.shard_map(
-        local,
+        slot_local if one_slot else local,
         mesh=mesh,
         in_specs=(
             P("fsdp", "ctx", None),

time: 1200 us -> 736 us (0.61)
  the two profiles are of different devices: /device:TPU:3 before, /device:TPU:15 now
where the time goes in v1:
time: 736 us; the launch traced here: 731 us
  Pallas kernels  503 us (68%)
  local copies, waits for them, and re-layouts  102 us (14%)
  matrix products  98.5 us (13%)
  other arithmetic  23.3 us (3%)
    pallas_call x9, Pallas kernels, _comm_call(): pl.pallas_call(kernel, out_shape=outs, in_specs=[pl.BlockSpec(memory_spac...  478 us
    dot_general x14, matrix products, dot_t(): lax.dot_general(left, right, (((1,), (1,)), ((), ())), preferred_element_...  39.6 us
    dot_general x14, matrix products, dot(): return jnp.dot(left, right, preferred_element_type=F32)  39.4 us
    unnamed x191, local copies, waits for them, and re-layouts  36.6 us
    slice x17, local copies, waits for them, and re-layouts, slot_local(): tables[..., start:start + n].reshape(tables.shape[0], RANK, 4 * n)  29.3 us
    reshape x10, local copies, waits for them, and re-layouts, slot_local(): tables[..., start:start + n].reshape(tables.shape[0], RANK, 4 * n)  17.4 us

profile of v1, /device:TPU:15, one launch (start us, length us, event | category | flops | bytes accessed | tf_op | source)
XLA Modules:
  0.0 731.3 jit_solution(3023967672760820320)
XLA Ops:
  5.6 73.9 %take_in.1 = (bf16[2,128,1536]{2,1,0:T(8,128)(2,1)}, bf16[2,128,1536]{2,1,0:T(8,128)(2,1)}, bf16[2,2,2,128,1536]{4,3,2,1,0:T(8,128)(2,1)}, bf16[2,2,2,128,1536]{4,3,2,1,0:T(8,128)(2,1)}) custom-call(bf16[2,128,1536]{2,1,0:T(8,128)(2,1)} %tok.1, bf16[2,128,1536]{2,1,0:T(8,128)(2,1)} %cot.1), custom_call_target="tpu_custom_call" | custom-call | tf_op jit(solution)/shard_map/take_in/pallas_call | solution.py:501
  103.7 10.3 %attend.1 = (bf16[1024,384]{1,0:T(8,128)(2,1)S(1)}, bf16[1024,1024]{1,0:T(8,128)(2,1)S(1)}, f32[1024,128]{1,0:T(8,128)S(1)}) custom-call(s32[1]{0:T(128)} %dynamic_slice.57.len_ref, f32[1024,1024]{1,0:T(8,128)} %multiply_add_fusion.2.proj_ref, f32[1024,128]{1,0:T(8,128)S(1)} %get-tuple-element.104.cos_ref, f32[1024,128]{1,0:T(8,128)S(1)} %get-tuple-element.103.sin_ref), custom_call_target="tpu_custom_call" | custom-call | tf_op jit(solution)/shard_map/attend/pallas_call | solution.py:789
  114.1 3.5 convolution_convert_fusion
  122.1 38.9 %scatter_o.1 = (f32[2,128,1536]{2,1,0:T(8,128)S(1)}, f32[2,128,128]{2,1,0:T(8,128)S(1)}) custom-call(bf16[2,2,2,128,1536]{4,3,2,1,0:T(8,128)(2,1)S(1)} %bitcast.198, bf16[2,2,2,128,128]{4,3,2,1,0:T(8,128)(2,1)S(1)} %bitcast.205), custom_call_target="tpu_custom_call" | custom-call | tf_op jit(solution)/shard_map/scatter_o/pallas_call | solution.py:501
  165.3 28.2 %gather_two.1 = (bf16[2,2,2,128,1536]{4,3,2,1,0:T(8,128)(2,1)}, bf16[2,2,2,128,128]{4,3,2,1,0:T(8,128)(2,1)}) custom-call(bf16[2,128,1536]{2,1,0:T(8,128)(2,1)} %bitcast.219, bf16[2,128,128]{2,1,0:T(8,128)(2,1)} %bitcast.242), custom_call_target="tpu_custom_call" | custom-call | tf_op jit(solution)/shard_map/gather_two/pallas_call | solution.py:501
  193.6 8.4 %fusion.104 = f32[1024,1024]{1,0:T(8,128)} fusion(bf16[1024,1536]{1,0:T(8,128)(2,1)} %bitcast.208, bf16[1536,1024]{1,0:T(8,128)(2,1)} %param.33), kind=kOutput, calls=%fused_computation.197 | convolution fusion | flops 3221225472 | bytes 10485760 | tf_op jit(solution)/shard_map/dot_general | solution.py:915
  213.5 3.4 fusion.105
  219.6 3.7 multiply_convert_fusion
  226.0 4.8 convolution_convert_fusion.2
  234.4 22.1 %scatter_out.1 = (f32[2,128,1536]{2,1,0:T(8,128)S(1)}, f32[2,128,128]{2,1,0:T(8,128)S(1)}) custom-call(bf16[2,2,2,128,1536]{4,3,2,1,0:T(8,128)(2,1)S(1)} %bitcast.199, bf16[2,2,2,128,128]{4,3,2,1,0:T(8,128)(2,1)S(1)} %bitcast.206), custom_call_target="tpu_custom_call" | custom-call | tf_op jit(solution)/shard_map/scatter_out/pallas_call | solution.py:501
  262.0 6.1 fusion.106
  268.2 4.2 add_convert_fusion
  272.3 22.9 %scatter_two.1 = (f32[2,128,1536]{2,1,0:T(8,128)S(1)}, f32[2,128,128]{2,1,0:T(8,128)S(1)}) custom-call(bf16[2,2,2,128,1536]{4,3,2,1,0:T(8,128)(2,1)S(1)} %bitcast.200, bf16[2,2,2,128,128]{4,3,2,1,0:T(8,128)(2,1)S(1)} %bitcast.203), custom_call_target="tpu_custom_call" | custom-call | tf_op jit(solution)/shard_map/scatter_two/pallas_call | solution.py:501
  299.8 4.6 fusion.96
  304.4 27.5 %gather_resid.1 = (bf16[2,2,2,128,1536]{4,3,2,1,0:T(8,128)(2,1)}, bf16[2,2,2,128,128]{4,3,2,1,0:T(8,128)(2,1)}) custom-call(bf16[2,128,1536]{2,1,0:T(8,128)(2,1)} %bitcast.217, bf16[2,128,128]{2,1,0:T(8,128)(2,1)} %bitcast.241), custom_call_target="tpu_custom_call" | custom-call | tf_op jit(solution)/shard_map/gather_resid/pallas_call | solution.py:501
  342.8 14.4 %attend_back.1 = bf16[1024,1024]{1,0:T(8,128)(2,1)S(1)} custom-call(s32[1]{0:T(128)} %dynamic_slice.57.len_ref, bf16[1024,1024]{1,0:T(8,128)(2,1)} %copy-done.11, f32[1024,128]{1,0:T(8,128)S(1)} %copy-done.13, bf16[1024,384]{1,0:T(8,128)(2,1)S(1)} %add_convert_fusion.1.g_ref, f32[1024,128]{1,0:T(8,128)S(1)} %copy-done.5, f32[1024,128]{1,0:T(8,128)S(1)} %copy-done.3), custom_call_target="tpu_custom_call" | custom-call | tf_op jit(solution)/shard_map/attend_back/pallas_call | solution.py:852
  357.3 4.8 convolution_convert_fusion.1
  365.0 23.0 %scatter_one.1 = (f32[2,128,1536]{2,1,0:T(8,128)S(1)}, f32[2,128,128]{2,1,0:T(8,128)S(1)}) custom-call(bf16[2,2,2,128,1536]{4,3,2,1,0:T(8,128)(2,1)S(1)} %bitcast.197, bf16[2,2,2,128,128]{4,3,2,1,0:T(8,128)(2,1)S(1)} %bitcast.204), custom_call_target="tpu_custom_call" | custom-call | tf_op jit(solution)/shard_map/scatter_one/pallas_call | solution.py:501
  394.0 36.7 %give_back.1 = (bf16[2,128,1536]{2,1,0:T(8,128)(2,1)}, bf16[2,128,1536]{2,1,0:T(8,128)(2,1)}, bf16[2,2,2,128,128]{4,3,2,1,0:T(8,128)(2,1)}) custom-call(bf16[2,128,1536]{2,1,0:T(8,128)(2,1)} %bitcast.218, bf16[2,128,1536]{2,1,0:T(8,128)(2,1)} %bitcast.216, bf16[2,128,128]{2,1,0:T(8,128)(2,1)} %bitcast.237), custom_call_target="tpu_custom_call" | custom-call | tf_op jit(solution)/shard_map/give_back/pallas_call | solution.py:501
  437.6 204.9 %gather_all.1 = bf16[8,4,16,6912]{3,2,1,0:T(8,128)(2,1)} custom-call(bf16[16,6912]{1,0:T(8,128)(2,1)} %concatenate.48.src), custom_call_target="tpu_custom_call" | custom-call | tf_op jit(solution)/shard_map/gather_all/pallas_call | solution.py:501
  643.2 7.2 convolution_bitcast_fusion
  650.4 5.0 copy-done.15
  676.1 5.1 fusion.97
  706.4 4.6 copy.85
  (316 shorter events, 158.6 us)
Async XLA Ops:
  0.6 212.9 %copy-start = (bf16[1024,1536]{1,0:T(8,128)(2,1)S(1)}, bf16[1024,1536]{1,0:T(8,128)(2,1)}, u32[]{:S(2)}) copy-start(bf16[1024,1536]{1,0:T(8,128)(2,1)} %param.34) | copy-start | bytes 9437188
  0.7 81.6 %copy-start.65 = (f32[1536]{0:T(1024)S(1)}, f32[1536]{0:T(1024)}, u32[]{:S(2)}) copy-start(f32[1536]{0:T(1024)} %param.26) | copy-start | bytes 18436
  5.6 77.5 %copy-start.45 = (bf16[1536,16]{0,1:T(8,128)(2,1)}, bf16[1536,16]{0,1:T(8,128)(2,1)S(1)}, u32[]{:S(2)}) copy-start(bf16[1536,16]{0,1:T(8,128)(2,1)S(1)} %get-tuple-element.99) | copy-start | bytes 147460
  5.6 77.5 %copy-start.47 = (bf16[1536,16]{0,1:T(8,128)(2,1)}, bf16[1536,16]{0,1:T(8,128)(2,1)S(1)}, u32[]{:S(2)}) copy-start(bf16[1536,16]{0,1:T(8,128)(2,1)S(1)} %get-tuple-element.100) | copy-start | bytes 147460
  86.9 10.8 %copy-start.56 = (bf16[16,512]{1,0:T(8,128)(2,1)}, bf16[16,512]{1,0:T(8,128)(2,1)S(1)}, u32[]{:S(2)}) copy-start(bf16[16,512]{1,0:T(8,128)(2,1)S(1)} %reshape.346) | copy-start | bytes 49156
  103.7 13.9 %copy-start.2 = (f32[1024,128]{1,0:T(8,128)}, f32[1024,128]{1,0:T(8,128)S(1)}, u32[]{:S(2)}) copy-start(f32[1024,128]{1,0:T(8,128)S(1)} %get-tuple-element.103.sin_ref) | copy-start | bytes 1572868
  103.7 13.9 %copy-start.4 = (f32[1024,128]{1,0:T(8,128)}, f32[1024,128]{1,0:T(8,128)S(1)}, u32[]{:S(2)}) copy-start(f32[1024,128]{1,0:T(8,128)S(1)} %get-tuple-element.104.cos_ref) | copy-start | bytes 1572868
  103.7 10.4 %copy-start.84 = (bf16[384,1536]{1,0:T(8,128)(2,1)S(1)}, bf16[384,1536]{1,0:T(8,128)(2,1)}, u32[]{:S(2)}) copy-start(bf16[384,1536]{1,0:T(8,128)(2,1)} %param.31) | copy-start | bytes 3538948
  122.1 38.9 %copy-start.19 = (bf16[2,128,1536]{2,1,0:T(8,128)(2,1)S(1)}, bf16[2,128,1536]{2,1,0:T(8,128)(2,1)}, u32[]{:S(2)}) copy-start(bf16[2,128,1536]{2,1,0:T(8,128)(2,1)} %get-tuple-element.32) | copy-start | bytes 2359300
  122.1 39.1 %copy-start.80 = (pred[128]{0:T(512)(128)(4,1)S(1)}, pred[128]{0:T(512)(128)(4,1)}, u32[]{:S(2)}) copy-start(pred[128]{0:T(512)(128)(4,1)} %constant.229.clone.1) | copy-start | bytes 388
  163.7 38.3 %copy-start.74 = (f32[256]{0:T(256)}, f32[256]{0:T(256)S(1)}, u32[]{:S(2)}) copy-start(f32[256]{0:T(256)S(1)} %get-tuple-element.118) | copy-start | bytes 3076
  272.3 23.0 %copy-start.73 = (bf16[256,16]{0,1:T(8,128)(2,1)S(1)}, bf16[256,16]{0,1:T(8,128)(2,1)}, u32[]{:S(2)}) copy-start(bf16[256,16]{0,1:T(8,128)(2,1)} %copy.89) | copy-start | bytes 24580
  299.8 32.1 %copy-start.51 = (bf16[2,2,2,128,128]{4,3,2,1,0:T(8,128)(2,1)S(1)}, bf16[2,2,2,128,128]{4,3,2,1,0:T(8,128)(2,1)}, u32[]{:S(2)}) copy-start(bf16[2,2,2,128,128]{4,3,2,1,0:T(8,128)(2,1)} %get-tuple-element.53) | copy-start | bytes 786436
  342.8 14.4 %copy-start.36 = (bf16[1536,4,2,64]{0,3,2,1:T(8,128)(2,1)S(1)}, bf16[1536,4,2,64]{0,3,2,1:T(8,128)(2,1)}, u32[]{:S(2)}) copy-start(bf16[1536,4,2,64]{0,3,2,1:T(8,128)(2,1)} %copy-done.35) | copy-start | bytes 4718596
  342.8 14.4 %copy-start.39 = (bf16[1536,2,128]{0,2,1:T(8,128)(2,1)S(1)}, bf16[1536,2,128]{0,2,1:T(8,128)(2,1)}, u32[]{:S(2)}) copy-start(bf16[1536,2,128]{0,2,1:T(8,128)(2,1)} %copy-done.38) | copy-start | bytes 2359300
  342.8 14.4 %copy-start.41 = (bf16[1536,2,2,64]{0,3,2,1:T(8,128)(2,1)S(1)}, bf16[1536,2,2,64]{0,3,2,1:T(8,128)(2,1)}, u32[]{:S(2)}) copy-start(bf16[1536,2,2,64]{0,3,2,1:T(8,128)(2,1)} %copy-done.40) | copy-start | bytes 2359300
  362.1 26.0 %copy-start.79 = (pred[128]{0:T(512)(128)(4,1)S(1)}, pred[128]{0:T(512)(128)(4,1)}, u32[]{:S(2)}) copy-start(pred[128]{0:T(512)(128)(4,1)} %constant.236.clone.1) | copy-start | bytes 388
  362.1 26.6 %copy-start.46 = (bf16[1536,16]{0,1:T(8,128)(2,1)S(1)}, bf16[1536,16]{0,1:T(8,128)(2,1)}, u32[]{:S(2)}) copy-start(bf16[1536,16]{0,1:T(8,128)(2,1)} %copy-done.45) | copy-start | bytes 147460
  362.1 26.6 %copy-start.48 = (bf16[1536,16]{0,1:T(8,128)(2,1)S(1)}, bf16[1536,16]{0,1:T(8,128)(2,1)}, u32[]{:S(2)}) copy-start(bf16[1536,16]{0,1:T(8,128)(2,1)} %copy-done.47) | copy-start | bytes 147460
  362.1 26.6 %copy-start.66 = (f32[1536]{0:T(1024)S(1)}, f32[1536]{0:T(1024)}, u32[]{:S(2)}) copy-start(f32[1536]{0:T(1024)} %param.26) | copy-start | bytes 18436
  365.0 25.4 %copy-start.20 = (bf16[2,128,1536]{2,1,0:T(8,128)(2,1)S(1)}, bf16[2,128,1536]{2,1,0:T(8,128)(2,1)}, u32[]{:S(2)}) copy-start(bf16[2,128,1536]{2,1,0:T(8,128)(2,1)} %get-tuple-element.32) | copy-start | bytes 2359300
  394.0 40.8 %copy-start.53 = (bf16[1024,16]{0,1:T(8,128)(2,1)S(1)}, bf16[1024,16]{0,1:T(8,128)(2,1)}, u32[]{:S(2)}) copy-start(bf16[1024,16]{0,1:T(8,128)(2,1)} %copy-done.52) | copy-start | bytes 98308
  437.6 204.9 %copy-start.81 = (s32[8]{0:T(128)S(1)}, s32[8]{0:T(128)}, u32[]{:S(2)}) copy-start(s32[8]{0:T(128)} %constant.268) | copy-start | bytes 100
  437.6 204.9 %copy-start.14 = (s32[8]{0:T(128)S(1)}, s32[8]{0:T(128)}, u32[]{:S(2)}) copy-start(s32[8]{0:T(128)} %param.25) | copy-start | bytes 100
  (63 other events, 279.1 us)

commit v2 on v1

--- a/solution.py
+++ b/solution.py
@@ -511,141 +511,289 @@
     )(*ins)
 
 
-def _gather_body(ins, outs, own_sem, send_sem, recv_sem, place):
+def _gather_steps(ins, outs, own_sem, send_sem, recv_sem, place):
     c, f, x, core, core_peer, x_peer = place
     h = 1 - core
     count = len(ins)
     local = []
     sends = []
-    for i in range(count):
-        for j in range(2):
-            k = i * 2 + j
+
+    def first():
+        for base, target in ((0, x_peer), (2 * count, core_peer)):
+            for i in range(count):
+                for j in range(2):
+                    k = base + i * 2 + j
+                    cp = _remote(
+                        ins[i].at[j], outs[i].at[h, j, x], send_sem.at[k], recv_sem.at[k], target
+                    )
+                    cp.start()
+                    sends.append(cp)
+        for i in range(count):
+            for j in range(2):
+                lc = pltpu.make_async_copy(
+                    ins[i].at[j], outs[i].at[h, j, x], own_sem.at[i * 2 + j]
+                )
+                lc.start()
+                local.append(lc)
+
+    def last():
+        forwards = []
+        for i in range(count):
+            for j in range(2):
+                k = i * 2 + j
+                sends[k].wait_recv()
+                cp = _remote(
+                    outs[i].at[h, j, 1 - x],
+                    outs[i].at[h, j, 1 - x],
+                    send_sem.at[4 * count + k],
+                    recv_sem.at[4 * count + k],
+                    core_peer,
+                )
+                cp.start()
+                forwards.append(cp)
+        for k in range(2 * count):
+            sends[2 * count + k].wait_recv()
+            forwards[k].wait_recv()
+        for cp in sends + forwards:
+            cp.wait_send()
+        for lc in local:
+            lc.wait()
+
+    return first, last
+
+
+def _gather_body(*args):
+    first, last = _gather_steps(*args)
+    first()
+    last()
+
+
+def _ctx_body(piece, out, own_sem, send_sem, recv_sem, place):
+    c, f, x, core, core_peer, x_peer = place
+    z, y = c // 2, c % 2
+    lc = pltpu.make_async_copy(piece, out.at[c, x, core], own_sem)
+    lc.start()
+    cross = _remote(piece, out.at[c, x, core], send_sem.at[0], recv_sem.at[0], x_peer)
+    cross.start()
+
+    def start():
+        lc.wait()
+        cross.wait_recv()
+        sends = []
+        for step in range(1, 4):
             cp = _remote(
-                ins[i].at[j], outs[i].at[h, j, x], send_sem.at[k], recv_sem.at[k], x_peer
+                out.at[c, :, core],
+                out.at[c, :, core],
+                send_sem.at[step],
+                recv_sem.at[step],
+                (2 * ((z + step) % 4) + y, f),
             )
             cp.start()
             sends.append(cp)
-    for i in range(count):
-        for j in range(2):
-            k = i * 2 + j
+        cp = _remote(
+            out.at[c, :, core],
+            out.at[c, :, core],
+            send_sem.at[4],
+            recv_sem.at[4],
+            (2 * z + 1 - y, f),
+        )
+        cp.start()
+        ys = [cp]
+        return sends, ys
+
+    def forward(state):
+        sends, ys = state
+        for step in range(1, 4):
+            sends[step - 1].wait_recv()
+            origin = 2 * ((z + 4 - step) % 4) + y
             cp = _remote(
-                ins[i].at[j],
-                outs[i].at[h, j, x],
-                send_sem.at[2 * count + k],
-                recv_sem.at[2 * count + k],
+                out.at[origin, :, core],
+                out.at[origin, :, core],
+                send_sem.at[4 + step],
+                recv_sem.at[4 + step],
+                (2 * z + 1 - y, f),
+            )
+            cp.start()
+            ys.append(cp)
+        return sends, ys
+
+    def finish(state):
+        sends, ys = state
+        last = []
+
+        def share(k, origin):
+            cp = _remote(
+                out.at[origin, :, core],
+                out.at[origin, :, core],
+                send_sem.at[8 + k],
+                recv_sem.at[8 + k],
                 core_peer,
             )
             cp.start()
-            sends.append(cp)
-            lc = pltpu.make_async_copy(ins[i].at[j], outs[i].at[h, j, x], own_sem.at[k])
-            lc.start()
-            local.append(lc)
-    forwards = []
-    for i in range(count):
-        for j in range(2):
-            k = i * 2 + j
-            sends[k].wait_recv()
-            cp = _remote(
-                outs[i].at[h, j, 1 - x],
-                outs[i].at[h, j, 1 - x],
-                send_sem.at[4 * count + k],
-                recv_sem.at[4 * count + k],
-                core_peer,
-            )
-            cp.start()
-            forwards.append(cp)
-    for k in range(2 * count):
-        sends[2 * count + k].wait_recv()
-        forwards[k].wait_recv()
-    for cp in sends + forwards:
-        cp.wait_send()
-    for lc in local:
-        lc.wait()
-
-
-def group_gather(arrays, cid, name):
-    count = len(arrays)
-
-    def kernel(*refs):
-        ins, outs = refs[:count], refs[count : 2 * count]
-        own_sem, send_sem, recv_sem = refs[2 * count :]
+            last.append(cp)
+
+        share(0, c)
+        for step in range(1, 4):
+            share(step, 2 * ((z + 4 - step) % 4) + y)
+        for step in range(4):
+            ys[step].wait_recv()
+            share(4 + step, 2 * ((z + 4 - step) % 4) + 1 - y)
+        for cp in last:
+            cp.wait_recv()
+        for cp in [cross] + sends + ys + last:
+            cp.wait_send()
+
+    return start, forward, finish
+
+
+def _ctx_peers(place):
+    c, f, x, core, core_peer, x_peer = place
+    z, y = c // 2, c % 2
+    return [(2 * ((z + step) % 4) + y, f) for step in range(1, 4)] + [(2 * z + 1 - y, f)]
+
+
+def _ctx_out(piece):
+    return jax.ShapeDtypeStruct((8, 2, 2) + piece.shape, piece.dtype)
+
+
+CTX_SEMS = [pltpu.SemaphoreType.DMA(()), _sem(16), _sem(16)]
+
+
+def group_gather(array, piece, cid, name):
+    def kernel(own, piece_in, whole, spread, own_sem, send_sem, recv_sem, *ctx_sems):
+        place = _place()
+        _greet([place[4], place[5]] + _ctx_peers(place))
+        start, forward, finish = _ctx_body(piece_in, spread, *ctx_sems, place)
+        first, last = _gather_steps([own], [whole], own_sem, send_sem, recv_sem, place)
+        first()
+        state = forward(start())
+        last()
+        finish(state)
+
+    outs = [jax.ShapeDtypeStruct((2, 2, 2) + array.shape[1:], array.dtype), _ctx_out(piece)]
+    return _comm_call(
+        kernel, [array, piece], outs, [_sem(2), _sem(6), _sem(6)] + CTX_SEMS, cid, name
+    )
+
+
+def plain_gather(array, cid, name):
+    def kernel(own, whole, own_sem, send_sem, recv_sem):
         place = _place()
         _greet([place[4], place[5]])
-        _gather_body(ins, outs, own_sem, send_sem, recv_sem, place)
-
-    outs = [jax.ShapeDtypeStruct((2, 2, 2) + a.shape[1:], a.dtype) for a in arrays]
-    return _comm_call(
-        kernel, arrays, outs, [_sem(2 * count), _sem(6 * count), _sem(6 * count)], cid, name
-    )
-
-
-def group_scatter(arrays, cid, name):
-    count = len(arrays)
+        _gather_body([own], [whole], own_sem, send_sem, recv_sem, place)
+
+    outs = [jax.ShapeDtypeStruct((2, 2, 2) + array.shape[1:], array.dtype)]
+    return _comm_call(kernel, [array], outs, [_sem(2), _sem(6), _sem(6)], cid, name)[0]
+
+
+def group_scatter(main, side, cid, name, piece=None):
+    spread = piece is not None
 
     def kernel(*refs):
-        ins, outs = refs[:count], refs[count : 2 * count]
-        first, staged, second = (
-            refs[2 * count : 3 * count],
-            refs[3 * count : 4 * count],
-            refs[4 * count : 5 * count],
+        main_in, side_in = refs[:2]
+        refs = refs[2:]
+        if spread:
+            piece_in, refs = refs[0], refs[1:]
+        sums, side_all = refs[:2]
+        refs = refs[2:]
+        if spread:
+            spread_out, refs = refs[0], refs[1:]
+        first, staged, second, side_first, side_staged, side_second, side_own = refs[:7]
+        send_sem, recv_sem, gsend_sem, grecv_sem, gown_sem = refs[7:12]
+        place = _place()
+        c, f, x, core, core_peer, x_peer = place
+        h = 1 - core
+        _greet([core_peer, x_peer] + (_ctx_peers(place) if spread else []))
+        if spread:
+            start, forward, finish = _ctx_body(piece_in, spread_out, *refs[12:], place)
+        group = (
+            (side_in, side_first, side_staged, side_second),
+            (main_in, first, staged, second),
         )
-        send_sem, recv_sem = refs[5 * count :]
-        c, f, x, core, core_peer, x_peer = _place()
-        h = 1 - core
-        _greet([core_peer, x_peer])
         one, two = {}, {}
-        for far in (1, 0):
-            for j in range(2):
-                for i in range(count):
+        for i, (src, land, _, _) in enumerate(group):
+            for far in (1, 0):
+                for j in range(2):
                     k = (i * 2 + j) * 2 + far
-                    xx = 1 - x if far else x
                     cp = _remote(
-                        ins[i].at[1 - h, j, xx],
-                        first[i].at[far, j],
+                        src.at[1 - h, j, 1 - x if far else x],
+                        land.at[far, j],
                         send_sem.at[k],
                         recv_sem.at[k],
                         core_peer,
                     )
                     cp.start()
                     one[(i, j, far)] = cp
-        for j in range(2):
-            for i in range(count):
+        for i, (src, land, stage, land_two) in enumerate(group):
+            for j in range(2):
                 one[(i, j, 1)].wait_recv()
-                staged[i][j] = (
-                    ins[i][h, j, 1 - x].astype(F32) + first[i][1, j].astype(F32)
-                ).astype(BF16)
-                k = 4 * count + i * 2 + j
-                cp = _remote(
-                    staged[i].at[j], second[i].at[j], send_sem.at[k], recv_sem.at[k], x_peer
-                )
+                stage[j] = (src[h, j, 1 - x].astype(F32) + land[1, j].astype(F32)).astype(BF16)
+                k = 8 + i * 2 + j
+                cp = _remote(stage.at[j], land_two.at[j], send_sem.at[k], recv_sem.at[k], x_peer)
                 cp.start()
                 two[(i, j)] = cp
+        if spread:
+            state = start()
         for j in range(2):
-            for i in range(count):
-                one[(i, j, 0)].wait_recv()
-                outs[i][j] = ins[i][h, j, x].astype(F32) + first[i][0, j].astype(F32)
+            one[(0, j, 0)].wait_recv()
+            two[(0, j)].wait_recv()
+            side_own[j] = (
+                side_in[h, j, x].astype(F32)
+                + side_first[0, j].astype(F32)
+                + side_second[j].astype(F32)
+            ).astype(BF16)
+        gfirst, glast = _gather_steps([side_own], [side_all], gown_sem, gsend_sem, grecv_sem, place)
+        gfirst()
         for j in range(2):
-            for i in range(count):
-                two[(i, j)].wait_recv()
-                outs[i][j] = outs[i][j] + second[i][j].astype(F32)
+            one[(1, j, 0)].wait_recv()
+            sums[j] = main_in[h, j, x].astype(F32) + first[0, j].astype(F32)
+        if spread:
+            state = forward(state)
+        glast()
+        for j in range(2):
+            two[(1, j)].wait_recv()
+            sums[j] = sums[j] + second[j].astype(F32)
+        if spread:
+            finish(state)
         for cp in list(one.values()) + list(two.values()):
             cp.wait_send()
 
-    outs = [jax.ShapeDtypeStruct((2,) + a.shape[3:], F32) for a in arrays]
-    rows = [a.shape[3:] for a in arrays]
-    scratch = (
-        [pltpu.VMEM((2, 2) + r, BF16) for r in rows]
-        + [pltpu.VMEM((2,) + r, BF16) for r in rows]
-        + [pltpu.VMEM((2,) + r, BF16) for r in rows]
-        + [_sem(6 * count), _sem(6 * count)]
-    )
-    return _comm_call(
-        kernel, arrays, outs, scratch, cid, name, pltpu.VMEM, pltpu.VMEM, 40 * 1024 * 1024
-    )
+    vmem, hbm = pl.BlockSpec(memory_space=pltpu.VMEM), pl.BlockSpec(memory_space=pl.ANY)
+    outs = [
+        jax.ShapeDtypeStruct((2,) + main.shape[3:], F32),
+        jax.ShapeDtypeStruct(side.shape, BF16),
+    ]
+    scratch = []
+    for rows in (main.shape[3:], side.shape[3:]):
+        scratch += [
+            pltpu.VMEM((2, 2) + rows, BF16),
+            pltpu.VMEM((2,) + rows, BF16),
+            pltpu.VMEM((2,) + rows, BF16),
+        ]
+    scratch += [pltpu.VMEM((2,) + side.shape[3:], BF16)]
+    scratch += [_sem(12), _sem(12), _sem(6), _sem(6), _sem(2)]
+    ins, in_specs, out_specs = [main, side], [vmem, vmem], [vmem, vmem]
+    if spread:
+        ins += [piece]
+        in_specs += [hbm]
+        out_specs += [hbm]
+        outs += [_ctx_out(piece)]
+        scratch += CTX_SEMS
+    return pl.pallas_call(
+        kernel,
+        out_shape=outs,
+        in_specs=in_specs,
+        out_specs=out_specs,
+        scratch_shapes=scratch,
+        compiler_params=pltpu.CompilerParams(
+            collective_id=cid, has_side_effects=True, vmem_limit_bytes=40 * 1024 * 1024
+        ),
+        name=name,
+    )(*ins)
 
 
 def take_in(tokens, cotangent, cid):
-    def kernel(tok, cot, tok_own, cot_own, tok_all, cot_all, land_s, land_r, own_sem, send_sem, recv_sem):
+    def kernel(tok, cot, tok_own, cot_own, tok_all, land_s, land_r, own_sem, send_sem, recv_sem):
         place = _place()
         c, f, x, core, core_peer, x_peer = place
         h = 1 - core
@@ -666,15 +814,19 @@
                 s = 2 * f + half
                 to_c = (s % 4) * 2 + s // 4
                 cp = _remote(
-                    src.at[half], dst.at[to_j], land_s.at[2 * a + half], land_r.at[2 * a + to_j], (to_c, to_f)
+                    src.at[half],
+                    dst.at[to_j],
+                    land_s.at[2 * a + half],
+                    land_r.at[2 * a + to_j],
+                    (to_c, to_f),
                 )
                 cp.start()
                 moves.append(cp)
-        for a in range(2):
-            for j in range(2):
-                dst = (tok_own, cot_own)[a]
-                pltpu.make_async_copy(dst.at[j], dst.at[j], land_r.at[2 * a + j]).wait()
-        _gather_body((tok_own, cot_own), (tok_all, cot_all), own_sem, send_sem, recv_sem, place)
+        for j in range(2):
+            pltpu.make_async_copy(tok_own.at[j], tok_own.at[j], land_r.at[j]).wait()
+        _gather_body([tok_own], [tok_all], own_sem, send_sem, recv_sem, place)
+        for j in range(2):
+            pltpu.make_async_copy(cot_own.at[j], cot_own.at[j], land_r.at[2 + j]).wait()
         for cp in moves:
             cp.wait_send()
 
@@ -683,76 +835,88 @@
     return _comm_call(
         kernel,
         [tokens, cotangent],
-        [own, own, whole, whole],
-        [_sem(4), _sem(4), _sem(4), _sem(12), _sem(12)],
+        [own, own, whole],
+        [_sem(4), _sem(4), _sem(2), _sem(6), _sem(6)],
         cid,
         "take_in",
     )
 
 
-def give_back(arrays, smalls, cid):
-    count, extra = len(arrays), len(smalls)
-
-    def kernel(*refs):
-        ins, small_in = refs[:count], refs[count : count + extra]
-        outs = refs[count + extra : 2 * count + extra]
-        small_out = refs[2 * count + extra : 2 * count + 2 * extra]
-        out_s, out_r, own_sem, send_sem, recv_sem = refs[2 * count + 2 * extra :]
-        place = _place()
-        c, f, x, core, core_peer, x_peer = place
-        h = 1 - core
-        slot = c // 2 + 4 * (c % 2)
-        barrier = pltpu.get_barrier_semaphore()
-        from_f = 2 * (c % 2) + 1 - c // 4
+def _back_steps(src, dst, out_s, out_r, place):
+    c, f, x, core, core_peer, x_peer = place
+    h = 1 - core
+    slot = c // 2 + 4 * (c % 2)
+    place_in = slot % 2
+    moves = []
+
+    def first():
+        for j in range(2):
+            cp = _remote(
+                src.at[j],
+                dst.at[place_in],
+                out_s.at[j],
+                out_r.at[place_in],
+                (x + 2 * j + 4 * h, slot // 2),
+            )
+            cp.start()
+            moves.append(cp)
+
+    def last():
         for half in range(2):
-            s = 2 * f + half
-            pl.semaphore_signal(
-                barrier, inc=1, device_id=((s % 4) * 2 + s // 4, from_f), device_id_type=MESH_ID
-            )
-        for target in (core_peer, x_peer):
-            pl.semaphore_signal(barrier, inc=1, device_id=target, device_id_type=MESH_ID)
-        pl.semaphore_wait(barrier, 4)
-        moves = []
-        place_in = slot % 2
-        for i in range(count):
-            for j in range(2):
-                cp = _remote(
-                    ins[i].at[j],
-                    outs[i].at[place_in],
-                    out_s.at[2 * i + j],
-                    out_r.at[2 * i + place_in],
-                    (x + 2 * j + 4 * h, slot // 2),
-                )
-                cp.start()
-                moves.append(cp)
-        _gather_body(small_in, small_out, own_sem, send_sem, recv_sem, place)
-        for i in range(count):
-            for half in range(2):
-                pltpu.make_async_copy(
-                    outs[i].at[half], outs[i].at[half], out_r.at[2 * i + half]
-                ).wait()
+            pltpu.make_async_copy(dst.at[half], dst.at[half], out_r.at[half]).wait()
         for cp in moves:
             cp.wait_send()
 
-    outs = [jax.ShapeDtypeStruct(a.shape, a.dtype) for a in arrays]
-    outs += [jax.ShapeDtypeStruct((2, 2, 2) + a.shape[1:], a.dtype) for a in smalls]
+    return first, last
+
+
+def _back_sources(place):
+    c, f = place[:2]
+    from_f = 2 * (c % 2) + 1 - c // 4
+    return [(((2 * f + half) % 4) * 2 + (2 * f + half) // 4, from_f) for half in range(2)]
+
+
+def give_back(array, piece, cid):
+    def kernel(own, piece_in, out, spread, out_s, out_r, *ctx_sems):
+        place = _place()
+        _greet(_back_sources(place) + [place[4], place[5]] + _ctx_peers(place))
+        start, forward, finish = _ctx_body(piece_in, spread, *ctx_sems, place)
+        first, last = _back_steps(own, out, out_s, out_r, place)
+        state = start()
+        first()
+        finish(forward(state))
+        last()
+
+    outs = [jax.ShapeDtypeStruct(array.shape, array.dtype), _ctx_out(piece)]
     return _comm_call(
-        kernel,
-        list(arrays) + list(smalls),
-        outs,
-        [_sem(2 * count), _sem(2 * count), _sem(2 * extra), _sem(6 * extra), _sem(6 * extra)],
-        cid,
-        "give_back",
-    )
-
-
-def attend_call(proj, cosine, sine, length):
+        kernel, [array, piece], outs, [_sem(2), _sem(2)] + CTX_SEMS, cid, "give_back"
+    )
+
+
+def attend_call(proj, cosine, sine, length, behind, cid):
     rows = proj.shape[0]
     step = 256
     scale = HEAD_DIM ** (-0.5)
     lane = PAD_HEAD
 
-    def kernel(len_ref, proj_ref, cos_ref, sin_ref, att_ref, qkv_ref, lse_ref):
+    def kernel(
+        len_ref,
+        proj_ref,
+        cos_ref,
+        sin_ref,
+        behind_ref,
+        att_ref,
+        qkv_ref,
+        lse_ref,
+        whole_ref,
+        own_sem,
+        send_sem,
+        recv_sem,
+    ):
+        place = _place()
+        _greet([place[4], place[5]])
+        first, last = _gather_steps([behind_ref], [whole_ref], own_sem, send_sem, recv_sem, place)
+        first()
         live = len_ref[0]
         for part in range(6):
             cols = slice(part * lane, (part + 1) * lane)
@@ -784,29 +948,53 @@
                 stats = jnp.where(lanes == head, top + jnp.log(total), stats)
             att_ref[row, :] = jnp.concatenate(pieces, axis=1).astype(BF16)
             lse_ref[row, :] = stats
-
-    vmem = pl.BlockSpec(memory_space=pltpu.VMEM)
+        last()
+
+    vmem, hbm = pl.BlockSpec(memory_space=pltpu.VMEM), pl.BlockSpec(memory_space=pl.ANY)
     return pl.pallas_call(
         kernel,
         out_shape=(
             jax.ShapeDtypeStruct((rows, 4 * HEAD_DIM), BF16),
             jax.ShapeDtypeStruct(proj.shape, BF16),
             jax.ShapeDtypeStruct((rows, lane), F32),
+            jax.ShapeDtypeStruct((2, 2, 2) + behind.shape[1:], behind.dtype),
         ),
-        in_specs=[pl.BlockSpec(memory_space=pltpu.SMEM), vmem, vmem, vmem],
-        out_specs=(vmem, vmem, vmem),
-        compiler_params=pltpu.CompilerParams(vmem_limit_bytes=48 * 1024 * 1024),
+        in_specs=[pl.BlockSpec(memory_space=pltpu.SMEM), vmem, vmem, vmem, hbm],
+        out_specs=(vmem, vmem, vmem, hbm),
+        scratch_shapes=[_sem(2), _sem(6), _sem(6)],
+        compiler_params=pltpu.CompilerParams(
+            collective_id=cid, has_side_effects=True, vmem_limit_bytes=40 * 1024 * 1024
+        ),
         name="attend",
-    )(length, proj, cosine, sine)
-
-
-def attend_back_call(qkv, stats, grad_att, cosine, sine, length):
+    )(length, proj, cosine, sine, behind)
+
+
+def attend_back_call(qkv, stats, grad_att, cosine, sine, length, behind, cid):
     rows = qkv.shape[0]
     step = 256
     scale = HEAD_DIM ** (-0.5)
     lane = PAD_HEAD
 
-    def kernel(len_ref, qkv_ref, lse_ref, g_ref, cos_ref, sin_ref, out_ref, dk_ref, dv_ref, do_ref):
+    def kernel(
+        len_ref,
+        qkv_ref,
+        lse_ref,
+        g_ref,
+        cos_ref,
+        sin_ref,
+        behind_ref,
+        out_ref,
+        back_ref,
+        dk_ref,
+        dv_ref,
+        do_ref,
+        out_s,
+        out_r,
+    ):
+        place = _place()
+        _greet(_back_sources(place))
+        first, last = _back_steps(behind_ref, back_ref, out_s, out_r, place)
+        first()
         live = len_ref[0]
         pad = jnp.zeros((rows, lane - HEAD_DIM), BF16)
         for head in range(4):
@@ -847,68 +1035,99 @@
             dk = dk * cos_ref[...] - pltpu.roll(dk, HALF_PAD, 1) * sin_ref[...]
             out_ref[:, (4 + kv) * lane : (5 + kv) * lane] = dk.astype(BF16)
             out_ref[:, (6 + kv) * lane : (7 + kv) * lane] = dv_ref[kv].astype(BF16)
-
-    vmem = pl.BlockSpec(memory_space=pltpu.VMEM)
+        last()
+
+    vmem, hbm = pl.BlockSpec(memory_space=pltpu.VMEM), pl.BlockSpec(memory_space=pl.ANY)
     return pl.pallas_call(
         kernel,
-        out_shape=jax.ShapeDtypeStruct(qkv.shape, BF16),
-        in_specs=[pl.BlockSpec(memory_space=pltpu.SMEM)] + [vmem] * 5,
-        out_specs=vmem,
+        out_shape=[
+            jax.ShapeDtypeStruct(qkv.shape, BF16),
+            jax.ShapeDtypeStruct(behind.shape, behind.dtype),
+        ],
+        in_specs=[pl.BlockSpec(memory_space=pltpu.SMEM)] + [vmem] * 5 + [hbm],
+        out_specs=[vmem, hbm],
         scratch_shapes=[
             pltpu.VMEM((2, rows, lane), F32),
             pltpu.VMEM((2, rows, lane), F32),
             pltpu.VMEM((4, rows, lane), BF16),
+            _sem(2),
+            _sem(2),
         ],
-        compiler_params=pltpu.CompilerParams(vmem_limit_bytes=48 * 1024 * 1024),
+        compiler_params=pltpu.CompilerParams(
+            collective_id=cid, has_side_effects=True, vmem_limit_bytes=40 * 1024 * 1024
+        ),
         name="attend_back",
-    )(length, qkv, stats, grad_att, cosine, sine)
-
-
-def gather_all(piece, cid):
-    def kernel(src, out, own_sem, send_sem, recv_sem):
-        c = lax.axis_index("ctx")
-        f = lax.axis_index("fsdp")
-        me = c * 4 + f
-        barrier = pltpu.get_barrier_semaphore()
-
-        def greet(step, carry):
-            to = lax.rem(me + step, 32)
-            pl.semaphore_signal(barrier, inc=1, device_id=(to // 4, to % 4), device_id_type=MESH_ID)
-            return carry
-
-        lax.fori_loop(1, 32, greet, 0)
-        pl.semaphore_wait(barrier, 31)
-        lc = pltpu.make_async_copy(src, out.at[c, f], own_sem)
-        lc.start()
-
-        def copy(step):
-            to = lax.rem(me + step, 32)
-            return _remote(
-                src, out.at[c, f], send_sem.at[step], recv_sem.at[step], (to // 4, to % 4)
-            )
-
-        def send(step, carry):
-            copy(step).start()
-            return carry
-
-        lax.fori_loop(1, 32, send, 0)
-
-        def done(step, carry):
-            copy(step).wait_recv()
-            copy(step).wait_send()
-            return carry
-
-        lax.fori_loop(1, 32, done, 0)
-        lc.wait()
-
-    return _comm_call(
+    )(length, qkv, stats, grad_att, cosine, sine, behind)
+
+
+def table_call(early, middle, late, adapters):
+    f32 = lambda *shape: jax.ShapeDtypeStruct(shape, F32)
+    choices = 8
+    outs = [
+        f32(choices, 5, RANK, 1536),
+        f32(choices, RANK, 1536),
+        f32(choices, RANK, 4096),
+        f32(choices, RANK, 1536),
+        f32(choices, 2, RANK, 768),
+        f32(choices, RANK, 1536),
+        f32(choices, 2, RANK, 4096),
+        f32(choices, RANK, 1536),
+    ]
+    plan = (
+        ((6, 0, 1024), (6, 1, 1024), (2, None, 1024), (0, 3, 384), (0, 4, 384), (7, None, 384)),
+        ((1, None, 384), (5, None, 384), (3, None, 384), (4, 0, 192), (4, 1, 192)),
+        ((0, 0, 384), (0, 1, 384), (0, 2, 384)),
+    )
+
+    def kernel(which, early_ref, middle_ref, late_ref, *refs):
+        outs, acc, sems = refs[:8], refs[8:16], refs[16]
+
+        def add(piece, ref):
+            def one_slot(origin, carry):
+                row = which[origin]
+                for f in range(4):
+                    at = 0
+                    for out, table, n in plan[piece]:
+                        value = ref[origin, f, :, at : at + n].astype(F32)
+                        cols = slice(f * n, (f + 1) * n)
+                        if table is None:
+                            acc[out][row, :, cols] += value
+                        else:
+                            acc[out][row, table, :, cols] += value
+                        at += n
+                return carry
+
+            lax.fori_loop(0, 8, one_slot, 0)
+
+        def send(out):
+            cp = pltpu.make_async_copy(acc[out], outs[out], sems.at[out])
+            cp.start()
+            return cp
+
+        for out in (2, 6, 7):
+            acc[out][...] = jnp.zeros_like(acc[out])
+        acc[0][...] = jnp.zeros_like(acc[0])
+        add(0, early_ref)
+        copies = [send(out) for out in (2, 6, 7)]
+        for out in (1, 3, 4, 5):
+            acc[out][...] = jnp.zeros_like(acc[out])
+        add(1, middle_ref)
+        copies += [send(out) for out in (1, 3, 4, 5)]
+        add(2, late_ref)
+        copies += [send(0)]
+        for cp in copies:
+            cp.wait()
+
+    vmem, hbm = pl.BlockSpec(memory_space=pltpu.VMEM), pl.BlockSpec(memory_space=pl.ANY)
+    return pl.pallas_call(
         kernel,
-        [piece],
-        jax.ShapeDtypeStruct((8, 4) + piece.shape, piece.dtype),
-        [pltpu.SemaphoreType.DMA(()), _sem(32), _sem(32)],
-        cid,
-        "gather_all",
-    )
+        out_shape=outs,
+        in_specs=[pl.BlockSpec(memory_space=pltpu.SMEM), vmem, vmem, vmem],
+        out_specs=[hbm] * 8,
+        scratch_shapes=[pltpu.VMEM(o.shape, F32) for o in outs] + [_sem(8)],
+        compiler_params=pltpu.CompilerParams(vmem_limit_bytes=40 * 1024 * 1024),
+        name="tables",
+    )(adapters, early, middle, late)
 
 
 def dot(left, right):
@@ -1034,38 +1253,39 @@
     cosine = jnp.concatenate([cos, gap, cos, gap], axis=1)
     sine = jnp.concatenate([-sin, gap, sin, gap], axis=1)
 
-    tok_own, cot_own, tok_all, cot_all = take_in(tokens, cotangent, 0)
+    tok_own, cot_own, tok_all = take_in(tokens, cotangent, 0)
     live_rows = (jnp.arange(rows, dtype=jnp.int32) < length[0])[:, None]
     block_of = x + 4 * (1 - core) + 2 * jnp.arange(2, dtype=jnp.int32)
     own_pos = (block_of[:, None] * 128 + jnp.arange(128, dtype=jnp.int32)[None, :]).reshape(-1)
     own_live = (own_pos < length[0])[:, None]
-    grad_out = jnp.where(live_rows, flat(cot_all), jnp.zeros((), BF16))
-    grad_out_own = jnp.where(own_live, flat(cot_own), jnp.zeros((), BF16))
+
+    def own_rows(whole):
+        part = lax.dynamic_slice(
+            whole, (1 - core, 0, x, 0, 0), (1, 2, 1, whole.shape[3], whole.shape[4])
+        )
+        return part.reshape(-1, whole.shape[4])
 
     tokens_f = flat(tok_all).astype(F32)
     normed_one = (tokens_f * rms_factor(tokens_f) * attention_norm_gain).astype(BF16)
     inner_qkv = dot(normed_one, first_all).astype(BF16)
     proj = dot(normed_one, weight_all) + ADAPTER_SCALE * dot(inner_qkv, second_all)
-    attn_b, qkv, stats = attend_call(proj, cosine, sine, length)
-
-    sums, side = group_scatter(
-        [
-            blocks(dot(attn_b, output_weight).astype(BF16)),
-            blocks(side_pad(dot(attn_b, first_o_own)).astype(BF16)),
-        ],
+    attn_b, qkv, stats, cot_all = attend_call(proj, cosine, sine, length, cot_own, 9)
+    grad_out = jnp.where(live_rows, flat(cot_all), jnp.zeros((), BF16))
+    grad_out_own = jnp.where(own_live, flat(cot_own), jnp.zeros((), BF16))
+
+    sums, side_all = group_scatter(
+        blocks(dot(attn_b, output_weight).astype(BF16)),
+        blocks(side_pad(dot(attn_b, first_o_own)).astype(BF16)),
         1,
         "scatter_o",
     )
-    inner_o_own = flat(side)[:, :RANK].astype(BF16)
+    inner_o = flat(side_all)[:, :RANK]
+    inner_o_own = own_rows(side_all)[:, :RANK]
     own_f = flat(tok_own).astype(F32)
     resid = own_f + flat(sums) + ADAPTER_SCALE * dot(inner_o_own, second_o)
     factor_two = rms_factor(resid)
     normed_two_own = (resid * factor_two * feedforward_norm_gain).astype(BF16)
-    normed_two, side_all = group_gather(
-        [own_blocks(normed_two_own), own_blocks(side_pad(inner_o_own))], 2, "gather_two"
-    )
-    normed_two = flat(normed_two)
-    inner_o = flat(side_all)[:, :RANK]
+    normed_two = flat(plain_gather(own_blocks(normed_two_own), 2, "gather_two"))
 
     inner_gu = dot(normed_two, first_gu).astype(BF16)
     gate = dot(normed_two, gate_weight) + ADAPTER_SCALE * dot(inner_gu[:, :RANK], second_gu[0])
@@ -1082,10 +1302,11 @@
     side_gu = ADAPTER_SCALE * jnp.concatenate(
         [dot_t(grad_gate, second_gu[0]), dot_t(grad_up, second_gu[1])], axis=1
     )
-    sums, side = group_scatter(
-        [blocks(grad_two), blocks(side_pad(side_gu).astype(BF16))], 3, "scatter_two"
-    )
-    grad_inner_gu_own = flat(side)[:, : 2 * RANK].astype(BF16)
+    sums, side_all = group_scatter(
+        blocks(grad_two), blocks(side_pad(side_gu).astype(BF16)), 3, "scatter_two"
+    )
+    grad_inner_gu = flat(side_all)[:, : 2 * RANK]
+    grad_inner_gu_own = own_rows(side_all)[:, : 2 * RANK]
     grad_normed_two = (
         (flat(sums) + dot_t(grad_inner_gu_own, first_gu)).astype(BF16).astype(F32)
     )
@@ -1094,106 +1315,82 @@
     )
     grad_low_own = grad_resid.astype(BF16)
 
-    out_sums, out_side = group_scatter(
-        [
-            blocks(dot(hidden, down_weight).astype(BF16)),
-            blocks(side_pad(dot(hidden, first_d_own)).astype(BF16)),
-        ],
+    sums, side_all = group_scatter(
+        blocks(dot(hidden, down_weight).astype(BF16)),
+        blocks(side_pad(dot(hidden, first_d_own)).astype(BF16)),
         4,
         "scatter_out",
     )
-    inner_d_own = flat(out_side)[:, :RANK].astype(BF16)
+    inner_d = flat(side_all)[:, :RANK]
+    inner_d_own = own_rows(side_all)[:, :RANK]
     out_own = jnp.where(
-        own_live, resid + flat(out_sums) + ADAPTER_SCALE * dot(inner_d_own, second_d), 0.0
+        own_live, resid + flat(sums) + ADAPTER_SCALE * dot(inner_d_own, second_d), 0.0
     ).astype(BF16)
 
-    grad_low, side_all = group_gather(
+    def pack(parts):
+        return jnp.concatenate(parts, axis=1).astype(BF16)
+
+    two_cut = cut(normed_two, 1, quarter)
+    in_gu = dot_rows(grad_inner_gu, two_cut)
+    early = pack(
         [
-            own_blocks(grad_low_own),
-            own_blocks(side_pad(jnp.concatenate([grad_inner_gu_own, inner_d_own], axis=1))),
-        ],
-        5,
-        "gather_resid",
-    )
+            ADAPTER_SCALE * dot_rows(inner_gu[:, :RANK], grad_gate),
+            ADAPTER_SCALE * dot_rows(inner_gu[:, RANK:], grad_up),
+            dot_rows(grad_inner_d, hidden),
+            in_gu[:RANK],
+            in_gu[RANK:],
+            ADAPTER_SCALE * dot_rows(inner_d, cut(grad_out, 1, quarter)),
+        ]
+    )
+    grad_low, early = group_gather(own_blocks(grad_low_own), early, 5, "gather_resid")
     grad_low = flat(grad_low)
-    side_all = flat(side_all)
-    grad_inner_gu = side_all[:, : 2 * RANK]
-    inner_d = side_all[:, 2 * RANK : 3 * RANK]
     grad_inner_o = (ADAPTER_SCALE * dot_t(grad_low, second_o)).astype(BF16)
     grad_att = (dot_t(grad_low, output_weight) + dot_t(grad_inner_o, first_o_own)).astype(BF16)
-    grad_qkv = attend_back_call(qkv, stats, grad_att, cosine, sine, length)
+    grad_qkv, out_tokens = attend_back_call(
+        qkv, stats, grad_att, cosine, sine, length, own_blocks(out_own), 10
+    )
     grad_one = dot_t(grad_qkv, weight_all).astype(BF16)
     side_qkv = ADAPTER_SCALE * dot_t(grad_qkv, second_all)
-    sums, side = group_scatter(
-        [blocks(grad_one), blocks(side_pad(side_qkv).astype(BF16))], 6, "scatter_one"
-    )
-    grad_inner_own = flat(side)[:, : 3 * RANK].astype(BF16)
+    all_b = ADAPTER_SCALE * dot_rows(inner_qkv, grad_qkv)
+    middle = pack(
+        [
+            dot_rows(grad_inner_o, attn_b),
+            ADAPTER_SCALE * dot_rows(inner_o, cut(grad_low, 1, quarter)),
+            unpad_turned(all_b[:RANK, : 4 * PAD_HEAD]),
+            unpad_turned(all_b[RANK : 2 * RANK, 4 * PAD_HEAD : 6 * PAD_HEAD]),
+            unpad_plain(all_b[2 * RANK :, 6 * PAD_HEAD :]),
+        ]
+    )
+    sums, side_all, middle = group_scatter(
+        blocks(grad_one), blocks(side_pad(side_qkv).astype(BF16)), 6, "scatter_one", middle
+    )
+    grad_inner_qkv = flat(side_all)[:, : 3 * RANK]
+    grad_inner_own = own_rows(side_all)[:, : 3 * RANK]
     grad_normed_one = (flat(sums) + dot_t(grad_inner_own, first_all)).astype(BF16).astype(F32)
     grad_tok_own = grad_resid + norm_back(
         own_f, rms_factor(own_f), attention_norm_gain, grad_normed_one
     )
-    out_tokens, grad_tokens, side_all = give_back(
-        [own_blocks(out_own), own_blocks(grad_tok_own.astype(BF16))],
-        [own_blocks(side_pad(grad_inner_own))],
-        7,
-    )
-    grad_inner_qkv = flat(side_all)[:, : 3 * RANK]
-
     one_cut = cut(normed_one, 1, quarter)
-    two_cut = cut(normed_two, 1, quarter)
     in_qkv = dot_rows(grad_inner_qkv, one_cut)
-    in_gu = dot_rows(grad_inner_gu, two_cut)
-    o_a = dot_rows(grad_inner_o, attn_b)
-    d_a = dot_rows(grad_inner_d, hidden)
-    all_b = ADAPTER_SCALE * dot_rows(inner_qkv, grad_qkv)
-    q_b = unpad_turned(all_b[:RANK, : 4 * PAD_HEAD])
-    k_b = unpad_turned(all_b[RANK : 2 * RANK, 4 * PAD_HEAD : 6 * PAD_HEAD])
-    v_b = unpad_plain(all_b[2 * RANK :, 6 * PAD_HEAD :])
-    o_b = ADAPTER_SCALE * dot_rows(inner_o, cut(grad_low, 1, quarter))
-    g_b = ADAPTER_SCALE * dot_rows(inner_gu[:, :RANK], grad_gate)
-    u_b = ADAPTER_SCALE * dot_rows(inner_gu[:, RANK:], grad_up)
-    d_b = ADAPTER_SCALE * dot_rows(inner_d, cut(grad_out, 1, quarter))
-    parts = [
-        in_qkv[:RANK],
-        in_qkv[RANK : 2 * RANK],
-        in_qkv[2 * RANK :],
-        in_gu[:RANK],
-        in_gu[RANK:],
-        o_a,
-        d_a,
-        q_b,
-        k_b,
-        v_b,
-        o_b,
-        g_b,
-        u_b,
-        d_b,
-    ]
-    gathered = gather_all(jnp.concatenate(parts, axis=1).astype(BF16), 8)
+    late = pack([in_qkv[:RANK], in_qkv[RANK : 2 * RANK], in_qkv[2 * RANK :]])
+    grad_tokens, late = give_back(own_blocks(grad_tok_own.astype(BF16)), late, 7)
+
     group_slot = [cc // 2 + 4 * (cc % 2) for cc in range(8)]
     group_adapter = slot_adapter_index[jnp.array(group_slot, dtype=jnp.int32)]
-    onehot = (
-        group_adapter[:, None] == jnp.arange(adapter_input_first.shape[0], dtype=jnp.int32)[None, :]
-    ).astype(BF16)
-    tables = jnp.einsum("sa,sfrn->arfn", onehot, gathered, preferred_element_type=F32)
-    full = []
-    start = 0
-    for part in parts:
-        n = part.shape[1]
-        full.append(tables[..., start : start + n].reshape(tables.shape[0], RANK, 4 * n))
-        start += n
-    turn = lambda t: jnp.swapaxes(t, 1, 2)
+    as_devices = lambda piece: piece.reshape((8, 4) + piece.shape[3:])
+    full = table_call(as_devices(early), as_devices(middle), as_devices(late), group_adapter)
+    turn = lambda t: jnp.swapaxes(t, -1, -2)
     return (
         out_tokens,
         grad_tokens.astype(F32),
-        jnp.stack([turn(t) for t in full[:5]], axis=1),
-        turn(full[5]),
-        turn(full[6]),
+        turn(full[0]),
+        turn(full[1]),
+        turn(full[2]),
+        full[3],
+        full[4],
+        full[5],
+        full[6],
         full[7],
-        jnp.stack([full[8], full[9]], axis=1),
-        full[10],
-        jnp.stack([full[11], full[12]], axis=1),
-        full[13],
     )
 
 

time: 736 us -> 487 us (0.66)
  the two profiles are of different devices: /device:TPU:15 before, /device:TPU:3 now
where the time goes in v2:
time: 487 us; the launch traced here: 478 us
  Pallas kernels  323 us (66%)
  matrix products  93 us (19%)
  local copies, waits for them, and re-layouts  35.3 us (7%)
  other arithmetic  22.2 us (5%)
    pallas_call x4, Pallas kernels, _comm_call(): pl.pallas_call(kernel, out_shape=outs, in_specs=[pl.BlockSpec(memory_spac...  158 us
    pallas_call x4, Pallas kernels, group_scatter(): pl.pallas_call(kernel, out_shape=outs, in_specs=in_specs, out_specs=out_s...  115 us
    dot_general x14, matrix products, dot(): return jnp.dot(left, right, preferred_element_type=F32)  49.2 us
    dot_general x14, matrix products, dot_t(): lax.dot_general(left, right, (((1,), (1,)), ((), ())), preferred_element_...  34.5 us
    pallas_call x1, Pallas kernels, attend_call(): pl.pallas_call(kernel, out_shape=(jax.ShapeDtypeStruct((rows, 4 * HEAD_DI...  23.7 us
    unnamed x183, local copies, waits for them, and re-layouts  20.5 us
    pallas_call x1, Pallas kernels, attend_back_call(): pl.pallas_call(kernel, out_shape=[jax.ShapeDtypeStruct(qkv.shape, BF16),...  19.2 us

profile of v2, /device:TPU:3, one launch (start us, length us, event | category | flops | bytes accessed | tf_op | source)
XLA Modules:
  0.0 478.3 jit_solution(10191570176315964609)
XLA Ops:
  2.1 55.6 %take_in.1 = (bf16[2,128,1536]{2,1,0:T(8,128)(2,1)}, bf16[2,128,1536]{2,1,0:T(8,128)(2,1)}, bf16[2,2,2,128,1536]{4,3,2,1,0:T(8,128)(2,1)}) custom-call(bf16[2,128,1536]{2,1,0:T(8,128)(2,1)} %tok.1, bf16[2,128,1536]{2,1,0:T(8,128)(2,1)} %cot.1), custom_call_target="tpu_custom_call" | custom-call | tf_op jit(solution)/shard_map/take_in/pallas_call | solution.py:501
  68.7 8.3 %fusion.18 = f32[1024,1024]{1,0:T(8,128)} fusion(bf16[1024,1536]{1,0:T(8,128)(2,1)} %fusion.1, bf16[1536,256]{0,1:T(8,128)(2,1)} %bitcast.200, bf16[1536,256]{0,1:T(8,128)(2,1)} %bitcast.202, bf16[1536,512]{0,1:T(8,128)(2,1)S(1)} %bitcast.198), kind=kOutput, calls=%fused_computation.50 | convolution fusion | flops 3230662656 | bytes 10485760 | tf_op jit(solution)/shard_map/dot_general | solution.py:1134
  92.0 23.7 %attend.1 = (bf16[1024,384]{1,0:T(8,128)(2,1)S(1)}, bf16[1024,1024]{1,0:T(8,128)(2,1)S(1)}, f32[1024,128]{1,0:T(8,128)S(1)}, bf16[2,2,2,128,1536]{4,3,2,1,0:T(8,128)(2,1)S(1)}) custom-call(s32[1]{0:T(128)} %dynamic_slice.69.len_ref, f32[1024,1024]{1,0:T(8,128)S(1)} %multiply_add_fusion.2.proj_ref, f32[1024,128]{1,0:T(8,128)S(1)} %get-tuple-element.83.cos_ref, ...), custom_call_target="tpu_custom_call" | custom-call | tf_op jit(solution)/shard_map/attend/pallas_call | solution.py:954
  115.7 3.7 convolution_convert_fusion
  122.7 25.1 %scatter_o.1 = (f32[2,128,1536]{2,1,0:T(8,128)S(1)}, bf16[2,2,2,128,128]{4,3,2,1,0:T(8,128)(2,1)S(1)}) custom-call(bf16[2,2,2,128,1536]{4,3,2,1,0:T(8,128)(2,1)S(1)} %bitcast.171, bf16[2,2,2,128,128]{4,3,2,1,0:T(8,128)(2,1)S(1)} %bitcast.179), custom_call_target="tpu_custom_call" | custom-call | tf_op jit(solution)/shard_map/scatter_o/pallas_call | solution.py:782
  153.2 26.4 %gather_two.1 = bf16[2,2,2,128,1536]{4,3,2,1,0:T(8,128)(2,1)} custom-call(bf16[2,128,1536]{2,1,0:T(8,128)(2,1)} %bitcast.197), custom_call_target="tpu_custom_call" | custom-call | tf_op jit(solution)/shard_map/gather_two/pallas_call | solution.py:501
  179.7 8.4 %fusion.101 = f32[1024,1024]{1,0:T(8,128)} fusion(bf16[1024,1536]{1,0:T(8,128)(2,1)} %bitcast.186, bf16[1536,1024]{1,0:T(8,128)(2,1)} %param.32), kind=kOutput, calls=%fused_computation.190 | convolution fusion | flops 3221225472 | bytes 10485760 | tf_op jit(solution)/shard_map/dot_general | solution.py:1134
  189.1 3.1 multiply_add_fusion
  193.5 3.4 fusion.99
  203.1 3.4 fusion.100
  206.5 5.0 %multiply_convert_fusion = (bf16[1024,1024]{1,0:T(8,128)(2,1)S(1)}, bf16[1024,1024]{1,0:T(8,128)(2,1)}, bf16[1024,1024]{1,0:T(8,128)(2,1)}) fusion(f32[1024,1024]{1,0:T(8,128)S(1)} %multiply_add_fusion, f32[1024,1024]{1,0:T(8,128)S(1)} %convolution_add_fusion.2, f32[1024,1024]{1,0:T(8,128)S(1)} %fusion.100, bf16[8,2,16,4096]{3,2,1,0:T(8,128)(2,1)} %param.41, ...), kind=kOutput, calls=%fused_computation.6 | convolution fusion | flops 52428800 | bytes 18939916 | tf_op jit(solution)/shard_map/dot_general | solution.py:1134
  211.5 4.9 %convolution_convert_fusion.2 = bf16[1024,1536]{1,0:T(8,128)(2,1)} fusion(bf16[1024,1024]{1,0:T(8,128)(2,1)S(1)} %get-tuple-element.72, bf16[1024,1536]{1,0:T(8,128)(2,1)S(1)} %copy-done), kind=kOutput, calls=%fused_computation.15 | convolution fusion | flops 3222798336 | bytes 8388608 | tf_op jit(solution)/shard_map/dot_general | solution.py:1134
  220.0 25.3 %scatter_out.1 = (f32[2,128,1536]{2,1,0:T(8,128)S(1)}, bf16[2,2,2,128,128]{4,3,2,1,0:T(8,128)(2,1)S(1)}) custom-call(bf16[2,2,2,128,1536]{4,3,2,1,0:T(8,128)(2,1)S(1)} %bitcast.172, bf16[2,2,2,128,128]{4,3,2,1,0:T(8,128)(2,1)S(1)} %bitcast.180), custom_call_target="tpu_custom_call" | custom-call | tf_op jit(solution)/shard_map/scatter_out/pallas_call | solution.py:782
  245.3 5.6 %fusion.102 = f32[1024,1536]{1,0:T(8,128)S(1)} fusion(bf16[1024,1024]{1,0:T(8,128)(2,1)} %get-tuple-element.73, bf16[1536,1024]{1,0:T(8,128)(2,1)S(1)} %copy-done.83), kind=kOutput, calls=%fused_computation.191 | convolution fusion | flops 3221225472 | bytes 11534336 | tf_op jit(solution)/shard_map/dot_general | solution.py:1138
  251.0 3.8 add_convert_fusion
  261.1 25.1 %scatter_two.1 = (f32[2,128,1536]{2,1,0:T(8,128)S(1)}, bf16[2,2,2,128,128]{4,3,2,1,0:T(8,128)(2,1)S(1)}) custom-call(bf16[2,2,2,128,1536]{4,3,2,1,0:T(8,128)(2,1)S(1)} %bitcast.170, bf16[2,2,2,128,128]{4,3,2,1,0:T(8,128)(2,1)S(1)} %bitcast.181), custom_call_target="tpu_custom_call" | custom-call | tf_op jit(solution)/shard_map/scatter_two/pallas_call | solution.py:782
  289.9 3.4 fusion.96
  298.7 43.5 %gather_resid.1 = (bf16[2,2,2,128,1536]{4,3,2,1,0:T(8,128)(2,1)}, bf16[8,2,2,16,4224]{4,3,2,1,0:T(8,128)(2,1)}) custom-call(bf16[2,128,1536]{2,1,0:T(8,128)(2,1)} %bitcast.195, bf16[16,4224]{1,0:T(8,128)(2,1)} %copy-done.68), custom_call_target="tpu_custom_call" | custom-call | tf_op jit(solution)/shard_map/gather_resid/pallas_call | solution.py:501
  342.3 4.2 fusion.103
  350.9 19.2 %attend_back.1 = (bf16[1024,1024]{1,0:T(8,128)(2,1)S(1)}, bf16[2,128,1536]{2,1,0:T(8,128)(2,1)S(1)}) custom-call(s32[1]{0:T(128)} %dynamic_slice.69.len_ref, bf16[1024,1024]{1,0:T(8,128)(2,1)S(1)} %copy-done.17, f32[1024,128]{1,0:T(8,128)S(1)} %copy-done.27, bf16[1024,384]{1,0:T(8,128)(2,1)S(1)} %add_convert_fusion.1.g_ref, f32[1024,128]{1,0:T(8,128)S(1)} %copy-done.7, ...), custom_call_target="tpu_custom_call" | custom-call | tf_op jit(solution)/shard_map/attend_back/pallas_call | solution.py:1041
  370.2 4.8 convolution_convert_fusion.1
  384.0 39.3 %scatter_one.1 = (f32[2,128,1536]{2,1,0:T(8,128)S(1)}, bf16[2,2,2,128,128]{4,3,2,1,0:T(8,128)(2,1)S(1)}, bf16[8,2,2,16,1536]{4,3,2,1,0:T(8,128)(2,1)S(1)}) custom-call(bf16[2,2,2,128,1536]{4,3,2,1,0:T(8,128)(2,1)S(1)} %bitcast.169, bf16[2,2,2,128,128]{4,3,2,1,0:T(8,128)(2,1)S(1)} %bitcast.178, bf16[16,1536]{1,0:T(8,128)(2,1)S(1)} %concatenate.53.refs_2_), custom_call_target="tpu_custom_call" | custom-call | tf_op jit(solution)/shard_map/scatter_one/pallas_call | solution.py:782
  428.7 32.9 %give_back.1 = (bf16[2,128,1536]{2,1,0:T(8,128)(2,1)}, bf16[8,2,2,16,1152]{4,3,2,1,0:T(8,128)(2,1)}) custom-call(bf16[2,128,1536]{2,1,0:T(8,128)(2,1)} %bitcast.196, bf16[16,1152]{1,0:T(8,128)(2,1)} %pad_maximum_fusion.13.piece_in), custom_call_target="tpu_custom_call" | custom-call | tf_op jit(solution)/shard_map/give_back/pallas_call | solution.py:501
  469.7 7.2 %tables.1 = (f32[8,5,16,1536]{3,2,1,0:T(8,128)}, f32[8,16,1536]{2,1,0:T(8,128)}, f32[8,16,4096]{2,1,0:T(8,128)}, f32[8,16,1536]{2,1,0:T(8,128)}, f32[8,2,16,768]...) custom-call(s32[8]{0:T(128)S(1)} %gather_fusion, ...), custom_call_target="tpu_custom_call" | custom-call | tf_op jit(solution)/shard_map/tables/pallas_call | solution.py:1122
  (271 shorter events, 88.4 us)
Async XLA Ops:
  0.6 192.8 %copy-start = (bf16[1024,1536]{1,0:T(8,128)(2,1)S(1)}, bf16[1024,1536]{1,0:T(8,128)(2,1)}, u32[]{:S(2)}) copy-start(bf16[1024,1536]{1,0:T(8,128)(2,1)} %param.34) | copy-start | bytes 9437188
  0.7 59.8 %copy-start.73 = (f32[1536]{0:T(1024)S(1)}, f32[1536]{0:T(1024)}, u32[]{:S(2)}) copy-start(f32[1536]{0:T(1024)} %param.26) | copy-start | bytes 18436
  68.7 8.4 %copy-start.50 = (bf16[1536,4,2,64]{0,3,2,1:T(8,128)(2,1)}, bf16[1536,4,2,64]{0,3,2,1:T(8,128)(2,1)S(1)}, u32[]{:S(2)}) copy-start(bf16[1536,4,2,64]{0,3,2,1:T(8,128)(2,1)S(1)} %pad.44) | copy-start | bytes 4718596
  91.9 27.5 %copy-start.4 = (f32[1024,128]{1,0:T(8,128)}, f32[1024,128]{1,0:T(8,128)S(1)}, u32[]{:S(2)}) copy-start(f32[1024,128]{1,0:T(8,128)S(1)} %get-tuple-element.82.sin_ref) | copy-start | bytes 1572868
  92.0 27.5 %copy-start.6 = (f32[1024,128]{1,0:T(8,128)}, f32[1024,128]{1,0:T(8,128)S(1)}, u32[]{:S(2)}) copy-start(f32[1024,128]{1,0:T(8,128)S(1)} %get-tuple-element.83.cos_ref) | copy-start | bytes 1572868
  92.0 23.8 %copy-start.86 = (bf16[384,1536]{1,0:T(8,128)(2,1)S(1)}, bf16[384,1536]{1,0:T(8,128)(2,1)}, u32[]{:S(2)}) copy-start(bf16[384,1536]{1,0:T(8,128)(2,1)} %param.31) | copy-start | bytes 3538948
  122.7 25.1 %copy-start.37 = (bf16[2,128,1536]{2,1,0:T(8,128)(2,1)S(1)}, bf16[2,128,1536]{2,1,0:T(8,128)(2,1)}, u32[]{:S(2)}) copy-start(bf16[2,128,1536]{2,1,0:T(8,128)(2,1)} %get-tuple-element.44) | copy-start | bytes 2359300
  147.8 40.3 %copy-start.28 = (bf16[2,2,2,128,128]{4,3,2,1,0:T(8,128)(2,1)}, bf16[2,2,2,128,128]{4,3,2,1,0:T(8,128)(2,1)S(1)}, u32[]{:S(2)}) copy-start(bf16[2,2,2,128,128]{4,3,2,1,0:T(8,128)(2,1)S(1)} %get-tuple-element.47) | copy-start | bytes 786436
  179.6 8.4 %copy-start.35 = (bf16[2,2,2,128,1536]{4,3,2,1,0:T(8,128)(2,1)S(1)}, bf16[2,2,2,128,1536]{4,3,2,1,0:T(8,128)(2,1)}, u32[]{:S(2)}) copy-start(bf16[2,2,2,128,1536]{4,3,2,1,0:T(8,128)(2,1)} %gather_two.1) | copy-start | bytes 9437188
  179.7 8.4 %copy-start.63 = (bf16[1536,16]{0,1:T(8,128)(2,1)S(1)}, bf16[1536,16]{0,1:T(8,128)(2,1)}, u32[]{:S(2)}) copy-start(bf16[1536,16]{0,1:T(8,128)(2,1)} %get-tuple-element.79) | copy-start | bytes 147460
  220.0 25.3 %copy-start.83 = (bf16[1536,1024]{1,0:T(8,128)(2,1)S(1)}, bf16[1536,1024]{1,0:T(8,128)(2,1)}, u32[]{:S(2)}) copy-start(bf16[1536,1024]{1,0:T(8,128)(2,1)} %param.32) | copy-start | bytes 9437188
  260.0 27.0 %copy-start.22 = (f32[2,128,1536]{2,1,0:T(8,128)S(1)}, f32[2,128,1536]{2,1,0:T(8,128)}, u32[]{:S(2)}) copy-start(f32[2,128,1536]{2,1,0:T(8,128)} %copy-done.21) | copy-start | bytes 4718596
  260.0 27.0 %copy-start.33 = (f32[256,1536]{1,0:T(8,128)S(1)}, f32[256,1536]{1,0:T(8,128)}, u32[]{:S(2)}) copy-start(f32[256,1536]{1,0:T(8,128)} %copy-done.32) | copy-start | bytes 4718596
  260.0 27.0 %copy-start.64 = (bf16[1536,16]{0,1:T(8,128)(2,1)S(1)}, bf16[1536,16]{0,1:T(8,128)(2,1)}, u32[]{:S(2)}) copy-start(bf16[1536,16]{0,1:T(8,128)(2,1)} %get-tuple-element.79) | copy-start | bytes 147460
  350.8 19.3 %copy-start.51 = (bf16[1536,4,2,64]{0,3,2,1:T(8,128)(2,1)S(1)}, bf16[1536,4,2,64]{0,3,2,1:T(8,128)(2,1)}, u32[]{:S(2)}) copy-start(bf16[1536,4,2,64]{0,3,2,1:T(8,128)(2,1)} %copy-done.50) | copy-start | bytes 4718596
  350.8 19.3 %copy-start.53 = (bf16[1536,2,128]{0,2,1:T(8,128)(2,1)S(1)}, bf16[1536,2,128]{0,2,1:T(8,128)(2,1)}, u32[]{:S(2)}) copy-start(bf16[1536,2,128]{0,2,1:T(8,128)(2,1)} %pad.46) | copy-start | bytes 2359300
  350.8 19.3 %copy-start.54 = (bf16[1536,2,2,64]{0,3,2,1:T(8,128)(2,1)S(1)}, bf16[1536,2,2,64]{0,3,2,1:T(8,128)(2,1)}, u32[]{:S(2)}) copy-start(bf16[1536,2,2,64]{0,3,2,1:T(8,128)(2,1)} %pad.45) | copy-start | bytes 2359300
  378.0 45.4 %copy-start.58 = (bf16[1536,16]{0,1:T(8,128)(2,1)S(1)}, bf16[1536,16]{0,1:T(8,128)(2,1)}, u32[]{:S(2)}) copy-start(bf16[1536,16]{0,1:T(8,128)(2,1)} %copy-done.57) | copy-start | bytes 147460
  378.0 45.4 %copy-start.74 = (f32[1536]{0:T(1024)S(1)}, f32[1536]{0:T(1024)}, u32[]{:S(2)}) copy-start(f32[1536]{0:T(1024)} %param.26) | copy-start | bytes 18436
  384.0 39.4 %copy-start.38 = (bf16[2,128,1536]{2,1,0:T(8,128)(2,1)S(1)}, bf16[2,128,1536]{2,1,0:T(8,128)(2,1)}, u32[]{:S(2)}) copy-start(bf16[2,128,1536]{2,1,0:T(8,128)(2,1)} %get-tuple-element.44) | copy-start | bytes 2359300
  384.0 39.4 %copy-start.60 = (bf16[1536,16]{0,1:T(8,128)(2,1)S(1)}, bf16[1536,16]{0,1:T(8,128)(2,1)}, u32[]{:S(2)}) copy-start(bf16[1536,16]{0,1:T(8,128)(2,1)} %copy-done.59) | copy-start | bytes 147460
  384.0 39.4 %copy-start.62 = (bf16[1536,16]{0,1:T(8,128)(2,1)S(1)}, bf16[1536,16]{0,1:T(8,128)(2,1)}, u32[]{:S(2)}) copy-start(bf16[1536,16]{0,1:T(8,128)(2,1)} %copy-done.61) | copy-start | bytes 147460
  426.6 37.4 %copy-start.82 = (s32[8]{0:T(128)S(1)}, s32[8]{0:T(128)}, u32[]{:S(2)}) copy-start(s32[8]{0:T(128)} %constant.264) | copy-start | bytes 100
  464.7 13.2 %copy-start.1 = (bf16[1024,1536]{1,0:T(8,128)(2,1)S(1)}, bf16[1024,1536]{1,0:T(8,128)(2,1)}, u32[]{:S(2)}) copy-start(bf16[1024,1536]{1,0:T(8,128)(2,1)} %param.34) | copy-start | bytes 9437188
  (63 other events, 227.1 us)

commit v3 on v2

--- a/solution.py
+++ b/solution.py
@@ -568,144 +568,354 @@
     last()
 
 
-def _ctx_body(piece, out, own_sem, send_sem, recv_sem, place):
+def _ctx_first(piece, lines, own_sem, send_sem, recv_sem, place):
     c, f, x, core, core_peer, x_peer = place
     z, y = c // 2, c % 2
-    lc = pltpu.make_async_copy(piece, out.at[c, x, core], own_sem)
-    lc.start()
-    cross = _remote(piece, out.at[c, x, core], send_sem.at[0], recv_sem.at[0], x_peer)
-    cross.start()
+    sends = []
+    local = []
 
     def start():
-        lc.wait()
-        cross.wait_recv()
-        sends = []
+        lc = pltpu.make_async_copy(piece, lines.at[z, x], own_sem)
+        lc.start()
+        local.append(lc)
+        cp = _remote(piece, lines.at[z, x], send_sem.at[0], recv_sem.at[0], x_peer)
+        cp.start()
+        sends.append(cp)
+
+    def spread():
+        local[0].wait()
+        sends[0].wait_recv()
         for step in range(1, 4):
             cp = _remote(
-                out.at[c, :, core],
-                out.at[c, :, core],
+                lines.at[z],
+                lines.at[z],
                 send_sem.at[step],
                 recv_sem.at[step],
                 (2 * ((z + step) % 4) + y, f),
             )
             cp.start()
             sends.append(cp)
+
+    def finish():
+        for cp in sends[1:]:
+            cp.wait_recv()
+        for cp in sends:
+            cp.wait_send()
+
+    return start, spread, finish
+
+
+def _ctx_second(lines, out, own_sem, send_sem, recv_sem, place):
+    c, f, x, core, core_peer, x_peer = place
+    z, y = c // 2, c % 2
+    y_peer = (2 * z + 1 - y, f)
+    sends = []
+    local = []
+
+    def start():
+        lc = pltpu.make_async_copy(lines, out.at[y, core], own_sem)
+        lc.start()
+        local.append(lc)
+        for k, target in ((0, y_peer), (1, core_peer)):
+            cp = _remote(lines, out.at[y, core], send_sem.at[k], recv_sem.at[k], target)
+            cp.start()
+            sends.append(cp)
+
+    def share():
+        sends[0].wait_recv()
         cp = _remote(
-            out.at[c, :, core],
-            out.at[c, :, core],
-            send_sem.at[4],
-            recv_sem.at[4],
-            (2 * z + 1 - y, f),
+            out.at[1 - y, core], out.at[1 - y, core], send_sem.at[2], recv_sem.at[2], core_peer
         )
         cp.start()
-        ys = [cp]
-        return sends, ys
-
-    def forward(state):
-        sends, ys = state
-        for step in range(1, 4):
-            sends[step - 1].wait_recv()
-            origin = 2 * ((z + 4 - step) % 4) + y
+        sends.append(cp)
+
+    def finish():
+        sends[1].wait_recv()
+        sends[2].wait_recv()
+        for cp in sends:
+            cp.wait_send()
+        local[0].wait()
+
+    return start, share, finish
+
+
+def _z_peers(place):
+    c, f = place[:2]
+    return [(2 * ((c // 2 + step) % 4) + c % 2, f) for step in range(1, 4)]
+
+
+def _y_peer(place):
+    c, f = place[:2]
+    return (2 * (c // 2) + 1 - c % 2, f)
+
+
+def _lines_of(n):
+    return (4, 2, RANK, n)
+
+
+def _spread_of(n):
+    return jax.ShapeDtypeStruct((2, 2, 4, 2, RANK, n), BF16)
+
+
+FIRST_SEMS = [pltpu.SemaphoreType.DMA(()), _sem(4), _sem(4)]
+SECOND_SEMS = [pltpu.SemaphoreType.DMA(()), _sem(3), _sem(3)]
+
+
+def _order_steps(own, order, own_sem, send_sem, recv_sem, place):
+    core_peer, x_peer = place[4:]
+    sends, local, forwards = [], [], []
+
+    def first():
+        for j in range(2):
+            cp = _remote(own.at[j], order.at[1 + j, 1], send_sem.at[j], recv_sem.at[j], x_peer)
+            cp.start()
+            sends.append(cp)
+        for j in range(2):
             cp = _remote(
-                out.at[origin, :, core],
-                out.at[origin, :, core],
-                send_sem.at[4 + step],
-                recv_sem.at[4 + step],
-                (2 * z + 1 - y, f),
+                own.at[j], order.at[3, j], send_sem.at[2 + j], recv_sem.at[2 + j], core_peer
             )
             cp.start()
-            ys.append(cp)
-        return sends, ys
-
-    def finish(state):
-        sends, ys = state
-        last = []
-
-        def share(k, origin):
-            cp = _remote(
-                out.at[origin, :, core],
-                out.at[origin, :, core],
-                send_sem.at[8 + k],
-                recv_sem.at[8 + k],
-                core_peer,
-            )
+            sends.append(cp)
+        for j in range(2):
+            lc = pltpu.make_async_copy(own.at[j], order.at[0, j], own_sem.at[j])
+            lc.start()
+            local.append(lc)
+
+    def forward(j):
+        sends[j].wait_recv()
+        cp = _remote(
+            order.at[1 + j, 1],
+            order.at[1 + j, 0],
+            send_sem.at[4 + j],
+            recv_sem.at[4 + j],
+            core_peer,
+        )
+        cp.start()
+        forwards.append(cp)
+
+    def own_here():
+        for lc in local:
+            lc.wait()
+
+    def core_here():
+        for j in range(2):
+            sends[2 + j].wait_recv()
+
+    def far_here(j):
+        forwards[j].wait_recv()
+
+    def last():
+        for cp in sends + forwards:
+            cp.wait_send()
+
+    return first, forward, own_here, core_here, far_here, last
+
+
+def _order_all(own, order, sems, place):
+    first, forward, own_here, core_here, far_here, last = _order_steps(own, order, *sems, place)
+    first()
+    own_here()
+    for j in range(2):
+        forward(j)
+    core_here()
+    for j in range(2):
+        far_here(j)
+    last()
+
+
+def feed_forward(own, grad_out, gate_w, up_w, down_w, first_gu, second_g, second_u, first_d, second_d, cid):
+    width, units = gate_w.shape
+    wide = width + SIDE
+    tile = 256
+
+    def kernel(
+        own_ref,
+        go_ref,
+        gate_ref,
+        up_ref,
+        down_ref,
+        first_ref,
+        sg_ref,
+        su_ref,
+        fd_ref,
+        sd_ref,
+        sums,
+        out_own,
+        out_far,
+        order,
+        gate_b,
+        up_b,
+        down_a,
+        hid_s,
+        gg_s,
+        gu_s,
+        in_s,
+        gid_s,
+        part,
+        out_part,
+        near,
+        out_near,
+        far,
+        out_land,
+        staged,
+        landed,
+        own_sem,
+        send_sem,
+        recv_sem,
+        s_sem,
+        r_sem,
+    ):
+        place = _place()
+        core_peer, x_peer = place[4:]
+        _greet([core_peer, x_peer])
+        first, forward, own_here, core_here, far_here, last = _order_steps(
+            own_ref, order, own_sem, send_sem, recv_sem, place
+        )
+        first()
+        copies = []
+
+        def work(step):
+            rows = order[step].reshape(2 * 128, width)
+            go = go_ref[step]
+            inner = dot(rows, first_ref[...]).astype(BF16)
+            gid = dot_t(go, sd_ref[...]).astype(BF16)
+            in_s[step] = inner
+            gid_s[step] = gid
+            for at in range(0, units, tile):
+                cols = slice(at, at + tile)
+                gate = dot(rows, gate_ref[:, cols]) + dot(inner, sg_ref[:, cols])
+                up = dot(rows, up_ref[:, cols]) + dot(inner, su_ref[:, cols])
+                grad = dot_t(go, down_ref[cols, :]) + dot_t(gid, fd_ref[cols, :])
+                sig = 1.0 / (1.0 + jnp.exp(-gate))
+                silu = gate * sig
+                hid_s[step, :, cols] = (silu * up).astype(BF16)
+                gg_s[step, :, cols] = (grad * up * sig * (1.0 + gate * (1.0 - sig))).astype(BF16)
+                gu_s[step, :, cols] = (grad * silu).astype(BF16)
+            gg, gu, hid = gg_s[step], gu_s[step], hid_s[step]
+            for at in range(0, width, tile):
+                cols = slice(at, at + tile)
+                value = dot_t(gg, gate_ref[cols, :]) + dot_t(gu, up_ref[cols, :])
+                out = dot(hid, down_ref[:, cols])
+                if step == 0:
+                    sums[:, :, cols] = value.reshape(2, 128, tile)
+                    out_own[:, :, cols] = out.reshape(2, 128, tile)
+                else:
+                    part[step - 1, :, :, cols] = value.astype(BF16).reshape(2, 128, tile)
+                    out_part[step - 1, :, :, cols] = out.astype(BF16).reshape(2, 128, tile)
+            value = dot_t(gg, sg_ref[...]) + dot_t(gu, su_ref[...])
+            out = dot(hid, fd_ref[...])
+            if step == 0:
+                sums[:, :, width:] = value.reshape(2, 128, SIDE)
+                out_own[:, :, width:] = out.reshape(2, 128, SIDE)
+            else:
+                part[step - 1, :, :, width:] = value.astype(BF16).reshape(2, 128, SIDE)
+                out_part[step - 1, :, :, width:] = out.astype(BF16).reshape(2, 128, SIDE)
+
+        def send(src, dst, k, target):
+            cp = _remote(src, dst, s_sem.at[k], r_sem.at[k], target)
             cp.start()
-            last.append(cp)
-
-        share(0, c)
-        for step in range(1, 4):
-            share(step, 2 * ((z + 4 - step) % 4) + y)
-        for step in range(4):
-            ys[step].wait_recv()
-            share(4 + step, 2 * ((z + 4 - step) % 4) + 1 - y)
-        for cp in last:
+            copies.append(cp)
+            return cp
+
+        own_here()
+        work(0)
+        core_here()
+        forward(0)
+        work(3)
+        near_cp = [
+            send(part.at[2], near, 0, core_peer),
+            send(out_part.at[2], out_near, 1, core_peer),
+        ]
+        across, out_cps = [], []
+        for j in range(2):
+            if j:
+                forward(j)
+            far_here(j)
+            work(1 + j)
+            cp = send(part.at[j, 0], far.at[j], 2 + j, core_peer)
+            out_cps.append(send(out_part.at[j, 0], out_land.at[j], 4 + j, core_peer))
             cp.wait_recv()
-        for cp in [cross] + sends + ys + last:
+            staged[j] = (part[j, 1].astype(F32) + far[j].astype(F32)).astype(BF16)
+            across.append(send(staged.at[j], landed.at[j], 6 + j, x_peer))
+        for j in range(2):
+            out_cps[j].wait_recv()
+            out_far[j] = (out_part[j, 1].astype(F32) + out_land[j].astype(F32)).astype(BF16)
+        for cp in near_cp:
+            cp.wait_recv()
+        sums[...] = sums[...] + near[...].astype(F32)
+        out_own[...] = out_own[...] + out_near[...].astype(F32)
+        for at in range(0, units, 512):
+            cols = slice(at, at + 512)
+            g = jnp.zeros((SIDE, 512), F32)
+            u = jnp.zeros((SIDE, 512), F32)
+            d = jnp.zeros((SIDE, 512), F32)
+            for step in range(4):
+                g += dot_rows(in_s[step], gg_s[step, :, cols])
+                u += dot_rows(in_s[step], gu_s[step, :, cols])
+                d += dot_rows(gid_s[step], hid_s[step, :, cols])
+            gate_b[:, cols] = ADAPTER_SCALE * g[:RANK]
+            up_b[:, cols] = ADAPTER_SCALE * u[RANK : 2 * RANK]
+            down_a[:, cols] = d[3 * RANK : 4 * RANK]
+        for j in range(2):
+            across[j].wait_recv()
+            sums[j] = sums[j] + landed[j].astype(F32)
+        last()
+        for cp in copies:
             cp.wait_send()
 
-    return start, forward, finish
-
-
-def _ctx_peers(place):
-    c, f, x, core, core_peer, x_peer = place
-    z, y = c // 2, c % 2
-    return [(2 * ((z + step) % 4) + y, f) for step in range(1, 4)] + [(2 * z + 1 - y, f)]
-
-
-def _ctx_out(piece):
-    return jax.ShapeDtypeStruct((8, 2, 2) + piece.shape, piece.dtype)
-
-
-CTX_SEMS = [pltpu.SemaphoreType.DMA(()), _sem(16), _sem(16)]
-
-
-def group_gather(array, piece, cid, name):
-    def kernel(own, piece_in, whole, spread, own_sem, send_sem, recv_sem, *ctx_sems):
-        place = _place()
-        _greet([place[4], place[5]] + _ctx_peers(place))
-        start, forward, finish = _ctx_body(piece_in, spread, *ctx_sems, place)
-        first, last = _gather_steps([own], [whole], own_sem, send_sem, recv_sem, place)
-        first()
-        state = forward(start())
-        last()
-        finish(state)
-
-    outs = [jax.ShapeDtypeStruct((2, 2, 2) + array.shape[1:], array.dtype), _ctx_out(piece)]
-    return _comm_call(
-        kernel, [array, piece], outs, [_sem(2), _sem(6), _sem(6)] + CTX_SEMS, cid, name
-    )
-
-
-def plain_gather(array, cid, name):
-    def kernel(own, whole, own_sem, send_sem, recv_sem):
-        place = _place()
-        _greet([place[4], place[5]])
-        _gather_body([own], [whole], own_sem, send_sem, recv_sem, place)
-
-    outs = [jax.ShapeDtypeStruct((2, 2, 2) + array.shape[1:], array.dtype)]
-    return _comm_call(kernel, [array], outs, [_sem(2), _sem(6), _sem(6)], cid, name)[0]
-
-
-def group_scatter(main, side, cid, name, piece=None):
-    spread = piece is not None
-
-    def kernel(*refs):
-        main_in, side_in = refs[:2]
-        refs = refs[2:]
-        if spread:
-            piece_in, refs = refs[0], refs[1:]
-        sums, side_all = refs[:2]
-        refs = refs[2:]
-        if spread:
-            spread_out, refs = refs[0], refs[1:]
-        first, staged, second, side_first, side_staged, side_second, side_own = refs[:7]
-        send_sem, recv_sem, gsend_sem, grecv_sem, gown_sem = refs[7:12]
+    vmem = pl.BlockSpec(memory_space=pltpu.VMEM)
+    rows = (2, 128, wide)
+    f32 = lambda *shape: jax.ShapeDtypeStruct(shape, F32)
+    ins = (own, grad_out, gate_w, up_w, down_w, first_gu, second_g, second_u, first_d, second_d)
+    outs = [
+        f32(*rows),
+        f32(*rows),
+        jax.ShapeDtypeStruct(rows, BF16),
+        jax.ShapeDtypeStruct((4, 2, 128, width), BF16),
+        f32(RANK, units),
+        f32(RANK, units),
+        f32(RANK, units),
+    ]
+    return pl.pallas_call(
+        kernel,
+        out_shape=outs,
+        in_specs=[vmem] * len(ins),
+        out_specs=[vmem] * len(outs),
+        scratch_shapes=[pltpu.VMEM((4, 256, units), BF16)] * 3
+        + [pltpu.VMEM((4, 256, SIDE), BF16)] * 2
+        + [pltpu.VMEM((3,) + rows, BF16)] * 2
+        + [pltpu.VMEM(rows, BF16)] * 6
+        + [_sem(2), _sem(6), _sem(6), _sem(8), _sem(8)],
+        compiler_params=pltpu.CompilerParams(
+            collective_id=cid, has_side_effects=True, vmem_limit_bytes=56 * 1024 * 1024
+        ),
+        name="feed_forward",
+    )(*ins)
+
+
+def group_scatter(main, side, cid, name):
+    def kernel(
+        main_in,
+        side_in,
+        sums,
+        side_all,
+        first,
+        staged,
+        second,
+        side_first,
+        side_staged,
+        side_second,
+        side_own,
+        send_sem,
+        recv_sem,
+        gown_sem,
+        gsend_sem,
+        grecv_sem,
+    ):
         place = _place()
         c, f, x, core, core_peer, x_peer = place
         h = 1 - core
-        _greet([core_peer, x_peer] + (_ctx_peers(place) if spread else []))
-        if spread:
-            start, forward, finish = _ctx_body(piece_in, spread_out, *refs[12:], place)
+        _greet([core_peer, x_peer])
         group = (
             (side_in, side_first, side_staged, side_second),
             (main_in, first, staged, second),
@@ -732,8 +942,6 @@
                 cp = _remote(stage.at[j], land_two.at[j], send_sem.at[k], recv_sem.at[k], x_peer)
                 cp.start()
                 two[(i, j)] = cp
-        if spread:
-            state = start()
         for j in range(2):
             one[(0, j, 0)].wait_recv()
             two[(0, j)].wait_recv()
@@ -747,18 +955,14 @@
         for j in range(2):
             one[(1, j, 0)].wait_recv()
             sums[j] = main_in[h, j, x].astype(F32) + first[0, j].astype(F32)
-        if spread:
-            state = forward(state)
         glast()
         for j in range(2):
             two[(1, j)].wait_recv()
             sums[j] = sums[j] + second[j].astype(F32)
-        if spread:
-            finish(state)
         for cp in list(one.values()) + list(two.values()):
             cp.wait_send()
 
-    vmem, hbm = pl.BlockSpec(memory_space=pltpu.VMEM), pl.BlockSpec(memory_space=pl.ANY)
+    vmem = pl.BlockSpec(memory_space=pltpu.VMEM)
     outs = [
         jax.ShapeDtypeStruct((2,) + main.shape[3:], F32),
         jax.ShapeDtypeStruct(side.shape, BF16),
@@ -771,25 +975,18 @@
             pltpu.VMEM((2,) + rows, BF16),
         ]
     scratch += [pltpu.VMEM((2,) + side.shape[3:], BF16)]
-    scratch += [_sem(12), _sem(12), _sem(6), _sem(6), _sem(2)]
-    ins, in_specs, out_specs = [main, side], [vmem, vmem], [vmem, vmem]
-    if spread:
-        ins += [piece]
-        in_specs += [hbm]
-        out_specs += [hbm]
-        outs += [_ctx_out(piece)]
-        scratch += CTX_SEMS
+    scratch += [_sem(12), _sem(12), _sem(2), _sem(6), _sem(6)]
     return pl.pallas_call(
         kernel,
         out_shape=outs,
-        in_specs=in_specs,
-        out_specs=out_specs,
+        in_specs=[vmem, vmem],
+        out_specs=[vmem, vmem],
         scratch_shapes=scratch,
         compiler_params=pltpu.CompilerParams(
             collective_id=cid, has_side_effects=True, vmem_limit_bytes=40 * 1024 * 1024
         ),
         name=name,
-    )(*ins)
+    )(main, side)
 
 
 def take_in(tokens, cotangent, cid):
@@ -876,21 +1073,50 @@
     return [(((2 * f + half) % 4) * 2 + (2 * f + half) // 4, from_f) for half in range(2)]
 
 
-def give_back(array, piece, cid):
-    def kernel(own, piece_in, out, spread, out_s, out_r, *ctx_sems):
+def give_back(arrays, piece, lines, cid):
+    count = len(arrays)
+    n = piece.shape[1]
+
+    def kernel(*refs):
+        owns, (piece_in, lines_in) = refs[:count], refs[count : count + 2]
+        backs = refs[count + 2 : 2 * count + 2]
+        spread, lines_out, late = refs[2 * count + 2 : 2 * count + 5]
+        sems = refs[2 * count + 5 :]
         place = _place()
-        _greet(_back_sources(place) + [place[4], place[5]] + _ctx_peers(place))
-        start, forward, finish = _ctx_body(piece_in, spread, *ctx_sems, place)
-        first, last = _back_steps(own, out, out_s, out_r, place)
-        state = start()
-        first()
-        finish(forward(state))
-        last()
-
-    outs = [jax.ShapeDtypeStruct(array.shape, array.dtype), _ctx_out(piece)]
+        _greet(
+            _back_sources(place) + [place[4], place[5], _y_peer(place)] + _z_peers(place)
+        )
+        start, across, finish = _ctx_first(piece_in, late, *sems[2 * count : 2 * count + 3], place)
+        second = _ctx_second(late, spread, *sems[2 * count + 3 : 2 * count + 6], place)
+        other = _ctx_second(lines_in, lines_out, *sems[2 * count + 6 :], place)
+        steps = [
+            _back_steps(owns[i], backs[i], sems[2 * i], sems[2 * i + 1], place)
+            for i in range(count)
+        ]
+        start()
+        other[0]()
+        across()
+        for first, _ in steps:
+            first()
+        finish()
+        second[0]()
+        other[1]()
+        second[1]()
+        other[2]()
+        second[2]()
+        for _, last in steps:
+            last()
+
+    outs = [jax.ShapeDtypeStruct(a.shape, a.dtype) for a in arrays]
+    outs += [_spread_of(n), _spread_of(lines.shape[-1]), jax.ShapeDtypeStruct(_lines_of(n), BF16)]
     return _comm_call(
-        kernel, [array, piece], outs, [_sem(2), _sem(2)] + CTX_SEMS, cid, "give_back"
-    )
+        kernel,
+        list(arrays) + [piece, lines],
+        outs,
+        [_sem(2)] * (2 * count) + FIRST_SEMS + SECOND_SEMS + SECOND_SEMS,
+        cid,
+        "give_back",
+    )[:-1]
 
 
 def attend_call(proj, cosine, sine, length, behind, cid):
@@ -915,7 +1141,9 @@
     ):
         place = _place()
         _greet([place[4], place[5]])
-        first, last = _gather_steps([behind_ref], [whole_ref], own_sem, send_sem, recv_sem, place)
+        first, forward, own_here, core_here, far_here, last = _order_steps(
+            behind_ref, whole_ref, own_sem, send_sem, recv_sem, place
+        )
         first()
         live = len_ref[0]
         for part in range(6):
@@ -930,7 +1158,6 @@
             qpos = block * step + lax.broadcasted_iota(jnp.int32, (step, keys), 0)
             kpos = lax.broadcasted_iota(jnp.int32, (step, keys), 1)
             allowed = (kpos <= qpos) & (kpos < live)
-            pieces = []
             stats = jnp.zeros((step, lane), F32)
             lanes = lax.broadcasted_iota(jnp.int32, (step, lane), 1)
             for head in range(4):
@@ -944,20 +1171,25 @@
                 p = jnp.where(allowed, jnp.exp(s - top), 0.0)
                 total = jnp.sum(p, axis=1, keepdims=True)
                 o = jnp.dot(p.astype(BF16), v, preferred_element_type=F32) / total
-                pieces.append(o[:, :HEAD_DIM])
+                att_ref[row, head * lane : (head + 1) * lane] = o.astype(BF16)
                 stats = jnp.where(lanes == head, top + jnp.log(total), stats)
-            att_ref[row, :] = jnp.concatenate(pieces, axis=1).astype(BF16)
             lse_ref[row, :] = stats
+        own_here()
+        core_here()
+        for j in range(2):
+            forward(j)
+        for j in range(2):
+            far_here(j)
         last()
 
     vmem, hbm = pl.BlockSpec(memory_space=pltpu.VMEM), pl.BlockSpec(memory_space=pl.ANY)
     return pl.pallas_call(
         kernel,
         out_shape=(
-            jax.ShapeDtypeStruct((rows, 4 * HEAD_DIM), BF16),
+            jax.ShapeDtypeStruct((rows, 4 * lane), BF16),
             jax.ShapeDtypeStruct(proj.shape, BF16),
             jax.ShapeDtypeStruct((rows, lane), F32),
-            jax.ShapeDtypeStruct((2, 2, 2) + behind.shape[1:], behind.dtype),
+            jax.ShapeDtypeStruct((4,) + behind.shape, behind.dtype),
         ),
         in_specs=[pl.BlockSpec(memory_space=pltpu.SMEM), vmem, vmem, vmem, hbm],
         out_specs=(vmem, vmem, vmem, hbm),
@@ -969,95 +1201,316 @@
     )(length, proj, cosine, sine, behind)
 
 
-def attend_back_call(qkv, stats, grad_att, cosine, sine, length, behind, cid):
+def attend_back_call(
+    low_own,
+    small_own,
+    early,
+    out_far,
+    out_side,
+    qkv,
+    stats,
+    att,
+    inner_o,
+    order,
+    cosine,
+    sine,
+    length,
+    out_w,
+    first_o,
+    second_o,
+    weight_all,
+    second_all,
+    cid,
+):
+    width = low_own.shape[-1]
     rows = qkv.shape[0]
-    step = 256
+    wide = width + SIDE
+    step_rows = 256
     scale = HEAD_DIM ** (-0.5)
     lane = PAD_HEAD
-
-    def kernel(
-        len_ref,
-        qkv_ref,
-        lse_ref,
-        g_ref,
-        cos_ref,
-        sin_ref,
-        behind_ref,
-        out_ref,
-        back_ref,
-        dk_ref,
-        dv_ref,
-        do_ref,
-        out_s,
-        out_r,
-    ):
+    quarter = width // 4
+    middle_n = 4 * quarter
+    early_n = early.shape[1]
+    big = (qkv, stats, att, inner_o, order, cosine, sine, out_w, first_o, second_o, weight_all, second_all)
+    count = len(big)
+
+    def kernel(*refs):
+        len_ref, low_ref, small_ref, early_ref, out_ref, out_side_ref = refs[:6]
+        big_in = refs[6 : 6 + count]
+        sums, side_all, grad_ref, landed_out, early_out, middle_lines, early_lines, small_out = refs[
+            6 + count : 14 + count
+        ]
+        refs = refs[14 + count :]
+        (
+            qkv_ref,
+            lse_ref,
+            att_ref,
+            inner_ref,
+            order_ref,
+            cos_ref,
+            sin_ref,
+            ow_ref,
+            fo_ref,
+            so_ref,
+            wa_ref,
+            sa_ref,
+        ) = refs[:count]
+        (
+            low,
+            do_ref,
+            gio_ref,
+            dk_ref,
+            dv_ref,
+            part,
+            land,
+            staged,
+            landed,
+            side_own,
+            middle_ref,
+            load_sem,
+            own_sem,
+            send_sem,
+            recv_sem,
+            s_sem,
+            r_sem,
+        ) = refs[count : count + 17]
+        sems = refs[count + 17 :]
         place = _place()
-        _greet(_back_sources(place))
-        first, last = _back_steps(behind_ref, back_ref, out_s, out_r, place)
-        first()
+        c, f, x, core, core_peer, x_peer = place
+        _greet([core_peer, x_peer, _y_peer(place)] + _z_peers(place))
+        loads = [
+            pltpu.make_async_copy(big_in[i], refs[i], load_sem.at[i]) for i in range(count)
+        ]
+        small_first, small_forward, small_own_here, small_core, small_far, small_last = _order_steps(
+            small_ref, small_out, *sems[0:3], place
+        )
+        early_start, early_across, early_finish = _ctx_first(early_ref, early_lines, *sems[3:6], place)
+        early_two = _ctx_second(early_lines, early_out, *sems[6:9], place)
+        mid_start, mid_across, mid_finish = _ctx_first(middle_ref, middle_lines, *sems[9:12], place)
+        side_first, side_last = _gather_steps([side_own], [side_all], *sems[12:15], place)
         live = len_ref[0]
-        pad = jnp.zeros((rows, lane - HEAD_DIM), BF16)
-        for head in range(4):
-            do_ref[head] = jnp.concatenate(
-                [g_ref[:, head * HEAD_DIM : (head + 1) * HEAD_DIM], pad], axis=1
-            )
+
+        sends = {}
+        hh = 1 - core
+        local = []
+        small_first()
+        early_start()
+        for k, target in ((0, x_peer), (2, core_peer)):
+            for j in (1, 0):
+                cp = _remote(
+                    low_ref.at[j], low.at[hh, j, x], send_sem.at[k + j], recv_sem.at[k + j], target
+                )
+                cp.start()
+                sends[(k, j)] = cp
+        for j in range(2):
+            lc = pltpu.make_async_copy(low_ref.at[j], low.at[hh, j, x], own_sem.at[j])
+            lc.start()
+            local.append(lc)
+        for cp in loads:
+            cp.start()
+        swaps = [
+            _remote(out_ref.at[j], landed_out.at[j], s_sem.at[8 + j], r_sem.at[8 + j], x_peer)
+            for j in range(2)
+        ]
         dk_ref[...] = jnp.zeros_like(dk_ref)
         dv_ref[...] = jnp.zeros_like(dv_ref)
-        for block in range(rows // step):
-            keys = (block + 1) * step
-            row = pl.ds(block * step, step)
-            qpos = block * step + lax.broadcasted_iota(jnp.int32, (step, keys), 0)
-            kpos = lax.broadcasted_iota(jnp.int32, (step, keys), 1)
+        early_across()
+        small_own_here()
+        for j in range(2):
+            small_forward(j)
+        for cp in loads:
+            cp.wait()
+        for lc in local:
+            lc.wait()
+
+        def arrive(j):
+            sends[(0, j)].wait_recv()
+            cp = _remote(
+                low.at[hh, j, 1 - x],
+                low.at[hh, j, 1 - x],
+                send_sem.at[4 + j],
+                recv_sem.at[4 + j],
+                core_peer,
+            )
+            cp.start()
+            sends[(4, j)] = cp
+            sends[(2, j)].wait_recv()
+            cp.wait_recv()
+
+        def through_output(t):
+            g = low[t // 2, t % 2].reshape(step_rows, width)
+            gio = dot_t(g, so_ref[...]).astype(BF16)
+            row = pl.ds(t * step_rows, step_rows)
+            gio_ref[row, :] = gio
+            do_ref[row, :] = (dot_t(g, ow_ref[...]) + dot_t(gio, fo_ref[...])).astype(BF16)
+
+        def attention(t, hook):
+            keys = (t + 1) * step_rows
+            row = pl.ds(t * step_rows, step_rows)
+            qpos = t * step_rows + lax.broadcasted_iota(jnp.int32, (step_rows, keys), 0)
+            kpos = lax.broadcasted_iota(jnp.int32, (step_rows, keys), 1)
             allowed = (kpos <= qpos) & (kpos < live)
             cos, sin = cos_ref[row, :], sin_ref[row, :]
             for head in range(4):
                 kv = head // 2
-                q = qkv_ref[row, head * lane : (head + 1) * lane]
+                at = slice(head * lane, (head + 1) * lane)
+                q = qkv_ref[row, at]
                 k = qkv_ref[:keys, (4 + kv) * lane : (5 + kv) * lane]
                 v = qkv_ref[:keys, (6 + kv) * lane : (7 + kv) * lane]
-                do = do_ref[head, row, :]
-                s = lax.dot_general(q, k, (((1,), (1,)), ((), ())), preferred_element_type=F32)
+                do = do_ref[row, at]
+                s = dot_t(q, k)
                 p = jnp.where(allowed, jnp.exp(s * scale - lse_ref[row, head : head + 1]), 0.0)
-                dp = lax.dot_general(do, v, (((1,), (1,)), ((), ())), preferred_element_type=F32)
-                dot = jnp.sum(p * dp, axis=1, keepdims=True)
-                ds = (p * (dp - dot)).astype(BF16)
-                dq = scale * jnp.dot(ds, k, preferred_element_type=F32)
+                dp = dot_t(do, v)
+                total = jnp.sum(p * dp, axis=1, keepdims=True)
+                ds = (p * (dp - total)).astype(BF16)
+                dq = scale * dot(ds, k)
                 dq = dq * cos - pltpu.roll(dq, HALF_PAD, 1) * sin
-                out_ref[row, head * lane : (head + 1) * lane] = dq.astype(BF16)
-                dk_ref[kv, :keys] += lax.dot_general(
-                    ds, q, (((0,), (0,)), ((), ())), preferred_element_type=F32
-                )
-                dv_ref[kv, :keys] += lax.dot_general(
-                    p.astype(BF16), do, (((0,), (0,)), ((), ())), preferred_element_type=F32
-                )
-        for kv in range(2):
-            dk = scale * dk_ref[kv]
-            dk = dk * cos_ref[...] - pltpu.roll(dk, HALF_PAD, 1) * sin_ref[...]
-            out_ref[:, (4 + kv) * lane : (5 + kv) * lane] = dk.astype(BF16)
-            out_ref[:, (6 + kv) * lane : (7 + kv) * lane] = dv_ref[kv].astype(BF16)
-        last()
+                grad_ref[row, at] = dq.astype(BF16)
+                dk_ref[kv, :keys] += dot_rows(ds, q)
+                dv_ref[kv, :keys] += dot_rows(p.astype(BF16), do)
+                if head == 1 and hook is not None:
+                    hook()
+            for kv in range(2):
+                dk = scale * dk_ref[kv, row, :]
+                dk = dk * cos - pltpu.roll(dk, HALF_PAD, 1) * sin
+                grad_ref[row, (4 + kv) * lane : (5 + kv) * lane] = dk.astype(BF16)
+                grad_ref[row, (6 + kv) * lane : (7 + kv) * lane] = dv_ref[kv, row, :].astype(BF16)
+            g = grad_ref[row, :]
+            for at in range(0, width, 256):
+                value = dot_t(g, wa_ref[at : at + 256, :])
+                part[t, :, :, at : at + 256] = value.astype(BF16).reshape(2, 128, 256)
+            part[t, :, :, width:] = dot_t(g, sa_ref[...]).astype(BF16).reshape(2, 128, SIDE)
+
+        def to_core(t):
+            h, j = t // 2, t % 2
+            return _remote(part.at[t], land.at[j], s_sem.at[j], r_sem.at[j], core_peer)
+
+        def to_x(j):
+            return _remote(staged.at[j], landed.at[j], s_sem.at[2 + j], r_sem.at[2 + j], x_peer)
+
+        def leave(t):
+            @pl.when(core == t // 2)
+            def _():
+                to_core(t).start()
+
+        def combine(t):
+            j = t % 2
+
+            @pl.when(core == 1 - t // 2)
+            def _():
+                to_core(t).wait_recv()
+                staged[j] = (part[t, 1 - x].astype(F32) + land[j, 1 - x].astype(F32)).astype(BF16)
+                to_x(j).start()
+                sums[j] = part[t, x].astype(F32) + land[j, x].astype(F32)
+
+        arrive(1)
+        through_output(3)
+        through_output(1)
+        for cp in swaps:
+            cp.start()
+        attention(3, None)
+        leave(3)
+        arrive(0)
+        through_output(2)
+        through_output(0)
+        o_a = dot_rows(gio_ref[...], att_ref[...])[:RANK]
+        o_a = jnp.concatenate(
+            [o_a[:, head * lane : head * lane + HEAD_DIM] for head in range(4)], axis=1
+        )
+        middle_ref[:, :quarter] = o_a.astype(BF16)
+        own_cols = pl.ds(pl.multiple_of(f * quarter, 128), quarter)
+        g = low[:, :, :, :, own_cols].reshape(rows, quarter)
+        middle_ref[:, quarter : 2 * quarter] = (ADAPTER_SCALE * dot_rows(inner_ref[...], g)[:RANK]).astype(BF16)
+        for j in range(2):
+            small_far(j)
+        small_core()
+        in_gu = jnp.zeros((SIDE, quarter), F32)
+        for k in range(4):
+            u = order_ref[k, :, :, own_cols].reshape(step_rows, quarter)
+            in_gu += dot_rows(small_out[k].reshape(step_rows, SIDE), u)
+        middle_ref[:, 2 * quarter : 3 * quarter] = in_gu[:RANK].astype(BF16)
+        middle_ref[:, 3 * quarter :] = in_gu[RANK : 2 * RANK].astype(BF16)
+        mid_start()
+        early_finish()
+        early_two[0]()
+        mid_across()
+        attention(2, lambda: combine(3))
+        leave(2)
+        attention(1, lambda: combine(2))
+        leave(1)
+        early_two[1]()
+        attention(0, lambda: combine(1))
+        leave(0)
+        combine(0)
+        for t in range(4):
+
+            @pl.when(core == t // 2)
+            def _():
+                to_core(t).wait_send()
+
+        for j in range(2):
+            swaps[j].wait()
+            cp = to_x(j)
+            cp.wait_recv()
+            sums[j] = sums[j] + landed[j].astype(F32)
+            cp.wait_send()
+            side_own[j] = (
+                sums[j, :, width:] + out_side_ref[j] + landed_out[j, :, width:].astype(F32)
+            ).astype(BF16)
+        side_first()
+        small_last()
+        early_two[2]()
+        mid_finish()
+        side_last()
+        for cp in sends.values():
+            cp.wait_send()
 
     vmem, hbm = pl.BlockSpec(memory_space=pltpu.VMEM), pl.BlockSpec(memory_space=pl.ANY)
+    shape = jax.ShapeDtypeStruct
     return pl.pallas_call(
         kernel,
         out_shape=[
-            jax.ShapeDtypeStruct(qkv.shape, BF16),
-            jax.ShapeDtypeStruct(behind.shape, behind.dtype),
+            shape((2, 128, wide), F32),
+            shape((2, 2, 2, 128, SIDE), BF16),
+            shape(qkv.shape, BF16),
+            shape(out_far.shape, BF16),
+            _spread_of(early_n),
+            shape(_lines_of(middle_n), BF16),
+            shape(_lines_of(early_n), BF16),
+            shape((4, 2, 128, SIDE), BF16),
         ],
-        in_specs=[pl.BlockSpec(memory_space=pltpu.SMEM)] + [vmem] * 5 + [hbm],
-        out_specs=[vmem, hbm],
-        scratch_shapes=[
+        in_specs=[pl.BlockSpec(memory_space=pltpu.SMEM)] + [hbm] * 4 + [vmem] + [hbm] * count,
+        out_specs=[vmem, hbm, vmem, vmem, hbm, hbm, hbm, vmem],
+        scratch_shapes=[pltpu.VMEM(a.shape, a.dtype) for a in big]
+        + [
+            pltpu.VMEM((2, 2, 2, 128, width), BF16),
+            pltpu.VMEM((rows, 4 * lane), BF16),
+            pltpu.VMEM((rows, SIDE), BF16),
             pltpu.VMEM((2, rows, lane), F32),
             pltpu.VMEM((2, rows, lane), F32),
-            pltpu.VMEM((4, rows, lane), BF16),
+            pltpu.VMEM((4, 2, 128, wide), BF16),
+            pltpu.VMEM((2, 2, 128, wide), BF16),
+            pltpu.VMEM((2, 128, wide), BF16),
+            pltpu.VMEM((2, 128, wide), BF16),
+            pltpu.VMEM((2, 128, SIDE), BF16),
+            pltpu.VMEM((RANK, middle_n), BF16),
+            _sem(count),
             _sem(2),
-            _sem(2),
-        ],
+            _sem(6),
+            _sem(6),
+            _sem(10),
+            _sem(10),
+        ]
+        + [_sem(2), _sem(6), _sem(6)]
+        + FIRST_SEMS
+        + SECOND_SEMS
+        + FIRST_SEMS
+        + [_sem(2), _sem(6), _sem(6)],
         compiler_params=pltpu.CompilerParams(
-            collective_id=cid, has_side_effects=True, vmem_limit_bytes=40 * 1024 * 1024
+            collective_id=cid, has_side_effects=True, vmem_limit_bytes=58 * 1024 * 1024
         ),
         name="attend_back",
-    )(length, qkv, stats, grad_att, cosine, sine, behind)
+    )(length, low_own, small_own, early, out_far, out_side, *big)
 
 
 def table_call(early, middle, late, adapters):
@@ -1074,9 +1527,17 @@
         f32(choices, RANK, 1536),
     ]
     plan = (
-        ((6, 0, 1024), (6, 1, 1024), (2, None, 1024), (0, 3, 384), (0, 4, 384), (7, None, 384)),
-        ((1, None, 384), (5, None, 384), (3, None, 384), (4, 0, 192), (4, 1, 192)),
-        ((0, 0, 384), (0, 1, 384), (0, 2, 384)),
+        ((6, 0, 1024), (6, 1, 1024), (2, None, 1024)),
+        ((1, None, 384), (5, None, 384), (0, 3, 384), (0, 4, 384)),
+        (
+            (0, 0, 384),
+            (0, 1, 384),
+            (0, 2, 384),
+            (3, None, 384),
+            (4, 0, 192),
+            (4, 1, 192),
+            (7, None, 384),
+        ),
     )
 
     def kernel(which, early_ref, middle_ref, late_ref, *refs):
@@ -1088,7 +1549,7 @@
                 for f in range(4):
                     at = 0
                     for out, table, n in plan[piece]:
-                        value = ref[origin, f, :, at : at + n].astype(F32)
+                        value = ref[origin // 4, f % 2, origin % 4, f // 2, :, at : at + n].astype(F32)
                         cols = slice(f * n, (f + 1) * n)
                         if table is None:
                             acc[out][row, :, cols] += value
@@ -1104,17 +1565,16 @@
             cp.start()
             return cp
 
-        for out in (2, 6, 7):
+        for out in (2, 6):
             acc[out][...] = jnp.zeros_like(acc[out])
-        acc[0][...] = jnp.zeros_like(acc[0])
         add(0, early_ref)
-        copies = [send(out) for out in (2, 6, 7)]
-        for out in (1, 3, 4, 5):
+        copies = [send(out) for out in (2, 6)]
+        for out in (0, 1, 3, 4, 5, 7):
             acc[out][...] = jnp.zeros_like(acc[out])
         add(1, middle_ref)
-        copies += [send(out) for out in (1, 3, 4, 5)]
+        copies += [send(out) for out in (1, 5)]
         add(2, late_ref)
-        copies += [send(0)]
+        copies += [send(out) for out in (0, 3, 4, 7)]
         for cp in copies:
             cp.wait()
 
@@ -1142,8 +1602,8 @@
     return lax.dot_general(left, right, (((0,), (0,)), ((), ())), preferred_element_type=F32)
 
 
-def side_pad(value):
-    return jnp.pad(value, ((0, 0), (0, SIDE - value.shape[1])))
+def side_pad(value, before=0):
+    return jnp.pad(value, ((0, 0), (before, SIDE - before - value.shape[1])))
 
 
 def blocks(value):
@@ -1228,6 +1688,13 @@
         rows = g.shape[0]
         return g.reshape(rows, -1, PAD_HEAD)[..., :HEAD_DIM].reshape(rows, -1)
 
+    def pad_heads(w):
+        w = w.reshape(-1, HEAD_DIM, w.shape[1])
+        w = jnp.pad(w, ((0, 0), (0, PAD_HEAD - HEAD_DIM), (0, 0)))
+        return w.reshape(-1, w.shape[2])
+
+    out_w = pad_heads(output_weight)
+    first_o_pad = pad_heads(side_pad(first_o_own))
     weight_all = jnp.concatenate(
         [pad_turned(query_weight), pad_turned(key_weight), pad_plain(value_weight)], axis=1
     )
@@ -1269,13 +1736,19 @@
     normed_one = (tokens_f * rms_factor(tokens_f) * attention_norm_gain).astype(BF16)
     inner_qkv = dot(normed_one, first_all).astype(BF16)
     proj = dot(normed_one, weight_all) + ADAPTER_SCALE * dot(inner_qkv, second_all)
-    attn_b, qkv, stats, cot_all = attend_call(proj, cosine, sine, length, cot_own, 9)
-    grad_out = jnp.where(live_rows, flat(cot_all), jnp.zeros((), BF16))
+    attn_b, qkv, stats, cot_order = attend_call(proj, cosine, sine, length, cot_own, 9)
+    block_x = x + jnp.array([[0, 0], [1, 1], [1, 1], [0, 0]]) * (1 - 2 * x)
+    block_core = core + jnp.array([[0, 0], [1, 0], [1, 0], [1, 1]]) * (1 - 2 * core)
+    block_j = jnp.array([[0, 1], [0, 0], [1, 1], [0, 1]])
+    order_block = (block_x + 2 * block_j + 4 * (1 - block_core)).reshape(8)
+    order_pos = 128 * order_block.reshape(4, 2, 1) + jnp.arange(128, dtype=jnp.int32)
+    order_live = (order_pos < length[0])[..., None]
+    grad_out = jnp.where(order_live, cot_order, jnp.zeros((), BF16)).reshape(4, 256, width)
     grad_out_own = jnp.where(own_live, flat(cot_own), jnp.zeros((), BF16))
 
     sums, side_all = group_scatter(
-        blocks(dot(attn_b, output_weight).astype(BF16)),
-        blocks(side_pad(dot(attn_b, first_o_own)).astype(BF16)),
+        blocks(dot(attn_b, out_w).astype(BF16)),
+        blocks(dot(attn_b, first_o_pad).astype(BF16)),
         1,
         "scatter_o",
     )
@@ -1285,100 +1758,93 @@
     resid = own_f + flat(sums) + ADAPTER_SCALE * dot(inner_o_own, second_o)
     factor_two = rms_factor(resid)
     normed_two_own = (resid * factor_two * feedforward_norm_gain).astype(BF16)
-    normed_two = flat(plain_gather(own_blocks(normed_two_own), 2, "gather_two"))
-
-    inner_gu = dot(normed_two, first_gu).astype(BF16)
-    gate = dot(normed_two, gate_weight) + ADAPTER_SCALE * dot(inner_gu[:, :RANK], second_gu[0])
-    up_proj = dot(normed_two, up_weight) + ADAPTER_SCALE * dot(inner_gu[:, RANK:], second_gu[1])
-    sigmoid_gate = jax.nn.sigmoid(gate)
-    hidden = (gate * sigmoid_gate * up_proj).astype(BF16)
-    grad_inner_d = (ADAPTER_SCALE * dot_t(grad_out, second_d)).astype(BF16)
-    grad_hidden = dot_t(grad_out, down_weight) + dot_t(grad_inner_d, first_d_own)
-    grad_gate = (grad_hidden * up_proj * sigmoid_gate * (1.0 + gate * (1.0 - sigmoid_gate))).astype(
-        BF16
-    )
-    grad_up = (grad_hidden * gate * sigmoid_gate).astype(BF16)
-    grad_two = (dot_t(grad_gate, gate_weight) + dot_t(grad_up, up_weight)).astype(BF16)
-    side_gu = ADAPTER_SCALE * jnp.concatenate(
-        [dot_t(grad_gate, second_gu[0]), dot_t(grad_up, second_gu[1])], axis=1
-    )
-    sums, side_all = group_scatter(
-        blocks(grad_two), blocks(side_pad(side_gu).astype(BF16)), 3, "scatter_two"
-    )
-    grad_inner_gu = flat(side_all)[:, : 2 * RANK]
-    grad_inner_gu_own = own_rows(side_all)[:, : 2 * RANK]
+
+    def pad_rank(table, before=0):
+        return jnp.pad(table, ((before, SIDE - before - table.shape[0]), (0, 0)))
+
+    sums, out_sums, out_far, order, gate_b, up_b, down_a = feed_forward(
+        own_blocks(normed_two_own),
+        grad_out,
+        gate_weight,
+        up_weight,
+        down_weight,
+        side_pad(first_gu),
+        pad_rank((ADAPTER_SCALE * second_gu[0]).astype(BF16)),
+        pad_rank((ADAPTER_SCALE * second_gu[1]).astype(BF16), RANK),
+        side_pad(first_d_own, 3 * RANK),
+        pad_rank((ADAPTER_SCALE * second_d).astype(BF16), 3 * RANK),
+        3,
+    )
+    sums = flat(sums)
+    grad_inner_gu_own = sums[:, width : width + 2 * RANK].astype(BF16)
+    sums = sums[:, :width]
     grad_normed_two = (
-        (flat(sums) + dot_t(grad_inner_gu_own, first_gu)).astype(BF16).astype(F32)
+        (sums + dot_t(grad_inner_gu_own, first_gu)).astype(BF16).astype(F32)
     )
     grad_resid = grad_out_own.astype(F32) + norm_back(
         resid, factor_two, feedforward_norm_gain, grad_normed_two
     )
     grad_low_own = grad_resid.astype(BF16)
 
-    sums, side_all = group_scatter(
-        blocks(dot(hidden, down_weight).astype(BF16)),
-        blocks(side_pad(dot(hidden, first_d_own)).astype(BF16)),
-        4,
-        "scatter_out",
-    )
-    inner_d = flat(side_all)[:, :RANK]
-    inner_d_own = own_rows(side_all)[:, :RANK]
-    out_own = jnp.where(
-        own_live, resid + flat(sums) + ADAPTER_SCALE * dot(inner_d_own, second_d), 0.0
-    ).astype(BF16)
-
     def pack(parts):
         return jnp.concatenate(parts, axis=1).astype(BF16)
 
-    two_cut = cut(normed_two, 1, quarter)
-    in_gu = dot_rows(grad_inner_gu, two_cut)
-    early = pack(
+    early = pack([gate_b, up_b, down_a])
+    second_scaled = (ADAPTER_SCALE * second_all).astype(BF16)
+    sums, side_all, grad_qkv, out_landed, early, middle = attend_back_call(
+        own_blocks(grad_low_own),
+        own_blocks(side_pad(grad_inner_gu_own)),
+        early,
+        out_far,
+        out_sums[..., width:],
+        qkv,
+        stats,
+        attn_b,
+        flat(side_all),
+        order,
+        cosine,
+        sine,
+        length,
+        out_w,
+        first_o_pad,
+        pad_rank((ADAPTER_SCALE * second_o).astype(BF16)),
+        weight_all,
+        jnp.pad(second_scaled, ((0, SIDE - 3 * RANK), (0, 0))),
+        10,
+    )[:6]
+    out_sums = flat(out_sums) + flat(out_landed).astype(F32)
+    inner_d_own = out_sums[:, width + 3 * RANK : width + 4 * RANK].astype(BF16)
+    out_own = jnp.where(
+        own_live, resid + out_sums[:, :width] + ADAPTER_SCALE * dot(inner_d_own, second_d), 0.0
+    ).astype(BF16)
+    all_b = ADAPTER_SCALE * dot_rows(inner_qkv, grad_qkv)
+    sums = flat(sums)
+    grad_inner_qkv = flat(side_all)[:, : 3 * RANK]
+    grad_inner_own = sums[:, width : width + 3 * RANK].astype(BF16)
+    grad_normed_one = (sums[:, :width] + dot_t(grad_inner_own, first_all)).astype(BF16).astype(F32)
+    grad_tok_own = grad_resid + norm_back(
+        own_f, rms_factor(own_f), attention_norm_gain, grad_normed_one
+    )
+    one_cut = cut(normed_one, 1, quarter)
+    in_qkv = dot_rows(grad_inner_qkv, one_cut)
+    inner_d = flat(side_all.reshape(8, 128, SIDE)[order_block])[:, 3 * RANK : 4 * RANK]
+    d_b = ADAPTER_SCALE * dot_rows(inner_d, cut(flat(grad_out), 1, quarter))
+    late = pack(
         [
-            ADAPTER_SCALE * dot_rows(inner_gu[:, :RANK], grad_gate),
-            ADAPTER_SCALE * dot_rows(inner_gu[:, RANK:], grad_up),
-            dot_rows(grad_inner_d, hidden),
-            in_gu[:RANK],
-            in_gu[RANK:],
-            ADAPTER_SCALE * dot_rows(inner_d, cut(grad_out, 1, quarter)),
-        ]
-    )
-    grad_low, early = group_gather(own_blocks(grad_low_own), early, 5, "gather_resid")
-    grad_low = flat(grad_low)
-    grad_inner_o = (ADAPTER_SCALE * dot_t(grad_low, second_o)).astype(BF16)
-    grad_att = (dot_t(grad_low, output_weight) + dot_t(grad_inner_o, first_o_own)).astype(BF16)
-    grad_qkv, out_tokens = attend_back_call(
-        qkv, stats, grad_att, cosine, sine, length, own_blocks(out_own), 10
-    )
-    grad_one = dot_t(grad_qkv, weight_all).astype(BF16)
-    side_qkv = ADAPTER_SCALE * dot_t(grad_qkv, second_all)
-    all_b = ADAPTER_SCALE * dot_rows(inner_qkv, grad_qkv)
-    middle = pack(
-        [
-            dot_rows(grad_inner_o, attn_b),
-            ADAPTER_SCALE * dot_rows(inner_o, cut(grad_low, 1, quarter)),
+            in_qkv[:RANK],
+            in_qkv[RANK : 2 * RANK],
+            in_qkv[2 * RANK :],
             unpad_turned(all_b[:RANK, : 4 * PAD_HEAD]),
             unpad_turned(all_b[RANK : 2 * RANK, 4 * PAD_HEAD : 6 * PAD_HEAD]),
             unpad_plain(all_b[2 * RANK :, 6 * PAD_HEAD :]),
+            d_b,
         ]
     )
-    sums, side_all, middle = group_scatter(
-        blocks(grad_one), blocks(side_pad(side_qkv).astype(BF16)), 6, "scatter_one", middle
-    )
-    grad_inner_qkv = flat(side_all)[:, : 3 * RANK]
-    grad_inner_own = own_rows(side_all)[:, : 3 * RANK]
-    grad_normed_one = (flat(sums) + dot_t(grad_inner_own, first_all)).astype(BF16).astype(F32)
-    grad_tok_own = grad_resid + norm_back(
-        own_f, rms_factor(own_f), attention_norm_gain, grad_normed_one
-    )
-    one_cut = cut(normed_one, 1, quarter)
-    in_qkv = dot_rows(grad_inner_qkv, one_cut)
-    late = pack([in_qkv[:RANK], in_qkv[RANK : 2 * RANK], in_qkv[2 * RANK :]])
-    grad_tokens, late = give_back(own_blocks(grad_tok_own.astype(BF16)), late, 7)
-
-    group_slot = [cc // 2 + 4 * (cc % 2) for cc in range(8)]
-    group_adapter = slot_adapter_index[jnp.array(group_slot, dtype=jnp.int32)]
-    as_devices = lambda piece: piece.reshape((8, 4) + piece.shape[3:])
-    full = table_call(as_devices(early), as_devices(middle), as_devices(late), group_adapter)
+    out_tokens, grad_tokens, late, middle = give_back(
+        [own_blocks(out_own), own_blocks(grad_tok_own.astype(BF16))], late, middle, 7
+    )
+
+    full = table_call(early, middle, late, slot_adapter_index)
     turn = lambda t: jnp.swapaxes(t, -1, -2)
     return (
         out_tokens,

time: 487 us -> 420 us (0.86)
  matrix products: 93 us -> 28.1 us
  Pallas kernels: 323 us -> 307 us
  other arithmetic: 22.2 us -> 31.1 us
  local copies, waits for them, and re-layouts: 35.3 us -> 42.4 us
    pallas_call x4 -> x2, Pallas kernels: 158 us -> 117 us  [_comm_call(): pl.pallas_call(kernel, out_shape=outs, in_specs=[pl.BlockSpec(memory_spac...]
    dot_general x14 -> x7, matrix products: 49.2 us -> 18 us  [dot(): return jnp.dot(left, right, preferred_element_type=F32)]
    dot_general x14 -> x2, matrix products: 34.5 us -> 5.11 us  [dot_t(): lax.dot_general(left, right, (((1,), (1,)), ((), ())), preferred_element_...]
    pallas_call x6 -> x4, Pallas kernels: 158 us -> 184 us  [the longest x1 78.3 us: attend_back_call(): pl.pallas_call(kernel, out_shape=[shape((2, 128, wide), F32), shape((2, 2...]
    unnamed x183 -> x137, local copies, waits for them, and re-layouts: 20.5 us -> 11.1 us
    pad x4 -> x11, local copies, waits for them, and re-layouts: 1.32 us -> 7.28 us  [the longest x4 3.37 us: side_pad(): return jnp.pad(value, ((0, 0), (before, SIDE - before - value.shape[1])))]
    reshape x2 -> x4, local copies, waits for them, and re-layouts: 0.19 us -> 5.29 us  [pad_turned(): return w.reshape(rows, -1)]
where the time goes in v3:
time: 420 us; the launch traced here: 412 us
  Pallas kernels  307 us (73%)
  local copies, waits for them, and re-layouts  42.4 us (10%)
  other arithmetic  31.1 us (7%)
  matrix products  28.1 us (7%)
    pallas_call x2, Pallas kernels, _comm_call(): pl.pallas_call(kernel, out_shape=outs, in_specs=[pl.BlockSpec(memory_spac...  117 us
    pallas_call x1, Pallas kernels, attend_back_call(): pl.pallas_call(kernel, out_shape=[shape((2, 128, wide), F32), shape((2, 2...  78.3 us
    pallas_call x1, Pallas kernels, feed_forward(): pl.pallas_call(kernel, out_shape=outs, in_specs=[vmem] * len(ins), out_sp...  56.7 us
    pallas_call x1, Pallas kernels, group_scatter(): pl.pallas_call(kernel, out_shape=outs, in_specs=[vmem, vmem], out_specs=[...  25.1 us
    pallas_call x1, Pallas kernels, attend_call(): pl.pallas_call(kernel, out_shape=(jax.ShapeDtypeStruct((rows, 4 * lane),...  23.6 us
    dot_general x7, matrix products, dot(): return jnp.dot(left, right, preferred_element_type=F32)  18 us
    unnamed x137, local copies, waits for them, and re-layouts  11.1 us

profile of v3, /device:TPU:3, one launch (start us, length us, event | category | flops | bytes accessed | tf_op | source)
XLA Modules:
  0.0 412.3 jit_solution(10249055196680397045)
XLA Ops:
  5.5 55.6 %take_in.1 = (bf16[2,128,1536]{2,1,0:T(8,128)(2,1)}, bf16[2,128,1536]{2,1,0:T(8,128)(2,1)}, bf16[2,2,2,128,1536]{4,3,2,1,0:T(8,128)(2,1)}) custom-call(bf16[2,128,1536]{2,1,0:T(8,128)(2,1)} %tok.1, bf16[2,128,1536]{2,1,0:T(8,128)(2,1)} %cot.1), custom_call_target="tpu_custom_call" | custom-call | tf_op jit(solution)/shard_map/take_in/pallas_call | solution.py:501
  61.2 2.7 multiply_reduce_fusion
  64.0 2.4 fusion.1
  66.4 3.0 convolution_convert_fusion.2
  80.4 2.3 copy.55
  82.8 5.5 %fusion.45 = f32[1024,1024]{1,0:T(8,128)S(1)} fusion(bf16[1024,1536]{1,0:T(8,128)(2,1)} %fusion.1, bf16[1536,256]{1,0:T(8,128)(2,1)S(1)} %bitcast.129, bf16[1536,256]{1,0:T(8,128)(2,1)} %copy.55, bf16[1536,512]{1,0:T(8,128)(2,1)S(1)} %copy-done.21), kind=kOutput, calls=%fused_computation.118 | convolution fusion | flops 3230662656 | bytes 10485760 | tf_op jit(solution)/shard_map/dot_general | solution.py:1594
  89.8 1.9 fusion.27
  92.9 23.6 %attend.1 = (bf16[1024,512]{1,0:T(8,128)(2,1)S(1)}, bf16[1024,1024]{1,0:T(8,128)(2,1)S(1)}, f32[1024,128]{1,0:T(8,128)S(1)}, bf16[4,2,128,1536]{3,2,1,0:T(8,128)(2,1)S(1)}) custom-call(s32[1]{0:T(128)} %dynamic_slice.54.len_ref.refs_0_, f32[1024,1024]{1,0:T(8,128)S(1)} %multiply_add_fusion.proj_ref, f32[1024,128]{1,0:T(8,128)S(1)} %get-tuple-element.88.cos_ref.refs_11_, ...), custom_call_target="tpu_custom_call" | custom-call | tf_op jit(solution)/shard_map/attend/pallas_call | solution.py:1186
  116.7 4.1 convolution_convert_fusion
  122.4 1.9 copy-done.9
  124.3 25.1 %scatter_o.1 = (f32[2,128,1536]{2,1,0:T(8,128)S(1)}, bf16[2,2,2,128,128]{4,3,2,1,0:T(8,128)(2,1)S(1)}) custom-call(bf16[2,2,2,128,1536]{4,3,2,1,0:T(8,128)(2,1)S(1)} %bitcast.118, bf16[2,2,2,128,128]{4,3,2,1,0:T(8,128)(2,1)S(1)} %bitcast.119), custom_call_target="tpu_custom_call" | custom-call | tf_op jit(solution)/shard_map/scatter_o/pallas_call | solution.py:979
  150.8 1.9 multiply_reduce_fusion.2
  156.3 3.9 broadcast_select_fusion
  162.6 1.8 pad.78.first_ref
  170.8 56.7 %feed_forward.1 = (f32[2,128,1664]{2,1,0:T(8,128)}, f32[2,128,1664]{2,1,0:T(8,128)}, bf16[2,128,1664]{2,1,0:T(8,128)(2,1)}, bf16[4,2,128,1536]{3,2,1,0:T(8,128)(...) custom-call(bf16[2,128,1536]{2,1,0:T(8,128)(2,1)} %bitcast.128, ...), custom_call_target="tpu_custom_call" | custom-call | tf_op jit(solution)/shard_map/feed_forward/pallas_call | solution.py:879
  230.8 3.0 multiply_reduce_fusion.1
  234.6 3.4 fusion.46
  242.9 1.9 pad_maximum_fusion.refs_16_
  244.8 78.3 %attend_back.1 = (f32[2,128,1664]{2,1,0:T(8,128)}, bf16[2,2,2,128,128]{4,3,2,1,0:T(8,128)(2,1)}, bf16[1024,1024]{1,0:T(8,128)(2,1)}, bf16[2,128,1664]{2,1,0:T(8,...) custom-call(s32[1]{0:T(128)} %dynamic_slice.54.len_ref.refs_0_, ...), custom_call_target="tpu_custom_call" | custom-call | tf_op jit(solution)/shard_map/attend_back/pallas_call | solution.py:1470
  326.4 2.1 fusion.18
  331.1 2.1 fusion.17
  336.9 2.3 fusion.5
  339.2 60.9 %give_back.1 = (bf16[2,128,1536]{2,1,0:T(8,128)(2,1)}, bf16[2,128,1536]{2,1,0:T(8,128)(2,1)}, bf16[2,2,4,2,16,2304]{5,4,3,2,1,0:T(8,128)(2,1)}, bf16[2,2,4,2,16,...) custom-call(bf16[2,128,1536]{2,1,0:T(8,128)(2,1)} %bitcast.134, bf16[2,128,1536]{2,1,0:T(8,128)(2,1)} %bitcast.131, ...), custom_call_target="tpu_custom_call" | custom-call | tf_op jit(solution)/shard_map/give_back/pallas_call | solution.py:501
  403.2 6.7 %tables.1 = (f32[8,5,16,1536]{3,2,1,0:T(8,128)}, f32[8,16,1536]{2,1,0:T(8,128)}, f32[8,16,4096]{2,1,0:T(8,128)}, f32[8,16,1536]{2,1,0:T(8,128)}, f32[8,2,16,768]...) custom-call(s32[8]{0:T(128)S(1)} %copy-done.15, ...), custom_call_target="tpu_custom_call" | custom-call | tf_op jit(solution)/shard_map/tables/pallas_call | solution.py:1582
  (219 shorter events, 55.3 us)
Async XLA Ops:
  0.6 163.8 %copy-start = (bf16[8,4096,16]{1,2,0:T(8,128)(2,1)S(1)}, bf16[8,4096,16]{1,2,0:T(8,128)(2,1)}, u32[]{:S(2)}) copy-start(bf16[8,4096,16]{1,2,0:T(8,128)(2,1)} %param.39) | copy-start | bytes 3145732
  5.5 60.9 %copy-start.37 = (bf16[1536,16]{0,1:T(8,128)(2,1)}, bf16[1536,16]{0,1:T(8,128)(2,1)S(1)}, u32[]{:S(2)}) copy-start(bf16[1536,16]{0,1:T(8,128)(2,1)S(1)} %get-tuple-element.84) | copy-start | bytes 147460
  5.5 60.9 %copy-start.39 = (bf16[1536,16]{0,1:T(8,128)(2,1)}, bf16[1536,16]{0,1:T(8,128)(2,1)S(1)}, u32[]{:S(2)}) copy-start(bf16[1536,16]{0,1:T(8,128)(2,1)S(1)} %get-tuple-element.85) | copy-start | bytes 147460
  66.4 7.0 %copy-start.29 = (bf16[1536,384]{1,0:T(8,128)(2,1)S(1)}, bf16[1536,384]{1,0:T(8,128)(2,1)}, u32[]{:S(2)}) copy-start(bf16[1536,384]{1,0:T(8,128)(2,1)} %param.30) | copy-start | bytes 3538948
  79.4 8.9 %copy-start.24 = (bf16[192,8,2,128]{3,1,2,0:T(8,128)(2,1)}, bf16[192,8,2,128]{3,1,2,0:T(8,128)(2,1)S(1)}, u32[]{:S(2)}) copy-start(bf16[192,8,2,128]{3,1,2,0:T(8,128)(2,1)S(1)} %copy.64) | copy-start | bytes 2359300
  92.3 24.1 %copy-start.2 = (f32[1024,128]{1,0:T(8,128)}, f32[1024,128]{1,0:T(8,128)S(1)}, u32[]{:S(2)}) copy-start(f32[1024,128]{1,0:T(8,128)S(1)} %get-tuple-element.87.sin_ref.refs_12_) | copy-start | bytes 1572868
  92.4 24.1 %copy-start.3 = (f32[1024,128]{1,0:T(8,128)}, f32[1024,128]{1,0:T(8,128)S(1)}, u32[]{:S(2)}) copy-start(f32[1024,128]{1,0:T(8,128)S(1)} %get-tuple-element.88.cos_ref.refs_11_) | copy-start | bytes 1572868
  92.9 23.7 %copy-start.30 = (bf16[384,1536]{1,0:T(8,128)(2,1)S(1)}, bf16[384,1536]{1,0:T(8,128)(2,1)}, u32[]{:S(2)}) copy-start(bf16[384,1536]{1,0:T(8,128)(2,1)} %param.33) | copy-start | bytes 3538948
  124.3 25.1 %copy-start.19 = (bf16[2,128,1536]{2,1,0:T(8,128)(2,1)S(1)}, bf16[2,128,1536]{2,1,0:T(8,128)(2,1)}, u32[]{:S(2)}) copy-start(bf16[2,128,1536]{2,1,0:T(8,128)(2,1)} %get-tuple-element.44) | copy-start | bytes 2359300
  152.7 81.8 %copy-start.16 = (f32[256,1536]{1,0:T(8,128)}, f32[256,1536]{1,0:T(8,128)S(1)}, u32[]{:S(2)}) copy-start(f32[256,1536]{1,0:T(8,128)S(1)} %get-tuple-element.104) | copy-start | bytes 4718596
  170.8 59.9 %copy-start.42 = (bf16[1536,16]{0,1:T(8,128)(2,1)S(1)}, bf16[1536,16]{0,1:T(8,128)(2,1)}, u32[]{:S(2)}) copy-start(bf16[1536,16]{0,1:T(8,128)(2,1)} %get-tuple-element.82) | copy-start | bytes 147460
  170.8 59.9 %copy-start.44 = (bf16[1536,16]{0,1:T(8,128)(2,1)S(1)}, bf16[1536,16]{0,1:T(8,128)(2,1)}, u32[]{:S(2)}) copy-start(bf16[1536,16]{0,1:T(8,128)(2,1)} %get-tuple-element.86) | copy-start | bytes 147460
  170.8 60.0 %copy-start.56 = (f32[1536]{0:T(1024)S(1)}, f32[1536]{0:T(1024)}, u32[]{:S(2)}) copy-start(f32[1536]{0:T(1024)} %param.29) | copy-start | bytes 18436
  234.5 6.7 %copy-start.46 = (bf16[16,512]{1,0:T(8,128)(2,1)S(1)}, bf16[16,512]{1,0:T(8,128)(2,1)}, u32[]{:S(2)}) copy-start(bf16[16,512]{1,0:T(8,128)(2,1)} %reshape.318) | copy-start | bytes 49156
  234.5 6.7 %copy-start.48 = (bf16[16,512]{1,0:T(8,128)(2,1)S(1)}, bf16[16,512]{1,0:T(8,128)(2,1)}, u32[]{:S(2)}) copy-start(bf16[16,512]{1,0:T(8,128)(2,1)} %copy-done.47) | copy-start | bytes 49156
  234.6 6.7 %copy-start.50 = (bf16[16,256]{1,0:T(8,128)(2,1)S(1)}, bf16[16,256]{1,0:T(8,128)(2,1)}, u32[]{:S(2)}) copy-start(bf16[16,256]{1,0:T(8,128)(2,1)} %reshape.319) | copy-start | bytes 24580
  234.6 6.7 %copy-start.52 = (bf16[2,8,2,128]{3,1,2,0:T(8,128)(2,1)S(1)}, bf16[2,8,2,128]{3,1,2,0:T(8,128)(2,1)}, u32[]{:S(2)}) copy-start(bf16[2,8,2,128]{3,1,2,0:T(8,128)(2,1)} %copy.65) | copy-start | bytes 24580
  234.6 6.7 %copy-start.54 = (bf16[16,256]{1,0:T(8,128)(2,1)S(1)}, bf16[16,256]{1,0:T(8,128)(2,1)}, u32[]{:S(2)}) copy-start(bf16[16,256]{1,0:T(8,128)(2,1)} %copy-done.53) | copy-start | bytes 24580
  234.6 8.3 %copy-start.22 = (bf16[1536,512]{1,0:T(8,128)(2,1)S(1)}, bf16[1536,512]{1,0:T(8,128)(2,1)}, u32[]{:S(2)}) copy-start(bf16[1536,512]{1,0:T(8,128)(2,1)} %copy.54) | copy-start | bytes 4718596
  234.6 8.3 %copy-start.26 = (bf16[1536,256]{1,0:T(8,128)(2,1)S(1)}, bf16[1536,256]{1,0:T(8,128)(2,1)}, u32[]{:S(2)}) copy-start(bf16[1536,256]{1,0:T(8,128)(2,1)} %copy.55) | copy-start | bytes 2359300
  244.8 78.3 %copy-start.61 = (s32[4,2]{1,0:T(4,128)S(1)}, s32[4,2]{1,0:T(4,128)}, u32[]{:S(2)}) copy-start(s32[4,2]{1,0:T(4,128)} %get-tuple-element.96) | copy-start | bytes 100
  336.9 63.2 %copy-start.5 = (bf16[2,2,4,2,16,3072]{5,4,3,2,1,0:T(8,128)(2,1)S(1)}, bf16[2,2,4,2,16,3072]{5,4,3,2,1,0:T(8,128)(2,1)}, u32[]{:S(2)}) copy-start(bf16[2,2,4,2,16,3072]{5,4,3,2,1,0:T(8,128)(2,1)} %get-tuple-element.67.early_ref) | copy-start | bytes 9437188
  336.9 63.2 %copy-start.15 = (s32[8]{0:T(128)S(1)}, s32[8]{0:T(128)}, u32[]{:S(2)}) copy-start(s32[8]{0:T(128)} %which.1) | copy-start | bytes 100
  403.2 6.7 %copy-start.34 = (bf16[2,128,1536]{2,1,0:T(8,128)(2,1)S(1)}, bf16[2,128,1536]{2,1,0:T(8,128)(2,1)}, u32[]{:S(2)}) copy-start(bf16[2,128,1536]{2,1,0:T(8,128)(2,1)} %get-tuple-element.66) | copy-start | bytes 2359300
  (42 other events, 122.8 us)
